TPU v7x, 32 devices: a whole 2x2x4 slice. The times are simulated.
32 devices in a mesh: section: 2 (over x), dp: 4 (over z), tensor: 4 (over y, core).
Axes of the slice: x: 2, y: 2, z: 4, core: 2. Of those that a mesh axis runs over, the one named last changes fastest.
Arguments:
- inputs: bfloat16 [2, 8, 512, 768], P(None, 'dp'), may hold values from -6 to 6
- cotangent: bfloat16 [2, 8, 512, 768], P(None, 'dp'), may hold values from -6 to 6
- segment_ids: int32 [2, 8, 512], P(None, 'dp'), may hold values from 0 to 1
- column_ids: int32 [2, 8, 512], P(None, 'dp'), may hold values from 0 to 255
- row_ids: int32 [2, 8, 512], P(None, 'dp'), may hold values from 0 to 255
- answer_ids: int32 [2, 8, 512], P(None, 'dp'), may hold values from 0 to 1
- lengths: int32 [2, 8], P(None, 'dp'), may hold values from 128 to 512, as said below
- type_table: bfloat16 [516, 768], replicated, may hold values from -4 to 4
- query_weight: bfloat16 [2, 768, 768], P('section', None, 'tensor'), may hold values from -0.21875 to 0.21875
- query_bias: bfloat16 [2, 768], P('section', 'tensor'), may hold values from -3 to 3
- key_weight: bfloat16 [2, 768, 768], P('section', None, 'tensor'), may hold values from -0.21875 to 0.21875
- value_weight: bfloat16 [2, 768, 768], P('section', None, 'tensor'), may hold values from -0.21875 to 0.21875
- value_bias: bfloat16 [2, 768], P('section', 'tensor'), may hold values from -3 to 3
- output_weight: bfloat16 [2, 768, 768], P('section', 'tensor'), may hold values from -1.75 to 1.75
- output_bias: bfloat16 [2, 768], P('section'), may hold values from -2 to 2
- first_gain: bfloat16 [2, 768], P('section'), may hold values from 0.5 to 1.5
- first_shift: bfloat16 [2, 768], P('section'), may hold values from -2 to 2
- up_weight: bfloat16 [2, 768, 3072], P('section', None, 'tensor'), may hold values from -0.21875 to 0.21875
- up_bias: bfloat16 [2, 3072], P('section', 'tensor'), may hold values from -3 to 3
- down_weight: bfloat16 [2, 3072, 768], P('section', 'tensor'), may hold values from -0.109375 to 0.109375
- down_bias: bfloat16 [2, 768], P('section'), may hold values from -2 to 2
- second_gain: bfloat16 [2, 768], P('section'), may hold values from 0.5 to 1.5
- second_shift: bfloat16 [2, 768], P('section'), may hold values from -2 to 2
Outputs:
- layer_outputs: bfloat16 [2, 2, 8, 512, 768], P('section', None, 'dp', None, 'tensor')
- layer_input_grads: float32 [2, 2, 8, 512, 768], P('section', None, 'dp', None, 'tensor')
- query_weight_grad: float32 [2, 768, 768], P('section', 'dp', 'tensor')
- query_bias_grad: float32 [2, 768], P('section', 'tensor')
- key_weight_grad: float32 [2, 768, 768], P('section', 'dp', 'tensor')
- value_weight_grad: float32 [2, 768, 768], P('section', 'dp', 'tensor')
- value_bias_grad: float32 [2, 768], P('section', 'tensor')
- output_weight_grad: float32 [2, 768, 768], P('section', 'tensor', 'dp')
- output_bias_grad: float32 [2, 768], P('section', 'tensor')
- first_gain_grad: float32 [2, 768], P('section', 'tensor')
- first_shift_grad: float32 [2, 768], P('section', 'tensor')
- up_weight_grad: float32 [2, 768, 3072], P('section', 'dp', 'tensor')
- up_bias_grad: float32 [2, 3072], P('section', 'tensor')
- down_weight_grad: float32 [2, 3072, 768], P('section', 'tensor', 'dp')
- down_bias_grad: float32 [2, 768], P('section', 'tensor')
- second_gain_grad: float32 [2, 768], P('section', 'tensor')
- second_shift_grad: float32 [2, 768], P('section', 'tensor')
- type_table_grad: float32 [516, 768], P('section', 'tensor')
Inputs may be any that keep to these rules, and one draw needn't show every extreme that they name: `lengths`: in each micro-batch some item has all 512 tokens.
All inputs are finite; a program needn't handle non-finite values.
Results may differ from a plain program's by a relative error of at most 0.025.
Values may be sent and summed in bfloat16 or wider, within the bound.
A program may use at most 192 MiB of HBM per device.

v0:
```python
import jax
import jax.numpy as jnp
from jax import lax
from jax.sharding import PartitionSpec as P

HD = 64
COLS = 256
ROWS = 256


EPSILON = 1e-12
MASKED = -1e30


def from_behind(value, axis, steps):
    count = lax.axis_size(axis)
    leading, last = (max(0, -steps), min(count, count - steps))
    return lax.ppermute(value, axis, [(source, source + steps) for source in range(leading, last)])


def layer_norm(value, gain, shift):
    averaged = jnp.mean(value, axis=-1, keepdims=True)
    centered = value - averaged
    variance = jnp.mean(centered * centered, axis=-1, keepdims=True)
    return centered * lax.rsqrt(variance + EPSILON) * gain + shift


def gelu_exact(value):
    return jax.nn.gelu(value, approximate=False)


def product(left, right):
    return jnp.dot(left, right, preferred_element_type=jnp.float32)


def product_back(left, right):
    return lax.dot_general(
        left, right, (((1,), (1,)), ((), ())), preferred_element_type=jnp.float32
    )


def over_rows(left, right):
    return lax.dot_general(
        left, right, (((0,), (0,)), ((), ())), preferred_element_type=jnp.float32
    )


def column_sum(value):
    return jnp.sum(value.astype(jnp.float32), axis=0)


def share_total(partial_value):
    return lax.psum_scatter(
        partial_value.astype(jnp.bfloat16), "tensor", scatter_dimension=0, tiled=True
    ).astype(jnp.float32)


def gather_rows(value):
    return lax.all_gather(value, "tensor", axis=0, tiled=True)


def own_rows(value):
    share = value.shape[0] // lax.axis_size("tensor")
    return lax.dynamic_slice_in_dim(value, lax.axis_index("tensor") * share, share, 0)


def split_heads(flat, sequences):
    return flat.reshape(sequences, -1, flat.shape[-1] // HD, HD)


def masked_scores(query_heads, key_heads, visible):
    scores = jnp.einsum(
        "bqhd,bkhd->bhqk", query_heads, key_heads, preferred_element_type=jnp.float32
    ) * HD ** (-0.5)
    return jnp.where(visible[:, None, None, :], scores, MASKED)


def attend(queries, keys_here, values, visible):
    sequences = visible.shape[0]
    scores = masked_scores(
        split_heads(queries, sequences), split_heads(keys_here, sequences), visible
    )
    maximum = jnp.max(scores, axis=-1, keepdims=True)
    log_total = maximum + jnp.log(jnp.sum(jnp.exp(scores - maximum), axis=-1, keepdims=True))
    weights = jnp.exp(scores - log_total).astype(jnp.bfloat16)
    context = jnp.einsum(
        "bhqk,bkhd->bqhd",
        weights,
        split_heads(values, sequences),
        preferred_element_type=jnp.float32,
    )
    return (context.reshape(queries.shape).astype(jnp.bfloat16), log_total)


def attend_back(queries, keys_here, values, visible, log_total, dcontext):
    sequences = visible.shape[0]
    query_heads = split_heads(queries, sequences)
    key_heads = split_heads(keys_here, sequences)
    value_heads = split_heads(values, sequences)
    dcontext_heads = split_heads(dcontext, sequences)
    weights = jnp.exp(masked_scores(query_heads, key_heads, visible) - log_total)
    dweights = jnp.einsum(
        "bqhd,bkhd->bhqk", dcontext_heads, value_heads, preferred_element_type=jnp.float32
    )
    row_inner = jnp.sum(weights * dweights, axis=-1, keepdims=True)
    dscores = (weights * (dweights - row_inner)).astype(jnp.bfloat16)
    factor = HD ** (-0.5)
    dquery = (
        jnp.einsum("bhqk,bkhd->bqhd", dscores, key_heads, preferred_element_type=jnp.float32)
        * factor
    )
    dkey = (
        jnp.einsum("bhqk,bqhd->bkhd", dscores, query_heads, preferred_element_type=jnp.float32)
        * factor
    )
    dvalue = jnp.einsum(
        "bhqk,bqhd->bkhd",
        weights.astype(jnp.bfloat16),
        dcontext_heads,
        preferred_element_type=jnp.float32,
    )
    return (
        dquery.reshape(queries.shape).astype(jnp.bfloat16),
        dkey.reshape(queries.shape).astype(jnp.bfloat16),
        dvalue.reshape(queries.shape).astype(jnp.bfloat16),
    )


def forward_layer(entering, visible, params):
    (
        query_weight,
        query_bias,
        key_weight,
        value_weight,
        value_bias,
        output_weight,
        output_bias,
        first_gain,
        first_shift,
        up_weight,
        up_bias,
        down_weight,
        down_bias,
        second_gain,
        second_shift,
    ) = params
    lowered = entering.astype(jnp.bfloat16)
    queries = (product(lowered, query_weight) + query_bias).astype(jnp.bfloat16)
    keys_here = product(lowered, key_weight).astype(jnp.bfloat16)
    values = (product(lowered, value_weight) + value_bias).astype(jnp.bfloat16)
    context, log_total = attend(queries, keys_here, values, visible)
    first_sum = own_rows(entering) + (share_total(product(context, output_weight)) + output_bias)
    normed = layer_norm(first_sum, first_gain, first_shift)
    normed_low = gather_rows(normed.astype(jnp.bfloat16))
    hidden = product(normed_low, up_weight) + up_bias
    active = gelu_exact(hidden).astype(jnp.bfloat16)
    second_sum = normed + (share_total(product(active, down_weight)) + down_bias)
    leaving = gather_rows(layer_norm(second_sum, second_gain, second_shift).astype(jnp.bfloat16))
    return (
        leaving,
        (
            entering,
            queries,
            keys_here,
            values,
            log_total,
            context,
            first_sum,
            normed_low,
            hidden,
            second_sum,
            visible,
        ),
    )


def backward_layer(arriving, saved_state, params):
    (
        query_weight,
        query_bias,
        key_weight,
        value_weight,
        value_bias,
        output_weight,
        output_bias,
        first_gain,
        first_shift,
        up_weight,
        up_bias,
        down_weight,
        down_bias,
        second_gain,
        second_shift,
    ) = params
    (
        entering,
        queries,
        keys_here,
        values,
        log_total,
        context,
        first_sum,
        normed_low,
        hidden,
        second_sum,
        visible,
    ) = saved_state
    dsecond, dsecond_gain, dsecond_shift = jax.vjp(
        layer_norm, second_sum, second_gain, second_shift
    )[1](arriving)
    ddown = dsecond.astype(jnp.bfloat16)
    ddown = gather_rows(ddown)
    active_value, gelu_pull = jax.vjp(gelu_exact, hidden)
    active = active_value.astype(jnp.bfloat16)
    dhidden = gelu_pull(product_back(ddown, down_weight))[0].astype(jnp.bfloat16)
    pushed = product_back(dhidden, up_weight)
    dnormed = dsecond + share_total(pushed)
    dfirst, dfirst_gain, dfirst_shift = jax.vjp(layer_norm, first_sum, first_gain, first_shift)[1](
        dnormed
    )
    doutput = dfirst.astype(jnp.bfloat16)
    doutput = gather_rows(doutput)
    dcontext = product_back(doutput, output_weight).astype(jnp.bfloat16)
    dquery, dkey, dvalue = attend_back(queries, keys_here, values, visible, log_total, dcontext)
    lowered = entering.astype(jnp.bfloat16)
    partial_value = (
        product_back(dquery, query_weight)
        + product_back(dkey, key_weight)
        + product_back(dvalue, value_weight)
    )
    dentering = dfirst + share_total(partial_value)
    gradients = (
        over_rows(lowered, dquery),
        column_sum(dquery),
        over_rows(lowered, dkey),
        over_rows(lowered, dvalue),
        column_sum(dvalue),
        over_rows(context, doutput),
        column_sum(doutput),
        dfirst_gain,
        dfirst_shift,
        over_rows(normed_low, dhidden),
        column_sum(dhidden),
        over_rows(active, ddown),
        column_sum(ddown),
        dsecond_gain,
        dsecond_shift,
    )
    return (gradients, dentering)


def split_gradients(gradients, column_block, column_share):

    def own_part(vector):
        return lax.dynamic_slice_in_dim(vector, column_block * column_share, column_share, 0)

    norm_terms = (
        lax.psum_scatter(gradients[7], "tensor", scatter_dimension=0, tiled=True),
        lax.psum_scatter(gradients[8], "tensor", scatter_dimension=0, tiled=True),
        lax.psum_scatter(gradients[13], "tensor", scatter_dimension=0, tiled=True),
        lax.psum_scatter(gradients[14], "tensor", scatter_dimension=0, tiled=True),
    )
    matrices = tuple((gradients[number][None] for number in (0, 2, 3, 5, 9, 11)))
    vectors = (
        gradients[1][None],
        gradients[4][None],
        own_part(gradients[6])[None],
        norm_terms[0][None],
        norm_terms[1][None],
        gradients[10][None],
        own_part(gradients[12])[None],
        norm_terms[2][None],
        norm_terms[3][None],
    )
    return (matrices, vectors)


def on_device(
    inputs,
    cotangent,
    segment_ids,
    column_ids,
    row_ids,
    answer_ids,
    lengths,
    type_table,
    query_weight,
    query_bias,
    key_weight,
    value_weight,
    value_bias,
    output_weight,
    output_bias,
    first_gain,
    first_shift,
    up_weight,
    up_bias,
    down_weight,
    down_bias,
    second_gain,
    second_shift,
):
    weights_in = (
        query_weight,
        query_bias,
        key_weight,
        value_weight,
        value_bias,
        output_weight,
        output_bias,
        first_gain,
        first_shift,
        up_weight,
        up_bias,
        down_weight,
        down_bias,
        second_gain,
        second_shift,
    )
    params = tuple(
        (
            stacked[0] if number in (0, 2, 3, 5, 9, 11) else stacked[0].astype(jnp.float32)
            for number, stacked in enumerate(weights_in)
        )
    )
    on_first = lax.axis_index("section") == 0
    first_factor = on_first.astype(jnp.float32)
    column_block = lax.axis_index("tensor")
    micro_count = inputs.shape[0]
    sequences = inputs.shape[1]
    length_here = inputs.shape[2]
    model_width = inputs.shape[3]
    column_share = model_width // lax.axis_size("tensor")
    rows_here = sequences * length_here
    type_count = 4 + COLS + ROWS
    type_rows = type_table.astype(jnp.float32)
    positions = jnp.arange(length_here)

    def own_columns(value):
        return lax.dynamic_slice_in_dim(value, column_block * column_share, column_share, 1)

    entering_list = []
    visible_list = []
    picks_list = []
    for number in range(micro_count):
        type_picks = (
            jax.nn.one_hot(segment_ids[number].reshape(rows_here), type_count, dtype=jnp.float32)
            + jax.nn.one_hot(
                column_ids[number].reshape(rows_here) + 2, type_count, dtype=jnp.float32
            )
            + jax.nn.one_hot(
                row_ids[number].reshape(rows_here) + 2 + COLS, type_count, dtype=jnp.float32
            )
            + jax.nn.one_hot(
                answer_ids[number].reshape(rows_here) + 2 + COLS + ROWS,
                type_count,
                dtype=jnp.float32,
            )
        )
        embedded = inputs[number].reshape(rows_here, model_width).astype(jnp.float32) + jnp.dot(
            type_picks, type_rows, precision=lax.Precision.HIGHEST
        )
        picks_list.append(type_picks)
        entering_list.append(embedded)
        visible_list.append(positions[None, :] < lengths[number][:, None])
    leaving_list = []
    saved_list = []
    for period in range(micro_count + 1):
        own_batch = min(period, micro_count - 1)
        prior_batch = max(period - 1, 0)
        visible = jnp.where(on_first, visible_list[own_batch], visible_list[prior_batch])
        if period == 0:
            entering = entering_list[0]
        else:
            arrived = from_behind(leaving_list[-1], "section", 1)
            entering = jnp.where(on_first, entering_list[own_batch], arrived.astype(jnp.float32))
        leaving, saved_state = forward_layer(entering, visible, params)
        leaving_list.append(leaving)
        saved_list.append(saved_state)
    accumulated = None
    sent_list = []
    dcolumn_list = []
    table_term = jnp.zeros((type_count, column_share), jnp.float32)
    for period in range(micro_count + 1):
        upper_batch = min(period, micro_count - 1)
        lower_batch = max(period - 1, 0)
        from_output = cotangent[upper_batch].reshape(rows_here, model_width).astype(jnp.float32)
        from_output = own_rows(from_output)
        if period == 0:
            arriving = from_output
        else:
            returned = from_behind(sent_list[-1], "section", -1)
            arriving = jnp.where(on_first, returned.astype(jnp.float32), from_output)
        saved_state = jax.tree.map(
            lambda low_side, high_side: jnp.where(on_first, low_side, high_side),
            saved_list[lower_batch],
            saved_list[upper_batch + 1],
        )
        gradients, dentering = backward_layer(arriving, saved_state, params)
        live_factor = jnp.where(
            on_first,
            jnp.float32(1.0 if period >= 1 else 0.0),
            jnp.float32(1.0 if period < micro_count else 0.0),
        )
        sent_list.append(dentering.astype(jnp.bfloat16))
        dcolumns = lax.all_to_all(
            dentering.astype(jnp.bfloat16), "tensor", split_axis=1, concat_axis=0, tiled=True
        ).astype(dentering.dtype)
        dcolumn_list.append(dcolumns)
        if period >= 1:
            table_term = table_term + first_factor * lax.dot_general(
                picks_list[lower_batch],
                dcolumns,
                (((0,), (0,)), ((), ())),
                precision=lax.Precision.HIGHEST,
                preferred_element_type=jnp.float32,
            )
        matrices, vectors = split_gradients(
            tuple((term * live_factor for term in gradients)), column_block, column_share
        )
        pieces = (tuple(matrices), tuple(vectors))
        accumulated = pieces if accumulated is None else jax.tree.map(jnp.add, accumulated, pieces)
    grad_query, grad_key, grad_value, grad_output, grad_up, grad_down = accumulated[0]
    (
        bias_query,
        bias_value,
        bias_output,
        gain_first,
        shift_first,
        bias_up,
        bias_down,
        gain_second,
        shift_second,
    ) = accumulated[1]
    matrices = (
        lax.psum_scatter(
            grad_query.astype(jnp.bfloat16), "dp", scatter_dimension=1, tiled=True
        ).astype(jnp.float32),
        lax.psum_scatter(
            grad_key.astype(jnp.bfloat16), "dp", scatter_dimension=1, tiled=True
        ).astype(jnp.float32),
        lax.psum_scatter(
            grad_value.astype(jnp.bfloat16), "dp", scatter_dimension=1, tiled=True
        ).astype(jnp.float32),
        lax.psum_scatter(
            grad_output.astype(jnp.bfloat16), "dp", scatter_dimension=2, tiled=True
        ).astype(jnp.float32),
        lax.psum_scatter(
            grad_up.astype(jnp.bfloat16), "dp", scatter_dimension=1, tiled=True
        ).astype(jnp.float32),
        lax.psum_scatter(
            grad_down.astype(jnp.bfloat16), "dp", scatter_dimension=2, tiled=True
        ).astype(jnp.float32),
    )
    vectors = lax.psum(
        (
            bias_query,
            bias_value,
            bias_output,
            gain_first,
            shift_first,
            bias_up,
            bias_down,
            gain_second,
            shift_second,
        ),
        "dp",
    )
    table_summed = lax.psum(table_term.astype(jnp.bfloat16), "dp")
    table_grad = lax.psum_scatter(table_summed, "section", scatter_dimension=0, tiled=True).astype(
        jnp.float32
    )
    layer_outputs = jnp.stack(
        [
            own_columns(
                jnp.where(on_first, leaving_list[number], leaving_list[number + 1])
            ).reshape(sequences, length_here, column_share)
            for number in range(micro_count)
        ]
    )[None]
    layer_input_grads = jnp.stack(
        [
            jnp.where(on_first, dcolumn_list[number + 1], dcolumn_list[number]).reshape(
                sequences, length_here, column_share
            )
            for number in range(micro_count)
        ]
    )[None]
    return (
        layer_outputs,
        layer_input_grads,
        matrices[0],
        vectors[0],
        matrices[1],
        matrices[2],
        vectors[1],
        matrices[3],
        vectors[2],
        vectors[3],
        vectors[4],
        matrices[4],
        vectors[5],
        matrices[5],
        vectors[6],
        vectors[7],
        vectors[8],
        table_grad,
    )


def solution(mesh):
    return jax.shard_map(
        on_device,
        mesh=mesh,
        in_specs=(
            P(None, "dp", None, None),
            P(None, "dp", None, None),
            P(None, "dp", None),
            P(None, "dp", None),
            P(None, "dp", None),
            P(None, "dp", None),
            P(None, "dp"),
            P(),
            P("section", None, "tensor"),
            P("section", "tensor"),
            P("section", None, "tensor"),
            P("section", None, "tensor"),
            P("section", "tensor"),
            P("section", "tensor", None),
            P("section", None),
            P("section", None),
            P("section", None),
            P("section", None, "tensor"),
            P("section", "tensor"),
            P("section", "tensor", None),
            P("section", None),
            P("section", None),
            P("section", None),
        ),
        out_specs=(
            P("section", None, "dp", None, "tensor"),
            P("section", None, "dp", None, "tensor"),
            P("section", "dp", "tensor"),
            P("section", "tensor"),
            P("section", "dp", "tensor"),
            P("section", "dp", "tensor"),
            P("section", "tensor"),
            P("section", "tensor", "dp"),
            P("section", "tensor"),
            P("section", "tensor"),
            P("section", "tensor"),
            P("section", "dp", "tensor"),
            P("section", "tensor"),
            P("section", "tensor", "dp"),
            P("section", "tensor"),
            P("section", "tensor"),
            P("section", "tensor"),
            P("section", "tensor"),
        ),
        check_vma=False,
    )
```

profile of v0, /device:TPU:0, one launch (start us, length us, event | category | flops | bytes accessed | tf_op | source)
XLA Modules:
  0.0 1172.2 jit_solution(12731910426834441694)
XLA Ops:
  23.6 8.7 fusion.75
  49.7 30.8 %reduce-scatter.31.cloned.1.call-done = bf16[256,768]{0,1:T(8,128)(2,1)} async-done(((bf16[1024,768]{0,1:T(8,128)(2,1)}), bf16[256,768]{0,1:T(8,128)(2,1)}) %reduce-scatter.31.cloned.1.call-update) | async-done | bytes 393232 | tf_op jit(solution)/shard_map/reduce_scatter | solution.py:53
  83.8 19.4 %all-gather.13.cloned.1.call-done = bf16[1024,768]{0,1:T(8,128)(2,1)} async-done(((bf16[256,768]{0,1:T(8,128)(2,1)}), bf16[1024,768]{0,1:T(8,128)(2,1)}) %all-gather.13.cloned.1.call-update) | async-done | bytes 1572880 | tf_op jit(solution)/shard_map/all_gather | solution.py:59
  107.9 9.5 convolution_convert_fusion.7
  117.6 28.2 %reduce-scatter.33.cloned.1.call-done = bf16[256,768]{0,1:T(8,128)(2,1)} async-done(((bf16[1024,768]{0,1:T(8,128)(2,1)}), bf16[256,768]{0,1:T(8,128)(2,1)}) %reduce-scatter.33.cloned.1.call-update) | async-done | bytes 393232 | tf_op jit(solution)/shard_map/reduce_scatter | solution.py:53
  148.4 19.9 %all-gather.15.cloned.1.call-done = bf16[1024,768]{0,1:T(8,128)(2,1)} async-done(((bf16[256,768]{0,1:T(8,128)(2,1)}), bf16[1024,768]{0,1:T(8,128)(2,1)}) %all-gather.15.cloned.1.call-update) | async-done | bytes 1572880 | tf_op jit(solution)/shard_map/all_gather | solution.py:59
  180.0 26.1 %collective-permute-done = bf16[1024,768]{0,1:T(8,128)(2,1)} collective-permute-done((bf16[1024,768]{0,1:T(8,128)(2,1)}, bf16[1024,768]{0,1:T(8,128)(2,1)}, u32[]{:S(2)}, u32[]{:S(2)}) %collective-permute-start) | collective-permute-done | bytes 1572896 | tf_op jit(solution)/shard_map/ppermute | solution.py:18
  206.1 10.4 select_convert_fusion.2
  233.4 28.8 %reduce-scatter.35.cloned.1.call-done = bf16[256,768]{0,1:T(8,128)(2,1)} async-done(((bf16[1024,768]{0,1:T(8,128)(2,1)}), bf16[256,768]{0,1:T(8,128)(2,1)}) %reduce-scatter.35.cloned.1.call-update) | async-done | bytes 393232 | tf_op jit(solution)/shard_map/reduce_scatter | solution.py:53
  268.9 19.7 %all-gather.17.cloned.1.call-done = bf16[1024,768]{0,1:T(8,128)(2,1)} async-done(((bf16[256,768]{0,1:T(8,128)(2,1)}), bf16[1024,768]{0,1:T(8,128)(2,1)}) %all-gather.17.cloned.1.call-update) | async-done | bytes 1572880 | tf_op jit(solution)/shard_map/all_gather | solution.py:59
  293.3 9.5 convolution_convert_fusion.5
  310.4 20.7 %reduce-scatter.37.cloned.1.call-done = bf16[256,768]{0,1:T(8,128)(2,1)} async-done(((bf16[1024,768]{0,1:T(8,128)(2,1)}), bf16[256,768]{0,1:T(8,128)(2,1)}) %reduce-scatter.37.cloned.1.call-update) | async-done | bytes 393232 | tf_op jit(solution)/shard_map/reduce_scatter | solution.py:53
  345.3 20.0 %all-gather.19.cloned.1.call-done = bf16[1024,768]{0,1:T(8,128)(2,1)} async-done(((bf16[256,768]{0,1:T(8,128)(2,1)}), bf16[1024,768]{0,1:T(8,128)(2,1)}) %all-gather.19.cloned.1.call-update) | async-done | bytes 1572880 | tf_op jit(solution)/shard_map/all_gather | solution.py:59
  369.2 33.9 %collective-permute-done.1 = bf16[1024,768]{0,1:T(8,128)(2,1)S(1)} collective-permute-done((bf16[1024,768]{0,1:T(8,128)(2,1)}, bf16[1024,768]{0,1:T(8,128)(2,1)S(1)}, u32[]{:S(2)}, u32[]{:S(2)}) %collective-permute-start.1) | collective-permute-done | bytes 1572896 | tf_op jit(solution)/shard_map/ppermute | solution.py:18
  403.0 5.1 select_convert_fusion.1
  429.0 27.4 %reduce-scatter.39.cloned.1.call-done = bf16[256,768]{0,1:T(8,128)(2,1)} async-done(((bf16[1024,768]{0,1:T(8,128)(2,1)}), bf16[256,768]{0,1:T(8,128)(2,1)}) %reduce-scatter.39.cloned.1.call-update) | async-done | bytes 393232 | tf_op jit(solution)/shard_map/reduce_scatter | solution.py:53
  466.9 18.2 %all-gather.21.cloned.1.call-done = bf16[1024,768]{0,1:T(8,128)(2,1)} async-done(((bf16[256,768]{0,1:T(8,128)(2,1)}), bf16[1024,768]{0,1:T(8,128)(2,1)}) %all-gather.21.cloned.1.call-update) | async-done | bytes 1572880 | tf_op jit(solution)/shard_map/all_gather | solution.py:59
  485.1 25.7 %fusion.16 = (f32[1024,768]{0,1:T(8,128)}, f32[1024,768]{0,1:T(8,128)}, f32[1024,768]{0,1:T(8,128)}, f32[1024,768]{0,1:T(8,128)}, f32[1024,768]{0,1:T(8,128)}, /*index=5*/f32[1024,768]{0,1:T(8,128)}, f32[1024,768]{0,1:T(8,128)}) fusion(f32[1024,768]{0,1:T(8,128)} %copy-done.228, f32[1024,768]{0,1:T(8,128)} %copy-done.227, f32[768]{0:T(1024)} %copy-done.200, ...), kind=kOutput, calls=%fused_computation.39 | convolution fusion | flops 1358954496 | bytes 31067136 | tf_op jit(solution)/shard_map/dot_general | solution.py:33
  510.8 6.2 convert_reduce_fusion.5
  520.8 11.3 convolution_convert_fusion.3
  535.1 14.0 %reduce-scatter.43.cloned.1.call-done = bf16[256,768]{0,1:T(8,128)(2,1)} async-done(((bf16[1024,768]{0,1:T(8,128)(2,1)}), bf16[256,768]{0,1:T(8,128)(2,1)}) %reduce-scatter.43.cloned.1.call-update) | async-done | bytes 393232 | tf_op jit(solution)/shard_map/reduce_scatter | solution.py:53
  552.6 27.2 %reduce-scatter.41.cloned.1.call-done = bf16[256,768]{0,1:T(8,128)(2,1)} async-done(((bf16[1024,768]{0,1:T(8,128)(2,1)}), bf16[256,768]{0,1:T(8,128)(2,1)}) %reduce-scatter.41.cloned.1.call-update) | async-done | bytes 393232 | tf_op jit(solution)/shard_map/reduce_scatter | solution.py:53
  592.5 12.6 %all-gather.27.cloned.1.call-done = bf16[1024,768]{0,1:T(8,128)(2,1)} async-done(((bf16[256,768]{0,1:T(8,128)(2,1)}), bf16[1024,768]{0,1:T(8,128)(2,1)}) %all-gather.27.cloned.1.call-update) | async-done | bytes 1572880 | tf_op jit(solution)/shard_map/all_gather | solution.py:59
  610.1 5.3 convert_reduce_fusion.11
  632.5 22.7 %reduce-scatter.45.cloned.1.call-done = bf16[256,768]{0,1:T(8,128)(2,1)} async-done(((bf16[1024,768]{0,1:T(8,128)(2,1)}), bf16[256,768]{0,1:T(8,128)(2,1)}) %reduce-scatter.45.cloned.1.call-update) | async-done | bytes 393232 | tf_op jit(solution)/shard_map/reduce_scatter | solution.py:53
  660.5 9.7 collective-permute-done.2
  675.9 19.0 %all-gather.29.cloned.1.call-done = bf16[1024,768]{0,1:T(8,128)(2,1)} async-done(((bf16[256,768]{0,1:T(8,128)(2,1)}), bf16[1024,768]{0,1:T(8,128)(2,1)}) %all-gather.29.cloned.1.call-update) | async-done | bytes 1572880 | tf_op jit(solution)/shard_map/all_gather | solution.py:59
  694.9 6.5 convert_reduce_fusion.4
  706.5 27.0 %reduce-scatter.47.cloned.1.call-done = bf16[256,768]{0,1:T(8,128)(2,1)} async-done(((bf16[1024,768]{0,1:T(8,128)(2,1)}), bf16[256,768]{0,1:T(8,128)(2,1)}) %reduce-scatter.47.cloned.1.call-update) | async-done | bytes 393232 | tf_op jit(solution)/shard_map/reduce_scatter | solution.py:53
  745.8 13.5 %all-gather.31.cloned.1.call-done = bf16[1024,768]{0,1:T(8,128)(2,1)} async-done(((bf16[256,768]{0,1:T(8,128)(2,1)}), bf16[1024,768]{0,1:T(8,128)(2,1)}) %all-gather.31.cloned.1.call-update) | async-done | bytes 1572880 | tf_op jit(solution)/shard_map/all_gather | solution.py:59
  764.2 5.3 convert_reduce_fusion.10
  780.8 28.3 %reduce-scatter.49.cloned.1.call-done = bf16[256,768]{0,1:T(8,128)(2,1)} async-done(((bf16[1024,768]{0,1:T(8,128)(2,1)}), bf16[256,768]{0,1:T(8,128)(2,1)}) %reduce-scatter.49.cloned.1.call-update) | async-done | bytes 393232 | tf_op jit(solution)/shard_map/reduce_scatter | solution.py:53
  812.4 11.5 collective-permute-done.3
  826.5 18.6 %all-gather.33.cloned.1.call-done = bf16[1024,768]{0,1:T(8,128)(2,1)} async-done(((bf16[256,768]{0,1:T(8,128)(2,1)}), bf16[1024,768]{0,1:T(8,128)(2,1)}) %all-gather.33.cloned.1.call-update) | async-done | bytes 1572880 | tf_op jit(solution)/shard_map/all_gather | solution.py:59
  845.2 6.5 convert_reduce_fusion.3
  880.6 4.9 fusion.76
  890.6 5.1 fusion.81
  898.1 7.2 all-gather.23.cloned.1.call-done
  908.8 4.9 fusion.77
  918.1 5.8 copy.361
  943.4 5.9 fusion.93
  954.4 6.8 multiply_reduce_fusion
  965.6 5.6 multiply_convert_fusion
  1006.8 12.3 %all-reduce.6 = (f32[768]{0:T(1024)}, f32[768]{0:T(1024)S(1)}, f32[768]{0:T(1024)S(1)}, f32[768]{0:T(1024)S(1)}) all-reduce(f32[768]{0:T(1024)S(1)} %add_add_fusion.15, f32[768]{0:T(1024)} %add_add_fusion.14, f32[768]{0:T(1024)} %add_add_fusion.13, ...), channel_id=26, replica_groups=mesh['section'=2,'dp'=4,'tensor'=4] {'tensor'}, use_global_device_ids=true, to_apply=%region_74.75.clone | all-reduce | flops 3072 | bytes 24576
  1056.4 19.9 %all-reduce.7 = (f32[1,192]{1,0:T(1,128)}, f32[1,192]{1,0:T(1,128)}, f32[1,192]{1,0:T(1,128)}, f32[1,192]{1,0:T(1,128)}, f32[1,192]{1,0:T(1,128)}, /*index=5*/f3...) all-reduce(f32[1,192]{1,0:T(1,128)S(1)} %add.879, ...), channel_id=1, replica_groups=mesh['section'=2,'dp'=4,'tensor'=4] {'dp'}, use_global_device_ids=true, to_apply=%region_61.62 | all-reduce | flops 2304 | bytes 18432 | tf_op jit(solution)/shard_map/psum | solution.py:455
  1087.3 17.7 %reduce-scatter.57.cloned.1.call-done = bf16[192,192]{1,0:T(8,128)(2,1)} async-done(((bf16[768,192]{1,0:T(8,128)(2,1)}), bf16[192,192]{1,0:T(8,128)(2,1)}) %reduce-scatter.57.cloned.1.call-update) | async-done | bytes 73744
  1114.9 8.7 fusion
  1133.6 29.9 %all-reduce.10.cloned.1.call-done = bf16[258,192]{1,0:T(8,128)(2,1)} async-done(((bf16[258,192]{1,0:T(8,128)(2,1)}), bf16[258,192]{1,0:T(8,128)(2,1)}) %all-reduce.10.cloned.1.call-update) | async-done | bytes 99088 | tf_op jit(solution)/shard_map/psum | solution.py:469
  (866 shorter events, 411.7 us)
Async XLA Ops:
  7.2 96.1 %copy-start = (bf16[1,768,768]{2,1,0:T(8,128)(2,1)S(1)}, bf16[1,768,768]{2,1,0:T(8,128)(2,1)}, u32[]{:S(2)}) copy-start(bf16[1,768,768]{2,1,0:T(8,128)(2,1)} %param.40) | copy-start | bytes 3538948
  7.2 73.4 %reduce-scatter.31.cloned.1.call-start = ((), (), s32[]{:S(2)}) async-start(), calls=%async_computation.21 | async-start | bytes 1966080 | tf_op jit(solution)/shard_map/reduce_scatter | solution.py:53
  44.8 183.9 %copy-start.128 = (f32[2,3,512]{2,1,0:T(4,128)}, f32[2,3,512]{2,1,0:T(4,128)S(1)}, u32[]{:S(2)}) copy-start(f32[2,3,512]{2,1,0:T(4,128)S(1)} %log_add_fusion.2) | copy-start | bytes 36868
  49.6 53.7 %all-gather.13.cloned.1.call-start = ((), (), s32[]{:S(2)}) async-start(), calls=%async_computation.22 | async-start | bytes 1966080 | tf_op jit(solution)/shard_map/all_gather | solution.py:59
  49.7 56.5 %copy-start.140 = (f32[768]{0:T(1024)}, f32[768]{0:T(1024)S(1)}, u32[]{:S(2)}) copy-start(f32[768]{0:T(1024)S(1)} %convert_reduce_fusion.21) | copy-start | bytes 9220
  83.2 62.5 %reduce-scatter.33.cloned.1.call-start = ((), (), s32[]{:S(2)}) async-start(), calls=%async_computation.23 | async-start | bytes 1966080 | tf_op jit(solution)/shard_map/reduce_scatter | solution.py:53
  117.4 55.7 %copy-start.174 = (s32[1,4,2,128]{3,2,1,0:T(2,128)S(1)}, s32[1,4,2,128]{3,2,1,0:T(2,128)}, u32[]{:S(2)}) copy-start(s32[1,4,2,128]{3,2,1,0:T(2,128)} %get-tuple-element.176) | copy-start | bytes 12292
  117.4 55.7 %copy-start.175 = (s32[1,4,2,128]{3,2,1,0:T(2,128)S(1)}, s32[1,4,2,128]{3,2,1,0:T(2,128)}, u32[]{:S(2)}) copy-start(s32[1,4,2,128]{3,2,1,0:T(2,128)} %get-tuple-element.178) | copy-start | bytes 12292
  117.4 55.7 %copy-start.176 = (s32[1,4,2,128]{3,2,1,0:T(2,128)S(1)}, s32[1,4,2,128]{3,2,1,0:T(2,128)}, u32[]{:S(2)}) copy-start(s32[1,4,2,128]{3,2,1,0:T(2,128)} %get-tuple-element.180) | copy-start | bytes 12292
  117.4 50.9 %all-gather.15.cloned.1.call-start = ((), (), s32[]{:S(2)}) async-start(), calls=%async_computation.24 | async-start | bytes 1966080 | tf_op jit(solution)/shard_map/all_gather | solution.py:59
  117.5 58.9 %copy-start.138 = (f32[768]{0:T(1024)}, f32[768]{0:T(1024)S(1)}, u32[]{:S(2)}) copy-start(f32[768]{0:T(1024)S(1)} %convert_reduce_fusion.17) | copy-start | bytes 9220
  117.6 224.2 %copy-start.126 = (f32[768]{0:T(1024)}, f32[768]{0:T(1024)S(1)}, u32[]{:S(2)}) copy-start(f32[768]{0:T(1024)S(1)} %get-tuple-element.234) | copy-start | bytes 9220
  117.6 224.2 %copy-start.136 = (f32[768]{0:T(1024)}, f32[768]{0:T(1024)S(1)}, u32[]{:S(2)}) copy-start(f32[768]{0:T(1024)S(1)} %get-tuple-element.233) | copy-start | bytes 9220
  148.4 113.8 %reduce-scatter.35.cloned.1.call-start = ((), (), s32[]{:S(2)}) async-start(), calls=%async_computation.25 | async-start | bytes 1966080 | tf_op jit(solution)/shard_map/reduce_scatter | solution.py:53
  168.4 37.7 %collective-permute-start = (bf16[1024,768]{0,1:T(8,128)(2,1)}, bf16[1024,768]{0,1:T(8,128)(2,1)}, u32[]{:S(2)}, u32[]{:S(2)}) collective-permute-start(bf16[1024,768]{0,1:T(8,128)(2,1)} %all-gather.15.cloned.1.call-done), channel_id=1, source_target_pairs={{0,16},{1,17},{2,18},{3,19},{4,20},{5,21},{6,22},{7,23},{8,24},{9,... | collective-permute-start | bytes 4718600 | tf_op jit(solution)/shard_map/ppermute | solution.py:18
  233.3 55.3 %all-gather.17.cloned.1.call-start = ((), (), s32[]{:S(2)}) async-start(), calls=%async_computation.26 | async-start | bytes 1966080 | tf_op jit(solution)/shard_map/all_gather | solution.py:59
  268.6 62.5 %reduce-scatter.37.cloned.1.call-start = ((), (), s32[]{:S(2)}) async-start(), calls=%async_computation.27 | async-start | bytes 1966080 | tf_op jit(solution)/shard_map/reduce_scatter | solution.py:53
  302.8 62.5 %all-gather.19.cloned.1.call-start = ((), (), s32[]{:S(2)}) async-start(), calls=%async_computation.28 | async-start | bytes 1966080 | tf_op jit(solution)/shard_map/all_gather | solution.py:59
  345.3 111.1 %reduce-scatter.39.cloned.1.call-start = ((), (), s32[]{:S(2)}) async-start(), calls=%async_computation.29 | async-start | bytes 1966080 | tf_op jit(solution)/shard_map/reduce_scatter | solution.py:53
  365.3 37.7 %collective-permute-start.1 = (bf16[1024,768]{0,1:T(8,128)(2,1)}, bf16[1024,768]{0,1:T(8,128)(2,1)S(1)}, u32[]{:S(2)}, u32[]{:S(2)}) collective-permute-start(bf16[1024,768]{0,1:T(8,128)(2,1)} %all-gather.19.cloned.1.call-done), channel_id=1, source_target_pairs={{0,16},{1,17},{2,18},{3,19},{4,20},{5,21},{6,22},{7,23},{8,24},{9,... | collective-permute-start | bytes 4718600 | tf_op jit(solution)/shard_map/ppermute | solution.py:18
  429.0 56.1 %all-gather.21.cloned.1.call-start = ((), (), s32[]{:S(2)}) async-start(), calls=%async_computation.30 | async-start | bytes 1966080 | tf_op jit(solution)/shard_map/all_gather | solution.py:59
  465.1 45.7 %all-gather.25.cloned.1.call-start = ((), (), s32[]{:S(2)}) async-start(), calls=%async_computation.33 | async-start | bytes 1966080 | tf_op jit(solution)/shard_map/all_gather | solution.py:59
  466.7 82.3 %reduce-scatter.43.cloned.1.call-start = ((), (), s32[]{:S(2)}) async-start(), calls=%async_computation.34 | async-start | bytes 1966080 | tf_op jit(solution)/shard_map/reduce_scatter | solution.py:53
  520.7 59.1 %reduce-scatter.41.cloned.1.call-start = ((), (), s32[]{:S(2)}) async-start(), calls=%async_computation.31 | async-start | bytes 1966080 | tf_op jit(solution)/shard_map/reduce_scatter | solution.py:53
  532.1 73.1 %all-gather.27.cloned.1.call-start = ((), (), s32[]{:S(2)}) async-start(), calls=%async_computation.35 | async-start | bytes 1966080 | tf_op jit(solution)/shard_map/all_gather | solution.py:59
  585.2 69.9 %reduce-scatter.45.cloned.1.call-start = ((), (), s32[]{:S(2)}) async-start(), calls=%async_computation.36 | async-start | bytes 1966080 | tf_op jit(solution)/shard_map/reduce_scatter | solution.py:53
  626.8 68.1 %all-gather.29.cloned.1.call-start = ((), (), s32[]{:S(2)}) async-start(), calls=%async_computation.37 | async-start | bytes 1966080 | tf_op jit(solution)/shard_map/all_gather | solution.py:59
  657.3 12.9 %collective-permute-start.2 = (bf16[256,768]{0,1:T(8,128)(2,1)}, bf16[256,768]{0,1:T(8,128)(2,1)S(1)}, u32[]{:S(2)}, u32[]{:S(2)}) collective-permute-start(bf16[256,768]{0,1:T(8,128)(2,1)} %add_convert_fusion.10), channel_id=1, source_target_pairs={{16,0},{17,1},{18,2},{19,3},{20,4},{21,5},{22,6},{23,7},{24,8},{25... | collective-permute-start | bytes 1179656 | tf_op jit(solution)/shard_map/ppermute | solution.py:18
  675.8 57.7 %reduce-scatter.47.cloned.1.call-start = ((), (), s32[]{:S(2)}) async-start(), calls=%async_computation.38 | async-start | bytes 1966080 | tf_op jit(solution)/shard_map/reduce_scatter | solution.py:53
  705.1 54.1 %all-gather.31.cloned.1.call-start = ((), (), s32[]{:S(2)}) async-start(), calls=%async_computation.39 | async-start | bytes 1966080 | tf_op jit(solution)/shard_map/all_gather | solution.py:59
  739.3 69.8 %reduce-scatter.49.cloned.1.call-start = ((), (), s32[]{:S(2)}) async-start(), calls=%async_computation.40 | async-start | bytes 1966080 | tf_op jit(solution)/shard_map/reduce_scatter | solution.py:53
  780.8 64.4 %all-gather.33.cloned.1.call-start = ((), (), s32[]{:S(2)}) async-start(), calls=%async_computation.41 | async-start | bytes 1966080 | tf_op jit(solution)/shard_map/all_gather | solution.py:59
  810.9 12.9 %collective-permute-start.3 = (bf16[256,768]{0,1:T(8,128)(2,1)}, bf16[256,768]{0,1:T(8,128)(2,1)S(1)}, u32[]{:S(2)}, u32[]{:S(2)}) collective-permute-start(bf16[256,768]{0,1:T(8,128)(2,1)} %add_convert_fusion.9), channel_id=1, source_target_pairs={{16,0},{17,1},{18,2},{19,3},{20,4},{21,5},{22,6},{23,7},{24,8},{25... | collective-permute-start | bytes 1179656 | tf_op jit(solution)/shard_map/ppermute | solution.py:18
  826.1 59.4 %reduce-scatter.51.cloned.1.call-start = ((), (), s32[]{:S(2)}) async-start(), calls=%async_computation.42 | async-start | bytes 1966080 | tf_op jit(solution)/shard_map/reduce_scatter | solution.py:53
  855.4 49.8 %all-gather.23.cloned.1.call-start = ((), (), s32[]{:S(2)}) async-start(), calls=%async_computation.32 | async-start | bytes 1966080 | tf_op jit(solution)/shard_map/all_gather | solution.py:59
  870.4 79.2 %all-gather.35.cloned.1.call-start = ((), (), s32[]{:S(2)}) async-start(), calls=%async_computation.43 | async-start | bytes 1966080 | tf_op jit(solution)/shard_map/all_gather | solution.py:59
  890.4 106.5 %reduce-scatter.65.cloned.1.call-start = ((), (), s32[]{:S(2)}) async-start(), calls=%async_computation.51 | async-start | bytes 1474560
  939.2 48.9 %all-to-all-start = ((bf16[256,4,192]{0,2,1:T(8,128)(2,1)}), bf16[256,4,192]{0,2,1:T(8,128)(2,1)}, u32[]{:S(2)}, u32[]{:S(2)}) async-start(bf16[256,4,192]{0,2,1:T(8,128)(2,1)} %bitcast.24), calls=%async_computation.10 | async-start | bytes 786432 | tf_op jit(solution)/shard_map/all_to_all | solution.py:406
  943.4 59.7 %reduce-scatter.55.cloned.1.call-start = ((), (), s32[]{:S(2)}) async-start(), calls=%async_computation.45 | async-start | bytes 1474560 | tf_op jit(solution)/shard_map/reduce_scatter | solution.py:448
  949.3 126.9 %reduce-scatter.63.cloned.1.call-start = ((), (), s32[]{:S(2)}) async-start(), calls=%async_computation.50 | async-start | bytes 491520
  981.0 97.1 %reduce-scatter.53.cloned.1.call-start = ((), (), s32[]{:S(2)}) async-start(), calls=%async_computation.44 | async-start | bytes 1966080 | tf_op jit(solution)/shard_map/reduce_scatter | solution.py:53
  985.2 98.3 %reduce-scatter.61.cloned.1.call-start = ((), (), s32[]{:S(2)}) async-start(), calls=%async_computation.49 | async-start | bytes 491520
  1034.8 50.6 %reduce-scatter.59.cloned.1.call-start = ((), (), s32[]{:S(2)}) async-start(), calls=%async_computation.48 | async-start | bytes 491520
  1047.6 57.4 %reduce-scatter.57.cloned.1.call-start = ((), (), s32[]{:S(2)}) async-start(), calls=%async_computation.47 | async-start | bytes 491520
  1080.0 26.9 %all-to-all-start.2 = ((bf16[256,4,192]{0,2,1:T(8,128)(2,1)}), bf16[256,4,192]{0,2,1:T(8,128)(2,1)S(1)}, u32[]{:S(2)}, u32[]{:S(2)}) async-start(bf16[256,4,192]{0,2,1:T(8,128)(2,1)} %bitcast.31), calls=%async_computation.14 | async-start | bytes 786432 | tf_op jit(solution)/shard_map/all_to_all | solution.py:406
  1106.9 19.2 %all-to-all-start.1 = ((bf16[256,4,192]{0,2,1:T(8,128)(2,1)}), bf16[256,4,192]{0,2,1:T(8,128)(2,1)S(1)}, u32[]{:S(2)}, u32[]{:S(2)}) async-start(bf16[256,4,192]{0,2,1:T(8,128)(2,1)} %bitcast.26), calls=%async_computation.11 | async-start | bytes 786432 | tf_op jit(solution)/shard_map/all_to_all | solution.py:406
  1110.4 53.1 %all-reduce.10.cloned.1.call-start = ((), (), s32[]{:S(2)}) async-start(), calls=%async_computation.46 | async-start | bytes 270336 | tf_op jit(solution)/shard_map/psum | solution.py:469
  1123.7 6.0 collective-permute-start.4
  (226 other events, 2100.3 us)
Sparse Core Ops, SparseCore 0:
  49.7 30.8 reduce-scatter.30
  83.3 19.8 all-gather.12
  117.6 28.1 reduce-scatter.32
  148.5 19.8 all-gather.14
  233.4 28.7 reduce-scatter.34
  268.7 19.8 all-gather.16
  302.9 28.1 reduce-scatter.36
  345.4 19.8 all-gather.18
  429.1 27.2 reduce-scatter.38
  465.2 19.8 all-gather.20
  486.7 19.8 all-gather.24
  520.8 28.1 reduce-scatter.42
  551.6 28.1 reduce-scatter.40
  585.3 19.8 all-gather.26
  626.9 28.1 reduce-scatter.44
  675.9 18.9 all-gather.28
  705.3 28.1 reduce-scatter.46
  739.4 19.8 all-gather.30
  780.9 28.1 reduce-scatter.48
  826.2 18.9 all-gather.32
  855.5 28.1 reduce-scatter.50
  885.4 19.8 all-gather.22
  906.9 19.8 all-gather.34
  929.0 29.1 reduce-scatter.64
  960.7 27.8 reduce-scatter.54
  990.8 19.2 reduce-scatter.62
  1013.1 26.4 reduce-scatter.52
  1042.0 20.6 reduce-scatter.60
  1065.0 18.9 reduce-scatter.58
  1086.2 18.8 reduce-scatter.56
  1131.6 31.8 all-reduce.9
where the time goes:
time: 1180 us; the launch traced here: 1170 us
  waiting for transfers between devices  552 us (47%)
  matrix products  264 us (22%)
  local copies, waits for them, and re-layouts  137 us (12%)
  other arithmetic  131 us (11%)
  blocking collectives  40.9 us (3%)
  starting transfers between devices  28.7 us (2%)
  between operations  18.8 us (2%)
    reduce_scatter x12, waiting for transfers between devices, share_total(): lax.psum_scatter(partial_value.astype(jnp.bfloat16), 'tensor', scatter_di...  255 us
    all_gather x12, waiting for transfers between devices, gather_rows(): return lax.all_gather(value, 'tensor', axis=0, tiled=True)  168 us
    ppermute x4, waiting for transfers between devices, from_behind(): lax.ppermute(value, axis, [(source, source + steps) for source in range(l...  81.2 us
    dot_general x18, matrix products, product(): return jnp.dot(left, right, preferred_element_type=jnp.float32)  80.1 us
    unnamed x531, local copies, waits for them, and re-layouts  76.8 us
    dot_general x18, matrix products, over_rows(): lax.dot_general(left, right, (((0,), (0,)), ((), ())), preferred_element_...  53.3 us
    dot_general x18, matrix products, product_back(): lax.dot_general(left, right, (((1,), (1,)), ((), ())), preferred_element_...  47.3 us
    reshape x21, local copies, waits for them, and re-layouts, split_heads(): return flat.reshape(sequences, -1, flat.shape[-1] // HD, HD)  30.2 us
  transfers between devices with their start and end apart: 39, of which 26 were waited for; matrix products, arithmetic and copies ran while one was open for 24% of the time, Pallas kernels for 0%

commit v1 on v0

v1 whole, which is shorter than its diff:
```python
import functools

import jax
import jax.numpy as jnp
from jax import lax
from jax.experimental import pallas as pl
from jax.experimental.pallas import tpu as pltpu
from jax.sharding import PartitionSpec as P

HD = 64
COLS = 256
ROWS = 256
EPSILON = 1e-12
MASKED = -1e30
BF = jnp.bfloat16
F32 = jnp.float32
MESH = pl.DeviceIdType.MESH
VMEM_LIMIT = 60 * 1024 * 1024
STEP = 128


def nn(left, right):
    return lax.dot_general(left, right, (((1,), (0,)), ((), ())), preferred_element_type=F32)


def nt(left, right):
    return lax.dot_general(left, right, (((1,), (1,)), ((), ())), preferred_element_type=F32)


def tn(left, right):
    return lax.dot_general(left, right, (((0,), (0,)), ((), ())), preferred_element_type=F32)


def normalize(value):
    centered = value - jnp.mean(value, axis=-1, keepdims=True)
    variance = jnp.mean(centered * centered, axis=-1, keepdims=True)
    scale = lax.rsqrt(variance + EPSILON)
    return centered * scale, scale


def place():
    section = lax.axis_index("section")
    data = lax.axis_index("dp")
    tensor = lax.axis_index("tensor")
    beside = tensor + 1 - 2 * (tensor % 2)
    across = tensor + 2 - 4 * ((tensor // 2) % 2)
    return section, data, tensor, beside, across


def greet(partners):
    barrier = pltpu.get_barrier_semaphore()
    for partner in partners:
        pl.semaphore_signal(barrier, inc=1, device_id=partner, device_id_type=MESH)
    pl.semaphore_wait(barrier, len(partners))


def remote(src, dst, send, recv, device):
    return pltpu.make_async_remote_copy(
        src_ref=src, dst_ref=dst, send_sem=send, recv_sem=recv, device_id=device, device_id_type=MESH
    )


def forward_kernel(
    inputs_ref,
    ids_ref,
    table_ref,
    length_ref,
    wa_ref,
    wu_ref,
    wd_ref,
    bias_ref,
    vec_ref,
    wa_out,
    wu_out,
    wd_out,
    p_out,
    lse_out,
    act_out,
    slope_out,
    n1_out,
    n2_out,
    rs1_out,
    rs2_out,
    x_out,
    y_out,
    wa,
    wu,
    wd,
    bias,
    p,
    lse,
    act,
    slope,
    xf,
    xb,
    first,
    low,
    n1,
    n2,
    rs1,
    rs2,
    y,
    gather_send,
    gather_recv,
    relay_send,
    relay_recv,
    local_sem,
    out_sem,
):
    section, data, tensor, beside, across = place()
    length, width = xf.shape
    ranks = wa.shape[0]
    heads = wa.shape[1] // (4 * HD)
    part = heads * HD
    steps = length // STEP
    sequences = inputs_ref.shape[1]
    near = (section, data, beside)
    far = (section, data, across)
    other = (1 - section, data, tensor)
    greet((near, far, other))

    shards = ((wa_ref, wa), (bias_ref, bias), (wu_ref, wu), (wd_ref, wd))
    to_far = []
    to_near = []
    onward = []
    own = []
    for number, (source, target) in enumerate(shards):
        to_far.append(
            remote(source, target.at[2], gather_send.at[number, 0], gather_recv.at[number, 0], far)
        )
        to_near.append(
            remote(source, target.at[1], gather_send.at[number, 1], gather_recv.at[number, 1], near)
        )
        onward.append(
            remote(
                target.at[2], target.at[3], gather_send.at[number, 2], gather_recv.at[number, 2], near
            )
        )
        own.append(pltpu.make_async_copy(source, target.at[0], local_sem.at[number]))
    for copy in to_far:
        copy.start()
    for copy in to_near:
        copy.start()
    for copy in own:
        copy.start()

    def pass_on(number):
        to_far[number].wait_recv()
        onward[number].start()

    def ready(number):
        own[number].wait()
        to_near[number].wait_recv()
        onward[number].wait_recv()

    out_copies = []

    def put_out(source, target):
        copy = pltpu.make_async_copy(source, target, out_sem.at[len(out_copies)])
        copy.start()
        out_copies.append(copy)

    relays = [
        remote(
            y.at[pl.ds(step * STEP, STEP)],
            xb.at[pl.ds(step * STEP, STEP)],
            relay_send.at[step],
            relay_recv.at[step],
            other,
        )
        for step in range(steps)
    ]

    @pl.when(section == 0)
    def _():
        copy = pltpu.make_async_copy(
            inputs_ref.at[tensor // sequences, tensor % sequences], xb, local_sem.at[4]
        )
        copy.start()
        copy.wait()

        def embed(step, carry):
            rows = pl.ds(pl.multiple_of(step * STEP, STEP), STEP)
            lane = lax.broadcasted_iota(jnp.int32, (STEP, table_ref.shape[0]), 1)
            picks = jnp.zeros((STEP, table_ref.shape[0]), F32)
            for column in range(4):
                picks = picks + jnp.where(ids_ref[rows, column : column + 1] == lane, 1.0, 0.0)
            value = xb[rows, :].astype(F32) + nn(picks.astype(BF), table_ref[...])
            xf[rows, :] = value
            xb[rows, :] = value.astype(BF)
            return carry

        lax.fori_loop(0, steps, embed, 0)

    pass_on(0)
    pass_on(1)

    @pl.when(section != 0)
    def _():
        for relay in relays:
            relay.wait_recv()
        xf[...] = xb[...].astype(F32)

    ready(0)
    ready(1)
    put_out(wa, wa_out)
    put_out(xb, x_out)

    def project(rank, carry):
        columns = jnp.transpose(bias[rank], (1, 0))
        p[rank, 0 : 3 * part, :] = (
            nt(wa[rank, 0 : 3 * part, :], xb[...]) + columns[0 : 3 * part, 1:2]
        ).astype(BF)
        return carry

    lax.fori_loop(0, ranks, project, 0)
    pass_on(2)

    visible = lax.broadcasted_iota(jnp.int32, (length, length), 0) < length_ref[0, 0]

    def attend(head, carry):
        rank = head // heads
        base = (head % heads) * HD
        query = p[rank, pl.ds(pl.multiple_of(base, HD), HD), :]
        keys = p[rank, pl.ds(pl.multiple_of(part + base, HD), HD), :]
        values = p[rank, pl.ds(pl.multiple_of(2 * part + base, HD), HD), :]
        query = (query.astype(F32) * HD ** (-0.5)).astype(BF)
        scores = jnp.where(visible, tn(keys, query), MASKED)
        maximum = jnp.max(scores, axis=0, keepdims=True)
        raised = jnp.exp(scores - maximum)
        total = jnp.sum(raised, axis=0, keepdims=True)
        context = nn(values, raised.astype(BF)) / total
        p[rank, pl.ds(pl.multiple_of(3 * part + base, HD), HD), :] = context.astype(BF)
        lse[head] = maximum + jnp.log(total)
        return carry

    lax.fori_loop(0, ranks * heads, attend, 0)
    put_out(p, p_out)
    put_out(lse, lse_out)

    def first_norm(step, carry):
        rows = pl.ds(pl.multiple_of(step * STEP, STEP), STEP)
        total = xf[rows, :] + vec_ref[0:1, :]
        for rank in range(ranks):
            total = total + tn(p[rank, 3 * part : 4 * part, rows], wa[rank, 3 * part : 4 * part, :])
        normal, scale = normalize(total)
        value = normal * vec_ref[1:2, :] + vec_ref[2:3, :]
        first[rows, :] = value
        low[rows, :] = value.astype(BF)
        n1[rows, :] = normal.astype(BF)
        rs1[rows, :] = jnp.broadcast_to(scale, (STEP, 128))
        return carry

    lax.fori_loop(0, steps, first_norm, 0)
    put_out(n1, n1_out)
    put_out(rs1, rs1_out)
    ready(2)
    put_out(wu, wu_out)
    block = 256
    blocks = wu.shape[2] // block

    def widen(index, carry):
        rank = index // blocks
        columns = pl.ds(pl.multiple_of((index % blocks) * block, block), block)
        hidden = nn(low[...], wu[rank, :, columns]) + bias[rank, 0:1, columns]
        inner = 0.5 * (1.0 + lax.erf(hidden * (0.5**0.5)))
        act[rank, :, columns] = (hidden * inner).astype(BF)
        density = jnp.exp(hidden * hidden * (-0.5)) * 0.3989422804014327
        slope[rank, :, columns] = (inner + hidden * density).astype(BF)
        return carry

    lax.fori_loop(0, ranks * blocks, widen, 0)
    put_out(act, act_out)
    put_out(slope, slope_out)
    pass_on(3)
    ready(3)
    put_out(wd, wd_out)

    for step in range(steps):
        rows = pl.ds(step * STEP, STEP)
        total = first[rows, :] + vec_ref[3:4, :]
        for rank in range(ranks):
            total = total + nn(act[rank, rows, :], wd[rank])
        normal, scale = normalize(total)
        y[rows, :] = (normal * vec_ref[4:5, :] + vec_ref[5:6, :]).astype(BF)
        n2[rows, :] = normal.astype(BF)
        rs2[rows, :] = jnp.broadcast_to(scale, (STEP, 128))

        @pl.when(section == 0)
        def _():
            relays[step].start()

    put_out(n2, n2_out)
    put_out(rs2, rs2_out)
    put_out(y, y_out)
    for copy in out_copies:
        copy.wait()
    for group in (to_far, to_near, onward):
        for copy in group:
            copy.wait_send()

    @pl.when(section == 0)
    def _():
        for relay in relays:
            relay.wait_send()


def forward(inputs, ids, table, length_here, wa, wu, wd, bias, vectors, ranks):
    length, width = inputs.shape[2], inputs.shape[3]
    rows_a = wa.shape[0]
    hidden = wu.shape[1]
    heads = ranks * (rows_a // (4 * HD))
    steps = length // STEP
    shapes = dict(
        wa=((ranks, rows_a, width), BF),
        wu=((ranks, width, hidden), BF),
        wd=((ranks, hidden, width), BF),
        p=((ranks, rows_a, length), BF),
        lse=((heads, 1, length), F32),
        act=((ranks, length, hidden), BF),
        slope=((ranks, length, hidden), BF),
        n1=((length, width), BF),
        n2=((length, width), BF),
        rs1=((length, 128), F32),
        rs2=((length, 128), F32),
        x=((length, width), BF),
        y=((length, width), BF),
    )

    def buffer(name):
        return pltpu.VMEM(*shapes[name])

    outs = ("wa", "wu", "wd", "p", "lse", "act", "slope", "n1", "n2", "rs1", "rs2", "x", "y")
    anywhere = pl.BlockSpec(memory_space=pl.ANY)
    inside = pl.BlockSpec(memory_space=pltpu.VMEM)
    return pl.pallas_call(
        forward_kernel,
        name="forward_layer",
        out_shape=tuple(jax.ShapeDtypeStruct(*shapes[name]) for name in outs),
        in_specs=[
            anywhere,
            inside,
            inside,
            pl.BlockSpec(memory_space=pltpu.SMEM),
            anywhere,
            anywhere,
            anywhere,
            anywhere,
            inside,
        ],
        out_specs=tuple(anywhere for _ in outs),
        scratch_shapes=[
            buffer("wa"),
            buffer("wu"),
            buffer("wd"),
            pltpu.VMEM((ranks,) + bias.shape, F32),
            buffer("p"),
            buffer("lse"),
            buffer("act"),
            buffer("slope"),
            pltpu.VMEM((length, width), F32),
            buffer("x"),
            pltpu.VMEM((length, width), F32),
            pltpu.VMEM((length, width), BF),
            buffer("n1"),
            buffer("n2"),
            buffer("rs1"),
            buffer("rs2"),
            buffer("y"),
            pltpu.SemaphoreType.DMA((4, 3)),
            pltpu.SemaphoreType.DMA((4, 3)),
            pltpu.SemaphoreType.DMA((steps,)),
            pltpu.SemaphoreType.DMA((steps,)),
            pltpu.SemaphoreType.DMA((5,)),
            pltpu.SemaphoreType.DMA((len(outs),)),
        ],
        compiler_params=pltpu.CompilerParams(
            collective_id=0, has_side_effects=True, vmem_limit_bytes=VMEM_LIMIT
        ),
        cost_estimate=pl.CostEstimate(
            flops=8_000_000_000, bytes_accessed=60_000_000, transcendentals=6_000_000
        ),
    )(inputs, ids, table, length_here, wa, wu, wd, bias, vectors)


def backward_kernel(
    cotangent_ref,
    wa_ref,
    wu_ref,
    wd_ref,
    p_ref,
    lse_ref,
    act_ref,
    slope_ref,
    n1_ref,
    n2_ref,
    rs1_ref,
    rs2_ref,
    x_ref,
    length_ref,
    vec_ref,
    sums_out,
    dx_out,
    vec_out,
    wa,
    wu,
    wd,
    p,
    lse,
    act,
    slope,
    n1,
    n2,
    rs1,
    rs2,
    xb,
    g,
    dsum,
    low,
    low_t,
    first_t,
    x_t,
    dcontext,
    dx,
    near_out,
    near_in,
    far_out,
    far_in,
    sums,
    load_sem,
    near_send,
    near_recv,
    far_send,
    far_recv,
    relay_send,
    relay_recv,
    out_sem,
):
    section, data, tensor, beside, across = place()
    length, width = g.shape
    ranks = wa.shape[0]
    heads = wa.shape[1] // (4 * HD)
    part = heads * HD
    steps = length // STEP
    sequences = cotangent_ref.shape[1]
    units = sums.shape[1]
    share = sums.shape[2]
    near = (section, data, beside)
    far = (section, data, across)
    other = (1 - section, data, tensor)
    greet((near, far, other))

    loads = {}
    for name, source, target in (
        ("n2", n2_ref, n2),
        ("rs2", rs2_ref, rs2),
        ("wd", wd_ref, wd),
        ("slope", slope_ref, slope),
        ("wu", wu_ref, wu),
        ("act", act_ref, act),
        ("n1", n1_ref, n1),
        ("rs1", rs1_ref, rs1),
        ("wa", wa_ref, wa),
        ("p", p_ref, p),
        ("lse", lse_ref, lse),
        ("xb", x_ref, xb),
    ):
        loads[name] = pltpu.make_async_copy(source, target, load_sem.at[len(loads)])
    start_g = pltpu.make_async_copy(
        cotangent_ref.at[tensor // sequences, tensor % sequences], g, load_sem.at[len(loads)]
    )
    relays = [
        remote(
            dx.at[pl.ds(step * STEP, STEP)],
            g.at[pl.ds(step * STEP, STEP)],
            relay_send.at[step],
            relay_recv.at[step],
            other,
        )
        for step in range(steps)
    ]

    @pl.when(section != 0)
    def _():
        start_g.start()

    for name in loads:
        loads[name].start()
    vec_out[...] = jnp.zeros_like(vec_out)
    loads["n2"].wait()
    loads["rs2"].wait()

    @pl.when(section != 0)
    def _():
        start_g.wait()

    def add_row(row, value):
        vec_out[row : row + 1, :] += jnp.sum(value, axis=0, keepdims=True)

    def norm_back(arriving, normal, scale, gain):
        scaled = arriving * gain
        return (
            scaled
            - jnp.mean(scaled, axis=-1, keepdims=True)
            - normal * jnp.mean(scaled * normal, axis=-1, keepdims=True)
        ) * scale

    for step in range(steps):
        rows = pl.ds(step * STEP, STEP)

        @pl.when(section == 0)
        def _():
            relays[step].wait_recv()

        arriving = g[rows, :].astype(F32)
        normal = n2[rows, :].astype(F32)
        add_row(12, arriving * normal)
        add_row(13, arriving)
        value = norm_back(arriving, normal, rs2[rows, 0:1], vec_ref[4:5, :])
        dsum[rows, :] = value
        value = value.astype(BF)
        low[rows, :] = value
        value = value.astype(F32)
        add_row(9, value)
        low_t[:, rows] = jnp.transpose(value, (1, 0)).astype(BF)

    def to_near(number, unit, which):
        return remote(
            near_out.at[unit, which],
            near_in.at[number, unit, which],
            near_send.at[unit, which],
            near_recv.at[number, unit, which],
            near,
        )

    def to_far(number, unit):
        return remote(
            far_out.at[number, unit],
            far_in.at[number, unit],
            far_send.at[number, unit],
            far_recv.at[number, unit],
            far,
        )

    def gradient(number, unit, rank):
        rows = pl.ds(pl.multiple_of(unit * share, share), share)
        if number == 0:
            return nn(low_t[rows, :], act[rank])
        if number == 1:
            return nn(first_t[rows, :], slope[rank])
        main = nt(x_t[rows, :], p[rank])
        edge = (3 * part // 256) * 256
        tail = nt(low_t[rows, :], p[rank, edge : 4 * part, :])
        lane = lax.broadcasted_iota(jnp.int32, tail.shape, 1)
        tail = jnp.where(lane < 3 * part - edge, main[:, edge:], tail)
        return jnp.concatenate([main[:, :edge], tail], axis=1)

    def reduce_stage(number):
        def body(index, carry):
            @pl.when(index < units)
            def _():
                for which, rank in ((1, 3), (0, 1)):
                    if number > 0:
                        to_near(number - 1, index, which).wait_send()
                    near_out[index, which] = gradient(number, index, rank).astype(BF)
                    to_near(number, index, which).start()

            @pl.when(index > 0)
            def _():
                unit = index - 1
                mine = gradient(number, unit, 2)
                to_near(number, unit, 1).wait_recv()
                far_out[number, unit] = (mine + near_in[number, unit, 1].astype(F32)).astype(BF)
                to_far(number, unit).start()
                mine = gradient(number, unit, 0)
                to_near(number, unit, 0).wait_recv()
                sums[number, unit] = (mine + near_in[number, unit, 0].astype(F32)).astype(BF)

            return carry

        lax.fori_loop(0, units + 1, body, 0)

    loads["act"].wait()

    @pl.when(section == 0)
    def _():
        reduce_stage(0)

    loads["wd"].wait()
    loads["slope"].wait()
    block = 256
    blocks = wu.shape[2] // block

    def narrow(index, carry):
        rank = index // blocks
        columns = pl.ds(pl.multiple_of((index % blocks) * block, block), block)
        value = nt(low[...], wd[rank, columns, :]) * slope[rank, :, columns].astype(F32)
        value = value.astype(BF)
        slope[rank, :, columns] = value
        vec_out[pl.ds(rank, 1), columns] = jnp.sum(value.astype(F32), axis=0, keepdims=True)
        return carry

    lax.fori_loop(0, ranks * blocks, narrow, 0)
    loads["n1"].wait()
    loads["rs1"].wait()

    def first_transpose(step, carry):
        rows = pl.ds(pl.multiple_of(step * STEP, STEP), STEP)
        value = n1[rows, :].astype(F32) * vec_ref[1:2, :] + vec_ref[2:3, :]
        first_t[:, rows] = jnp.transpose(value, (1, 0)).astype(BF)
        return carry

    lax.fori_loop(0, steps, first_transpose, 0)

    @pl.when(section == 0)
    def _():
        reduce_stage(1)

    loads["wu"].wait()

    if True:

        @pl.when(section != 0)
        def _():
            reduce_stage(0)

    def first_back(step, carry):
        rows = pl.ds(pl.multiple_of(step * STEP, STEP), STEP)
        arriving = dsum[rows, :]
        for rank in range(ranks):
            arriving = arriving + nt(slope[rank, rows, :], wu[rank])
        normal = n1[rows, :].astype(F32)
        add_row(10, arriving * normal)
        add_row(11, arriving)
        value = norm_back(arriving, normal, rs1[rows, 0:1], vec_ref[1:2, :])
        dsum[rows, :] = value
        value = value.astype(BF)
        low[rows, :] = value
        value = value.astype(F32)
        add_row(8, value)
        low_t[:, rows] = jnp.transpose(value, (1, 0)).astype(BF)
        return carry

    lax.fori_loop(0, steps, first_back, 0)
    loads["wa"].wait()
    loads["p"].wait()
    loads["lse"].wait()

    def context_back(rank, carry):
        dcontext[rank] = nt(wa[rank, 3 * part : 4 * part, :], low[...]).astype(BF)
        return carry

    lax.fori_loop(0, ranks, context_back, 0)
    visible = lax.broadcasted_iota(jnp.int32, (length, length), 0) < length_ref[0, 0]

    def attend_back(head, carry):
        rank = head // heads
        base = (head % heads) * HD
        at_query = pl.ds(pl.multiple_of(base, HD), HD)
        at_keys = pl.ds(pl.multiple_of(part + base, HD), HD)
        at_values = pl.ds(pl.multiple_of(2 * part + base, HD), HD)
        query = (p[rank, at_query, :].astype(F32) * HD ** (-0.5)).astype(BF)
        keys = p[rank, at_keys, :]
        values = p[rank, at_values, :]
        dout = dcontext[rank, at_query, :]
        weights = jnp.where(visible, jnp.exp(tn(keys, query) - lse[head]), 0.0)
        dweights = tn(values, dout)
        inner = jnp.sum(weights * dweights, axis=0, keepdims=True)
        dscores = (weights * (dweights - inner)).astype(BF)
        p[rank, at_query, :] = (nn(keys, dscores) * HD ** (-0.5)).astype(BF)
        p[rank, at_keys, :] = nt(query, dscores).astype(BF)
        p[rank, at_values, :] = nt(dout, weights.astype(BF)).astype(BF)
        return carry

    lax.fori_loop(0, ranks * heads, attend_back, 0)
    for rank in range(ranks):
        vec_out[4 + rank : 5 + rank, :] = nt(jnp.ones((8, length), BF), p[rank])[0:1, :]
    loads["xb"].wait()

    def entering_transpose(step, carry):
        rows = pl.ds(pl.multiple_of(step * STEP, STEP), STEP)
        x_t[:, rows] = jnp.transpose(xb[rows, :].astype(F32), (1, 0)).astype(BF)
        return carry

    lax.fori_loop(0, steps, entering_transpose, 0)

    for step in range(steps):
        rows = pl.ds(step * STEP, STEP)
        total = dsum[rows, :]
        for rank in range(ranks):
            total = total + tn(p[rank, 0 : 3 * part, rows], wa[rank, 0 : 3 * part, :])
        dx[rows, :] = total.astype(BF)

        @pl.when(section != 0)
        def _():
            relays[step].start()

    dx_copy = pltpu.make_async_copy(dx, dx_out, out_sem.at[0])
    dx_copy.start()

    @pl.when(section != 0)
    def _():
        reduce_stage(1)

    reduce_stage(2)

    def finish(index, carry):
        number = index // units
        unit = index % units
        to_far(number, unit).wait_recv()
        sums[number, unit] = (
            sums[number, unit].astype(F32) + far_in[number, unit].astype(F32)
        ).astype(BF)
        return carry

    lax.fori_loop(0, 3 * units, finish, 0)
    sums_copy = pltpu.make_async_copy(sums, sums_out, out_sem.at[1])
    sums_copy.start()
    for unit in range(units):
        for which in range(2):
            to_near(2, unit, which).wait_send()
    for number in range(3):
        for unit in range(units):
            to_far(number, unit).wait_send()

    @pl.when(section != 0)
    def _():
        for relay in relays:
            relay.wait_send()

    dx_copy.wait()
    sums_copy.wait()


def backward(cotangent, saved, length_here, vectors):
    wa, wu, wd, p, lse, act, slope, n1, n2, rs1, rs2, x = saved
    ranks = wa.shape[0]
    length, width = x.shape
    steps = length // STEP
    units = 4
    share = width // units
    anywhere = pl.BlockSpec(memory_space=pl.ANY)
    inside = pl.BlockSpec(memory_space=pltpu.VMEM)
    part = wa.shape[1] // 4

    def like(value):
        return pltpu.VMEM(value.shape, value.dtype)

    plane = (length, width)
    turned = (width, length)
    chunk = (share, width)
    return pl.pallas_call(
        backward_kernel,
        name="backward_layer",
        out_shape=(
            jax.ShapeDtypeStruct((3, units) + chunk, BF),
            jax.ShapeDtypeStruct(plane, BF),
            jax.ShapeDtypeStruct((16, width), F32),
        ),
        in_specs=[anywhere] * 13 + [pl.BlockSpec(memory_space=pltpu.SMEM), inside],
        out_specs=(anywhere, anywhere, inside),
        scratch_shapes=[like(value) for value in saved]
        + [
            pltpu.VMEM(plane, BF),
            pltpu.VMEM(plane, F32),
            pltpu.VMEM(plane, BF),
            pltpu.VMEM(turned, BF),
            pltpu.VMEM(turned, BF),
            pltpu.VMEM(turned, BF),
            pltpu.VMEM((ranks, part, length), BF),
            pltpu.VMEM(plane, BF),
            pltpu.VMEM((units, 2) + chunk, BF),
            pltpu.VMEM((3, units, 2) + chunk, BF),
            pltpu.VMEM((3, units) + chunk, BF),
            pltpu.VMEM((3, units) + chunk, BF),
            pltpu.VMEM((3, units) + chunk, BF),
            pltpu.SemaphoreType.DMA((13,)),
            pltpu.SemaphoreType.DMA((units, 2)),
            pltpu.SemaphoreType.DMA((3, units, 2)),
            pltpu.SemaphoreType.DMA((3, units)),
            pltpu.SemaphoreType.DMA((3, units)),
            pltpu.SemaphoreType.DMA((steps,)),
            pltpu.SemaphoreType.DMA((steps,)),
            pltpu.SemaphoreType.DMA((2,)),
        ],
        compiler_params=pltpu.CompilerParams(
            collective_id=1, has_side_effects=True, vmem_limit_bytes=VMEM_LIMIT
        ),
        cost_estimate=pl.CostEstimate(
            flops=17_000_000_000, bytes_accessed=60_000_000, transcendentals=3_000_000
        ),
    )(cotangent, *saved, length_here, vectors)


def on_device(
    inputs,
    cotangent,
    segment_ids,
    column_ids,
    row_ids,
    answer_ids,
    lengths,
    type_table,
    query_weight,
    query_bias,
    key_weight,
    value_weight,
    value_bias,
    output_weight,
    output_bias,
    first_gain,
    first_shift,
    up_weight,
    up_bias,
    down_weight,
    down_bias,
    second_gain,
    second_shift,
):
    section = lax.axis_index("section")
    tensor = lax.axis_index("tensor")
    ranks = lax.axis_size("tensor")
    micro_count, sequences, length, width = inputs.shape
    items = micro_count * sequences
    type_count = 4 + COLS + ROWS
    padded_types = -(-type_count // 16) * 16
    part = query_weight.shape[2]
    hidden = up_weight.shape[2]

    ids = jnp.stack(
        [segment_ids, column_ids + 2, row_ids + 2 + COLS, answer_ids + 2 + COLS + ROWS], axis=-1
    ).reshape(items, length, 4)
    own_ids = lax.dynamic_index_in_dim(ids, tensor, 0, keepdims=False)
    length_here = lax.dynamic_slice_in_dim(lengths.reshape(items), tensor, 1, 0).reshape(1, 1)
    table = jnp.pad(type_table, ((0, padded_types - type_count), (0, 0)))
    wa = jnp.concatenate(
        [query_weight[0].T, key_weight[0].T, value_weight[0].T, output_weight[0]], axis=0
    )
    gap = jnp.zeros((part,), F32)
    bias = jnp.zeros((8, hidden), F32)
    bias = bias.at[0].set(up_bias[0].astype(F32))
    bias = bias.at[1].set(
        jnp.concatenate([query_bias[0].astype(F32), gap, value_bias[0].astype(F32), gap])
    )
    vectors = jnp.concatenate(
        [output_bias, first_gain, first_shift, down_bias, second_gain, second_shift]
    ).astype(F32)
    vectors = jnp.pad(vectors, ((0, 2), (0, 0)))

    results = forward(
        inputs, own_ids, table, length_here, wa, up_weight[0], down_weight[0], bias, vectors, ranks
    )
    saved, leaving = results[:-1], results[-1]
    layer_outputs = lax.all_to_all(leaving, "tensor", split_axis=1, concat_axis=0, tiled=True)
    layer_outputs = layer_outputs.reshape(1, micro_count, sequences, length, width // ranks)

    sums, dx, vecs = backward(cotangent, saved, length_here, vectors)

    dcolumns = lax.all_to_all(dx, "tensor", split_axis=1, concat_axis=0, tiled=True)
    layer_input_grads = dcolumns.astype(F32).reshape(
        1, micro_count, sequences, length, width // ranks
    )
    picks = jax.nn.one_hot(ids.reshape(items * length, 4), type_count, dtype=BF).sum(axis=1)
    table_term = lax.dot_general(
        picks, dcolumns, (((0,), (0,)), ((), ())), preferred_element_type=F32
    )
    table_term = jnp.where(section == 0, table_term, 0.0).astype(BF)
    table_sum = lax.psum(table_term, "dp")
    table_grad = lax.psum_scatter(table_sum, "section", scatter_dimension=0, tiled=True).astype(F32)

    summed = lax.psum_scatter(
        sums.reshape(3, width, width), "dp", scatter_dimension=1, tiled=True
    ).astype(F32)
    order = jnp.arange(ranks) ^ tensor
    packed = jnp.concatenate(
        [jnp.take(vecs[0:ranks], order, axis=0), jnp.take(vecs[4 : 4 + ranks], order, axis=0)]
        + [vecs[row].reshape(ranks, width // ranks) for row in range(8, 14)],
        axis=1,
    )
    packed = lax.psum(packed, ("tensor", "dp"))
    mine = lax.dynamic_slice_in_dim(packed, tensor, 1, 0)

    def vector(start, count):
        return mine[:, start : start + count]

    share = width // ranks
    after = 2 * width
    return (
        layer_outputs,
        layer_input_grads,
        summed[2, :, 0:part][None],
        vector(width, part),
        summed[2, :, part : 2 * part][None],
        summed[2, :, 2 * part : 3 * part][None],
        vector(width + 2 * part, part),
        summed[2, :, 3 * part : 4 * part].T[None],
        vector(after, share),
        vector(after + 2 * share, share),
        vector(after + 3 * share, share),
        summed[1][None],
        vector(0, hidden),
        summed[0].T[None],
        vector(after + share, share),
        vector(after + 4 * share, share),
        vector(after + 5 * share, share),
        table_grad,
    )


def solution(mesh):
    return jax.shard_map(
        on_device,
        mesh=mesh,
        in_specs=(
            P(None, "dp", None, None),
            P(None, "dp", None, None),
            P(None, "dp", None),
            P(None, "dp", None),
            P(None, "dp", None),
            P(None, "dp", None),
            P(None, "dp"),
            P(),
            P("section", None, "tensor"),
            P("section", "tensor"),
            P("section", None, "tensor"),
            P("section", None, "tensor"),
            P("section", "tensor"),
            P("section", "tensor", None),
            P("section", None),
            P("section", None),
            P("section", None),
            P("section", None, "tensor"),
            P("section", "tensor"),
            P("section", "tensor", None),
            P("section", None),
            P("section", None),
            P("section", None),
        ),
        out_specs=(
            P("section", None, "dp", None, "tensor"),
            P("section", None, "dp", None, "tensor"),
            P("section", "dp", "tensor"),
            P("section", "tensor"),
            P("section", "dp", "tensor"),
            P("section", "dp", "tensor"),
            P("section", "tensor"),
            P("section", "tensor", "dp"),
            P("section", "tensor"),
            P("section", "tensor"),
            P("section", "tensor"),
            P("section", "dp", "tensor"),
            P("section", "tensor"),
            P("section", "tensor", "dp"),
            P("section", "tensor"),
            P("section", "tensor"),
            P("section", "tensor"),
            P("section", "tensor"),
        ),
        check_vma=False,
    )
```

time: 1180 us -> 461 us (0.39)
  waiting for transfers between devices: 552 us -> 22.4 us
  Pallas kernels: 0 us -> 286 us
  matrix products: 264 us -> 0.76 us
  other arithmetic: 131 us -> 21 us
  local copies, waits for them, and re-layouts: 137 us -> 32.3 us
  blocking collectives: 40.9 us -> 72.3 us
  starting transfers between devices: 28.7 us -> 10.9 us
    pallas_call x0 -> x2, Pallas kernels: none -> 286 us  [the longest x1 182 us: backward(): pl.pallas_call(backward_kernel, name='backward_layer', out_shape=(jax.Sha...]
    dot_general x79 -> x1, matrix products: 264 us -> 0.76 us  [on_device(): lax.dot_general(picks, dcolumns, (((0,), (0,)), ((), ())), preferred_elem...]
    reduce_scatter x13 -> x0, waiting for transfers between devices: 255 us -> none  [the longest x12 255 us: share_total(): lax.psum_scatter(partial_value.astype(jnp.bfloat16), 'tensor', scatter_di...]
    all_gather x12 -> x0, waiting for transfers between devices: 168 us -> none  [gather_rows(): return lax.all_gather(value, 'tensor', axis=0, tiled=True)]
    ppermute x4 -> x0, waiting for transfers between devices: 81.2 us -> none  [from_behind(): lax.ppermute(value, axis, [(source, source + steps) for source in range(l...]
    unnamed x531 -> x32, local copies, waits for them, and re-layouts: 76.8 us -> 18.8 us
    reduce_sum x44 -> x1, other arithmetic: 57.5 us -> 11.7 us  [on_device(): jax.nn.one_hot(ids.reshape(items * length, 4), type_count, dtype=BF)]
    psum x1, blocking collectives: 19.9 us -> 65 us  [on_device(): packed = lax.psum(packed, ('tensor', 'dp'))]
  transfers between devices with their start and end apart: 39 -> 5, of which waited for: 26 -> 2; matrix products, arithmetic and copies ran while one was open for 24% -> 6% of each run, Pallas kernels for 0% -> 0%
where the time goes in v1:
time: 461 us; the launch traced here: 460 us
  Pallas kernels  286 us (62%)
  blocking collectives  72.3 us (16%)
  local copies, waits for them, and re-layouts  32.3 us (7%)
  waiting for transfers between devices  22.4 us (5%)
  other arithmetic  21 us (5%)
  between operations  15.1 us (3%)
  starting transfers between devices  10.9 us (2%)
    pallas_call x1, Pallas kernels, backward(): pl.pallas_call(backward_kernel, name='backward_layer', out_shape=(jax.Sha...  182 us
    pallas_call x1, Pallas kernels, forward(): pl.pallas_call(forward_kernel, name='forward_layer', out_shape=tuple((jax...  104 us
    psum x1, blocking collectives, on_device(): packed = lax.psum(packed, ('tensor', 'dp'))  65 us
    unnamed x4, waiting for transfers between devices  22.4 us
    unnamed x32, local copies, waits for them, and re-layouts  18.8 us
    reduce_sum x1, other arithmetic, on_device(): jax.nn.one_hot(ids.reshape(items * length, 4), type_count, dtype=BF)  11.7 us
  transfers between devices with their start and end apart: 5, of which 2 were waited for; matrix products, arithmetic and copies ran while one was open for 6% of the time, Pallas kernels for 0%

profile of v1, /device:TPU:0, one launch (start us, length us, event | category | flops | bytes accessed | tf_op | source)
XLA Modules:
  0.0 460.3 jit_solution(3334491159023404501)
XLA Ops:
  7.2 0.8 stack.25
  8.0 0.7 broadcast_add_fusion.2
  8.8 0.7 broadcast_add_fusion.1
  9.5 0.7 broadcast_add_fusion
  10.3 0.9 copy.73
  11.1 0.8 reshape.145
  11.9 0.6 dynamic_slice.11
  12.5 0.7 pad_convert_fusion.1
  13.1 0.7 convert_element_type.58
  13.8 0.7 convert_element_type.57
  14.6 0.8 concatenate.20
  15.4 0.6 pad_convert_fusion.vec_ref
  16.0 2.1 pad.16.table_ref
  18.2 1.1 pad_maximum_fusion.wa_ref
  19.3 103.7 %forward_layer.1 = (bf16[4,768,768]{2,1,0:T(8,128)(2,1)}, bf16[4,768,768]{2,1,0:T(8,128)(2,1)}, bf16[4,768,768]{2,1,0:T(8,128)(2,1)}, bf16[4,768,512]{2,1,0:T(8,...) custom-call(bf16[2,2,512,768]{3,2,1,0:T(8,128)(2,1)} %inputs_ref.1, ...), custom_call_target="tpu_custom_call" | custom-call | flops 8000000000 | bytes 60000000 | tf_op jit(solution)/shard_map/forward_layer/pallas_call | solution.py:336
  123.0 181.8 %backward_layer.1 = (bf16[3,4,192,768]{3,2,1,0:T(8,128)(2,1)}, bf16[512,768]{1,0:T(8,128)(2,1)}, f32[16,768]{1,0:T(8,128)}) custom-call(bf16[2,2,512,768]{3,2,1,0:T(8,128)(2,1)} %cotangent_ref.1, bf16[4,768,768]{2,1,0:T(8,128)(2,1)} %get-tuple-element.60.wa_ref, bf16[4,768,768]{2,1,0:T(8,128)(2,1)} %get-tuple-element.61.wu_ref, ...), custom_call_target="tpu_custom_call" | custom-call | flops 16999999488 | bytes 60000000 | tf_op jit(solution)/shard_map/backward_layer/pallas_call | solution.py:752
  304.9 2.3 copy.75
  307.2 3.5 all-to-all-start.1
  310.7 0.3 all-reduce.7.cloned.1.call-start
  311.1 11.7 %fusion.2 = bf16[2048,516]{0,1:T(8,128)(2,1)S(1)} fusion(s32[2048,4]{0,1:T(4,128)S(1)} %add_bitcast_fusion), kind=kLoop, calls=%fused_computation.4 | loop fusion | flops 11624448 | bytes 2146304 | tf_op jit(solution)/shard_map/reduce_sum | solution.py:863
  323.0 0.8 fusion.3
  323.7 7.3 %fusion = bf16[264,192]{1,0:T(8,128)(2,1)S(1)} fusion(bf16[516,192]{1,0:T(8,128)(2,1)S(1)} %fusion.3), kind=kCustom, calls=%all-reduce-scatter | all-reduce-scatter fusion | flops 101377 | bytes 300032
  331.1 3.6 collective-permute-start
  334.7 0.6 dynamic-slice.28
  336.0 0.3 concatenate.22
  336.3 0.7 constant_dynamic-slice_fusion
  337.1 5.0 %copy.87 = bf16[3,768,768]{2,0,1:T(4,128)(2,1)S(1)} copy(bf16[3,768,768]{2,1,0:T(8,128)(2,1)} %bitcast.61) | data formatting | bytes 7077888
  342.1 2.5 copy.91
  344.7 1.1 copy-done
  345.8 1.2 copy.74
  347.0 3.5 all-to-all-start
  350.6 0.6 gather_fusion.1
  351.1 0.6 gather_fusion
  352.4 65.0 %psum.14 = f32[4,2688]{1,0:T(4,128)S(1)} all-reduce(f32[4,2688]{1,0:T(4,128)S(1)} %concatenate.21), channel_id=1, replica_groups=mesh['section'=2,'dp'=4,'tensor'=4] {'tensor','dp'}, use_global_device_ids=true, to_apply=%region_1.3 | all-reduce | flops 10752 | bytes 86016 | tf_op jit(solution)/shard_map/psum | solution.py:880
  417.3 0.6 constant_dynamic-slice_fusion.1
  417.9 0.7 fusion.9
  418.6 1.4 convert.8
  419.9 1.6 convert_element_type.56
  421.6 22.3 %reduce-scatter.6.cloned.1.call-done = bf16[192,2304]{1,0:T(8,128)(2,1)} async-done(((bf16[768,2304]{1,0:T(8,128)(2,1)}), bf16[192,2304]{1,0:T(8,128)(2,1)}) %reduce-scatter.6.cloned.1.call-update) | async-done | bytes 884752
  443.9 2.2 reshape.176
  446.1 0.9 copy.88
  447.3 0.7 slice_bitcast_fusion.1
  448.0 0.8 copy.82
  448.8 0.8 copy.83
  449.6 0.8 copy.84
  450.4 1.1 copy.85
  451.5 1.1 copy.86
  452.6 0.9 copy.95
  (56 shorter events, 1.7 us)
Async XLA Ops:
  7.2 11.0 %copy-start.1 = (bf16[1,192,768]{2,1,0:T(8,128)(2,1)S(1)}, bf16[1,192,768]{2,1,0:T(8,128)(2,1)}, u32[]{:S(2)}) copy-start(bf16[1,192,768]{2,1,0:T(8,128)(2,1)} %param.42) | copy-start | bytes 884740
  7.2 11.0 %copy-start.2 = (bf16[1,768,192]{1,2,0:T(8,128)(2,1)S(1)}, bf16[1,768,192]{1,2,0:T(8,128)(2,1)}, u32[]{:S(2)}) copy-start(bf16[1,768,192]{1,2,0:T(8,128)(2,1)} %param.40) | copy-start | bytes 884740
  7.2 11.0 %copy-start.3 = (bf16[1,768,192]{1,2,0:T(8,128)(2,1)S(1)}, bf16[1,768,192]{1,2,0:T(8,128)(2,1)}, u32[]{:S(2)}) copy-start(bf16[1,768,192]{1,2,0:T(8,128)(2,1)} %param.39) | copy-start | bytes 884740
  7.2 11.0 %copy-start.4 = (bf16[1,768,192]{1,2,0:T(8,128)(2,1)S(1)}, bf16[1,768,192]{1,2,0:T(8,128)(2,1)}, u32[]{:S(2)}) copy-start(bf16[1,768,192]{1,2,0:T(8,128)(2,1)} %param.37) | copy-start | bytes 884740
  18.1 1.1 copy-start.7
  304.9 6.2 %copy-start.6 = (s32[2,2,512]{2,1,0:T(2,128)S(1)}, s32[2,2,512]{2,1,0:T(2,128)}, u32[]{:S(2)}) copy-start(s32[2,2,512]{2,1,0:T(2,128)} %param.31) | copy-start | bytes 24580
  307.2 15.7 %all-to-all-start.1 = ((bf16[512,4,192]{0,2,1:T(8,128)(2,1)}), bf16[512,4,192]{0,2,1:T(8,128)(2,1)S(1)}, u32[]{:S(2)}, u32[]{:S(2)}) async-start(bf16[512,4,192]{0,2,1:T(8,128)(2,1)} %bitcast.16), calls=%async_computation.1 | async-start | bytes 1572864 | tf_op jit(solution)/shard_map/all_to_all | solution.py:859
  310.7 109.2 %all-reduce.7.cloned.1.call-start = ((), (), s32[]{:S(2)}) async-start(), calls=%async_computation.3 | async-start | bytes 270336 | tf_op jit(solution)/shard_map/psum | solution.py:868
  323.0 11.8 %copy-start.8 = (u32[32]{0:T(128)S(1)}, u32[32]{0:T(128)}, u32[]{:S(2)}) copy-start(u32[32]{0:T(128)} %constant.129) | copy-start | bytes 388
  331.1 5.0 %collective-permute-start = (bf16[6,192]{1,0:T(8,128)(2,1)S(1)}, bf16[6,192]{1,0:T(8,128)(2,1)S(1)}, u32[]{:S(2)}, u32[]{:S(2)}) collective-permute-start(bf16[6,192]{1,0:T(8,128)(2,1)S(1)} %slice.131), channel_id=1, source_target_pairs={{0,16},{1,17},{2,18},{3,19},{4,20},{5,21},{6,22},{7,23},{8,24},{9,... | collective-permute-start | bytes 6920
  337.0 106.8 %reduce-scatter.6.cloned.1.call-start = ((), (), s32[]{:S(2)}) async-start(), calls=%async_computation.4 | async-start | bytes 4423680
  344.7 1.1 copy-start
  344.7 5.8 %copy-start.5 = (f32[16,768]{1,0:T(8,128)S(1)}, f32[16,768]{1,0:T(8,128)}, u32[]{:S(2)}) copy-start(f32[16,768]{1,0:T(8,128)} %get-tuple-element.74) | copy-start | bytes 147460
  347.0 71.6 %all-to-all-start = ((bf16[512,4,192]{0,2,1:T(8,128)(2,1)}), bf16[512,4,192]{0,2,1:T(8,128)(2,1)S(1)}, u32[]{:S(2)}, u32[]{:S(2)}) async-start(bf16[512,4,192]{0,2,1:T(8,128)(2,1)} %bitcast.13), calls=%async_computation | async-start | bytes 1572864 | tf_op jit(solution)/shard_map/all_to_all | solution.py:854
Sparse Core Ops, SparseCore 0:
  337.2 36.5 all-reduce.6
  376.2 67.5 reduce-scatter.5

commit v2 on v1

--- a/solution.py
+++ b/solution.py
@@ -384,6 +384,7 @@
 
 
 def backward_kernel(
+    inner,
     cotangent_ref,
     wa_ref,
     wu_ref,
@@ -397,11 +398,15 @@
     rs1_ref,
     rs2_ref,
     x_ref,
+    y_ref,
     length_ref,
     vec_ref,
+    ids_ref,
     sums_out,
     dx_out,
+    y_out,
     vec_out,
+    table_out,
     wa,
     wu,
     wd,
@@ -414,44 +419,72 @@
     rs1,
     rs2,
     xb,
+    y,
     g,
     dsum,
     low,
     low_t,
+    out_t,
     first_t,
     x_t,
     dcontext,
     dx,
+    dx_t,
+    dx_in,
+    y_t,
     near_out,
     near_in,
-    far_out,
     far_in,
-    sums,
+    depth_in,
+    final,
+    vec,
+    vec_in,
+    table,
+    table_away,
+    table_in,
     load_sem,
     near_send,
     near_recv,
     far_send,
     far_recv,
+    depth_send,
+    depth_recv,
     relay_send,
     relay_recv,
+    dx_send,
+    dx_recv,
+    y_send,
+    y_recv,
+    vec_send,
+    vec_recv,
+    table_send,
+    table_recv,
     out_sem,
 ):
     section, data, tensor, beside, across = place()
+    diagonal = beside + 2 - 4 * ((beside // 2) % 2)
     length, width = g.shape
     ranks = wa.shape[0]
     heads = wa.shape[1] // (4 * HD)
     part = heads * HD
     steps = length // STEP
     sequences = cotangent_ref.shape[1]
-    units = sums.shape[1]
-    share = sums.shape[2]
+    units = near_in.shape[1]
+    share = near_in.shape[3]
+    columns_each = width // ranks
+    depth = lax.axis_size("dp")
     near = (section, data, beside)
     far = (section, data, across)
+    corner = (section, data, diagonal)
     other = (1 - section, data, tensor)
-    greet((near, far, other))
+    deep = []
+    if inner:
+        deep = [(section, (data + 1 + hop) % depth, tensor) for hop in range(depth - 1)]
+    greet([near, far, corner, other] + deep)
 
     loads = {}
     for name, source, target in (
+        ("y", y_ref, y),
         ("n2", n2_ref, n2),
         ("rs2", rs2_ref, rs2),
         ("wd", wd_ref, wd),
@@ -479,6 +512,32 @@
         )
         for step in range(steps)
     ]
+    around = ((beside, near), (across, far), (diagonal, corner))
+    y_copies = [
+        remote(y_t.at[rank], y_out.at[tensor], y_send.at[number], y_recv.at[number], device)
+        for number, (rank, device) in enumerate(around)
+    ]
+    y_own = pltpu.make_async_copy(y_t.at[tensor], y_out.at[tensor], out_sem.at[0])
+    dx_copies = [
+        remote(dx_t.at[rank], dx_in.at[tensor], dx_send.at[number], dx_recv.at[number], device)
+        for number, (rank, device) in enumerate(around)
+    ]
+
+    def turn(source, target):
+        def body(step, carry):
+            rows = pl.ds(pl.multiple_of(step * STEP, STEP), STEP)
+            value = jnp.transpose(source[rows, :].astype(F32), (1, 0)).astype(BF)
+            for rank in range(ranks):
+                target[rank, :, rows] = value[rank * columns_each : (rank + 1) * columns_each]
+            return carry
+
+        lax.fori_loop(0, steps, body, 0)
+
+    def share_outputs():
+        turn(y, y_t)
+        for copy in y_copies:
+            copy.start()
+        y_own.start()
 
     @pl.when(section != 0)
     def _():
@@ -486,7 +545,13 @@
 
     for name in loads:
         loads[name].start()
-    vec_out[...] = jnp.zeros_like(vec_out)
+    vec[0] = jnp.zeros(vec.shape[1:], F32)
+    loads["y"].wait()
+
+    @pl.when(section == 0)
+    def _():
+        share_outputs()
+
     loads["n2"].wait()
     loads["rs2"].wait()
 
@@ -495,7 +560,7 @@
         start_g.wait()
 
     def add_row(row, value):
-        vec_out[row : row + 1, :] += jnp.sum(value, axis=0, keepdims=True)
+        vec[0, row : row + 1, :] += jnp.sum(value, axis=0, keepdims=True)
 
     def norm_back(arriving, normal, scale, gain):
         scaled = arriving * gain
@@ -535,22 +600,32 @@
 
     def to_far(number, unit):
         return remote(
-            far_out.at[number, unit],
+            near_in.at[number, unit, 1],
             far_in.at[number, unit],
             far_send.at[number, unit],
             far_recv.at[number, unit],
             far,
         )
 
+    def to_depth(number, unit):
+        return remote(
+            near_in.at[number, unit, 0],
+            depth_in.at[number, unit],
+            depth_send.at[number, unit],
+            depth_recv.at[number, unit],
+            (section, (data + 1 + unit) % depth, tensor),
+        )
+
     def gradient(number, unit, rank):
-        rows = pl.ds(pl.multiple_of(unit * share, share), share)
+        at = (data + 1 + unit) % depth if inner else unit
+        rows = pl.ds(pl.multiple_of(at * share, share), share)
         if number == 0:
             return nn(low_t[rows, :], act[rank])
         if number == 1:
             return nn(first_t[rows, :], slope[rank])
         main = nt(x_t[rows, :], p[rank])
         edge = (3 * part // 256) * 256
-        tail = nt(low_t[rows, :], p[rank, edge : 4 * part, :])
+        tail = nt(out_t[rows, :], p[rank, edge : 4 * part, :])
         lane = lax.broadcasted_iota(jnp.int32, tail.shape, 1)
         tail = jnp.where(lane < 3 * part - edge, main[:, edge:], tail)
         return jnp.concatenate([main[:, :edge], tail], axis=1)
@@ -568,17 +643,31 @@
             @pl.when(index > 0)
             def _():
                 unit = index - 1
-                mine = gradient(number, unit, 2)
-                to_near(number, unit, 1).wait_recv()
-                far_out[number, unit] = (mine + near_in[number, unit, 1].astype(F32)).astype(BF)
-                to_far(number, unit).start()
-                mine = gradient(number, unit, 0)
-                to_near(number, unit, 0).wait_recv()
-                sums[number, unit] = (mine + near_in[number, unit, 0].astype(F32)).astype(BF)
+                for which, rank in ((1, 2), (0, 0)):
+                    mine = gradient(number, unit, rank)
+                    to_near(number, unit, which).wait_recv()
+                    near_in[number, unit, which] = (
+                        mine + near_in[number, unit, which].astype(F32)
+                    ).astype(BF)
+                    if which == 1:
+                        to_far(number, unit).start()
 
             return carry
 
         lax.fori_loop(0, units + 1, body, 0)
+
+    def finish(index):
+        number = index // units
+        unit = index % units
+        to_far(number, unit).wait_recv()
+        near_in[number, unit, 0] = (
+            near_in[number, unit, 0].astype(F32) + far_in[number, unit].astype(F32)
+        ).astype(BF)
+        if inner:
+
+            @pl.when(unit < units - 1)
+            def _():
+                to_depth(number, unit).start()
 
     loads["act"].wait()
 
@@ -597,7 +686,7 @@
         value = nt(low[...], wd[rank, columns, :]) * slope[rank, :, columns].astype(F32)
         value = value.astype(BF)
         slope[rank, :, columns] = value
-        vec_out[pl.ds(rank, 1), columns] = jnp.sum(value.astype(F32), axis=0, keepdims=True)
+        vec[0, pl.ds(rank, 1), columns] = jnp.sum(value.astype(F32), axis=0, keepdims=True)
         return carry
 
     lax.fori_loop(0, ranks * blocks, narrow, 0)
@@ -617,12 +706,6 @@
         reduce_stage(1)
 
     loads["wu"].wait()
-
-    if True:
-
-        @pl.when(section != 0)
-        def _():
-            reduce_stage(0)
 
     def first_back(step, carry):
         rows = pl.ds(pl.multiple_of(step * STEP, STEP), STEP)
@@ -638,10 +721,16 @@
         low[rows, :] = value
         value = value.astype(F32)
         add_row(8, value)
-        low_t[:, rows] = jnp.transpose(value, (1, 0)).astype(BF)
+        out_t[:, rows] = jnp.transpose(value, (1, 0)).astype(BF)
         return carry
 
     lax.fori_loop(0, steps, first_back, 0)
+
+    @pl.when(section == 0)
+    def _():
+        finish(0)
+        finish(1)
+
     loads["wa"].wait()
     loads["p"].wait()
     loads["lse"].wait()
@@ -665,24 +754,25 @@
         dout = dcontext[rank, at_query, :]
         weights = jnp.where(visible, jnp.exp(tn(keys, query) - lse[head]), 0.0)
         dweights = tn(values, dout)
-        inner = jnp.sum(weights * dweights, axis=0, keepdims=True)
-        dscores = (weights * (dweights - inner)).astype(BF)
+        inner_sum = jnp.sum(weights * dweights, axis=0, keepdims=True)
+        dscores = (weights * (dweights - inner_sum)).astype(BF)
         p[rank, at_query, :] = (nn(keys, dscores) * HD ** (-0.5)).astype(BF)
         p[rank, at_keys, :] = nt(query, dscores).astype(BF)
         p[rank, at_values, :] = nt(dout, weights.astype(BF)).astype(BF)
+
+        @pl.when((section == 0) & (head % 3 == 2))
+        def _():
+            finish(2 + head // 3)
+
         return carry
 
     lax.fori_loop(0, ranks * heads, attend_back, 0)
+    early = 2 + ranks * heads // 3
     for rank in range(ranks):
-        vec_out[4 + rank : 5 + rank, :] = nt(jnp.ones((8, length), BF), p[rank])[0:1, :]
+        vec[0, 4 + rank : 5 + rank, :] = nt(jnp.ones((8, length), BF), p[rank])[0:1, :]
+    vec_near = remote(vec.at[0], vec_in.at[0], vec_send.at[0], vec_recv.at[0], near)
+    vec_near.start()
     loads["xb"].wait()
-
-    def entering_transpose(step, carry):
-        rows = pl.ds(pl.multiple_of(step * STEP, STEP), STEP)
-        x_t[:, rows] = jnp.transpose(xb[rows, :].astype(F32), (1, 0)).astype(BF)
-        return carry
-
-    lax.fori_loop(0, steps, entering_transpose, 0)
 
     for step in range(steps):
         rows = pl.ds(step * STEP, STEP)
@@ -695,53 +785,161 @@
         def _():
             relays[step].start()
 
-    dx_copy = pltpu.make_async_copy(dx, dx_out, out_sem.at[0])
-    dx_copy.start()
+    vec_near.wait_recv()
+
+    def join(level, swap):
+        for row in range(vec.shape[1]):
+            pair = row ^ swap if row < 8 else row
+            vec[level + 1, row : row + 1, :] = (
+                vec[level, row : row + 1, :] + vec_in[level, pair : pair + 1, :]
+            )
+
+    join(0, 1)
+    vec_far = remote(vec.at[1], vec_in.at[1], vec_send.at[1], vec_recv.at[1], far)
+    vec_far.start()
+    turn(dx, dx_t)
+    for copy in dx_copies:
+        copy.start()
+    dx_in[tensor] = dx_t[tensor]
 
     @pl.when(section != 0)
     def _():
+        reduce_stage(0)
         reduce_stage(1)
 
+    def entering_transpose(step, carry):
+        rows = pl.ds(pl.multiple_of(step * STEP, STEP), STEP)
+        x_t[:, rows] = jnp.transpose(xb[rows, :].astype(F32), (1, 0)).astype(BF)
+        return carry
+
+    lax.fori_loop(0, steps, entering_transpose, 0)
     reduce_stage(2)
 
-    def finish(index, carry):
-        number = index // units
-        unit = index % units
-        to_far(number, unit).wait_recv()
-        sums[number, unit] = (
-            sums[number, unit].astype(F32) + far_in[number, unit].astype(F32)
-        ).astype(BF)
-        return carry
-
-    lax.fori_loop(0, 3 * units, finish, 0)
-    sums_copy = pltpu.make_async_copy(sums, sums_out, out_sem.at[1])
-    sums_copy.start()
+    vec_far.wait_recv()
+    join(1, 2)
+    vec_deep = [
+        remote(vec.at[2], vec_in.at[2 + hop], vec_send.at[2 + hop], vec_recv.at[2 + hop], device)
+        for hop, device in enumerate(deep)
+    ]
+    for copy in vec_deep:
+        copy.start()
+
+    @pl.when(section != 0)
+    def _():
+        share_outputs()
+        lax.fori_loop(0, early, lambda index, carry: (finish(index), carry)[1], 0)
+
+    for copy in dx_copies:
+        copy.wait_recv()
+    dx_done = pltpu.make_async_copy(dx_in, dx_out, out_sem.at[1])
+    dx_done.start()
+    half = table.shape[0]
+    table_x = remote(table_away, table, table_send.at[0], table_recv.at[0], other)
+
+    @pl.when(section == 0)
+    def _():
+        total = jnp.zeros((2 * half, columns_each), F32)
+        for item in range(ranks):
+            row = lax.broadcasted_iota(jnp.int32, (2 * half, length), 0)
+            picks = jnp.zeros((2 * half, length), F32)
+            for kind in range(4):
+                at = 4 * item + kind
+                picks = picks + jnp.where(ids_ref[at : at + 1, :] == row, 1.0, 0.0)
+            total = total + nt(picks.astype(BF), dx_in[item])
+        table[...] = total[:half].astype(BF)
+        table_away[...] = total[half:].astype(BF)
+        table_x.start()
+
+    lax.fori_loop(early, 3 * units, lambda index, carry: (finish(index), carry)[1], 0)
+
+    @pl.when(section != 0)
+    def _():
+        table_x.wait_recv()
+
+    table_deep = [
+        remote(
+            table, table_in.at[hop], table_send.at[1 + hop], table_recv.at[1 + hop], device
+        )
+        for hop, device in enumerate(deep)
+    ]
+    for copy in table_deep:
+        copy.start()
+
+    copies = []
+    if inner:
+        for number in range(3):
+            total = near_in[number, units - 1, 0].astype(F32)
+            for unit in range(units - 1):
+                to_depth(number, unit).wait_recv()
+                total = total + depth_in[number, unit].astype(F32)
+            final[number] = total
+            copy = pltpu.make_async_copy(
+                final.at[number], sums_out.at[number], out_sem.at[2 + number]
+            )
+            copy.start()
+            copies.append(copy)
+    else:
+        copy = pltpu.make_async_copy(
+            near_in.at[:, :, 0], sums_out, out_sem.at[2]
+        )
+        copy.start()
+        copies.append(copy)
+    total = vec[2]
+    for hop, copy in enumerate(vec_deep):
+        copy.wait_recv()
+        total = total + vec_in[2 + hop]
+    vec_out[...] = total
+    total = table[...].astype(F32)
+    for hop, copy in enumerate(table_deep):
+        copy.wait_recv()
+        total = total + table_in[hop].astype(F32)
+    table_out[...] = total
+
+    for copy in y_copies:
+        copy.wait()
+    y_own.wait()
+    for copy in dx_copies:
+        copy.wait_send()
+    vec_near.wait_send()
+    vec_far.wait_send()
+    for copy in vec_deep + table_deep:
+        copy.wait_send()
     for unit in range(units):
         for which in range(2):
             to_near(2, unit, which).wait_send()
     for number in range(3):
         for unit in range(units):
             to_far(number, unit).wait_send()
+            if inner and unit < units - 1:
+                to_depth(number, unit).wait_send()
 
     @pl.when(section != 0)
     def _():
         for relay in relays:
             relay.wait_send()
 
-    dx_copy.wait()
-    sums_copy.wait()
-
-
-def backward(cotangent, saved, length_here, vectors):
-    wa, wu, wd, p, lse, act, slope, n1, n2, rs1, rs2, x = saved
+    @pl.when(section == 0)
+    def _():
+        table_x.wait_send()
+
+    dx_done.wait()
+    for copy in copies:
+        copy.wait()
+
+
+def backward(cotangent, saved, length_here, vectors, ids, half, inner):
+    wa, wu, wd, p, lse, act, slope, n1, n2, rs1, rs2, x, y = saved
     ranks = wa.shape[0]
     length, width = x.shape
     steps = length // STEP
-    units = 4
+    depth = lax.axis_size("dp")
+    units = depth if inner else 4
+    hops = depth - 1 if inner else 0
     share = width // units
     anywhere = pl.BlockSpec(memory_space=pl.ANY)
     inside = pl.BlockSpec(memory_space=pltpu.VMEM)
     part = wa.shape[1] // 4
+    each = width // ranks
 
     def like(value):
         return pltpu.VMEM(value.shape, value.dtype)
@@ -749,16 +947,21 @@
     plane = (length, width)
     turned = (width, length)
     chunk = (share, width)
+    spread = (ranks, each, length)
+    semaphores = pltpu.SemaphoreType.DMA
+    sums = ((3,) + chunk, F32) if inner else ((3, units) + chunk, BF)
     return pl.pallas_call(
-        backward_kernel,
+        functools.partial(backward_kernel, inner),
         name="backward_layer",
         out_shape=(
-            jax.ShapeDtypeStruct((3, units) + chunk, BF),
-            jax.ShapeDtypeStruct(plane, BF),
+            jax.ShapeDtypeStruct(*sums),
+            jax.ShapeDtypeStruct(spread, BF),
+            jax.ShapeDtypeStruct(spread, BF),
             jax.ShapeDtypeStruct((16, width), F32),
+            jax.ShapeDtypeStruct((half, each), F32),
         ),
-        in_specs=[anywhere] * 13 + [pl.BlockSpec(memory_space=pltpu.SMEM), inside],
-        out_specs=(anywhere, anywhere, inside),
+        in_specs=[anywhere] * 14 + [pl.BlockSpec(memory_space=pltpu.SMEM), inside, inside],
+        out_specs=(anywhere, anywhere, anywhere, inside, inside),
         scratch_shapes=[like(value) for value in saved]
         + [
             pltpu.VMEM(plane, BF),
@@ -767,21 +970,40 @@
             pltpu.VMEM(turned, BF),
             pltpu.VMEM(turned, BF),
             pltpu.VMEM(turned, BF),
+            pltpu.VMEM(turned, BF),
             pltpu.VMEM((ranks, part, length), BF),
             pltpu.VMEM(plane, BF),
+            pltpu.VMEM(spread, BF),
+            pltpu.VMEM(spread, BF),
+            pltpu.VMEM(spread, BF),
             pltpu.VMEM((units, 2) + chunk, BF),
             pltpu.VMEM((3, units, 2) + chunk, BF),
             pltpu.VMEM((3, units) + chunk, BF),
-            pltpu.VMEM((3, units) + chunk, BF),
-            pltpu.VMEM((3, units) + chunk, BF),
-            pltpu.SemaphoreType.DMA((13,)),
-            pltpu.SemaphoreType.DMA((units, 2)),
-            pltpu.SemaphoreType.DMA((3, units, 2)),
-            pltpu.SemaphoreType.DMA((3, units)),
-            pltpu.SemaphoreType.DMA((3, units)),
-            pltpu.SemaphoreType.DMA((steps,)),
-            pltpu.SemaphoreType.DMA((steps,)),
-            pltpu.SemaphoreType.DMA((2,)),
+            pltpu.VMEM((3, max(hops, 1)) + (chunk if inner else (16, 128)), BF),
+            pltpu.VMEM((3,) + (chunk if inner else (16, 128)), F32),
+            pltpu.VMEM((3, 16, width), F32),
+            pltpu.VMEM((2 + hops, 16, width), F32),
+            pltpu.VMEM((half, each), BF),
+            pltpu.VMEM((half, each), BF),
+            pltpu.VMEM((max(hops, 1), half, each), BF),
+            semaphores((14,)),
+            semaphores((units, 2)),
+            semaphores((3, units, 2)),
+            semaphores((3, units)),
+            semaphores((3, units)),
+            semaphores((3, units)),
+            semaphores((3, units)),
+            semaphores((steps,)),
+            semaphores((steps,)),
+            semaphores((3,)),
+            semaphores((3,)),
+            semaphores((3,)),
+            semaphores((3,)),
+            semaphores((2 + hops,)),
+            semaphores((2 + hops,)),
+            semaphores((1 + hops,)),
+            semaphores((1 + hops,)),
+            semaphores((5,)),
         ],
         compiler_params=pltpu.CompilerParams(
             collective_id=1, has_side_effects=True, vmem_limit_bytes=VMEM_LIMIT
@@ -789,7 +1011,7 @@
         cost_estimate=pl.CostEstimate(
             flops=17_000_000_000, bytes_accessed=60_000_000, transcendentals=3_000_000
         ),
-    )(cotangent, *saved, length_here, vectors)
+    )(cotangent, *saved, length_here, vectors, ids)
 
 
 def on_device(
@@ -847,38 +1069,39 @@
     ).astype(F32)
     vectors = jnp.pad(vectors, ((0, 2), (0, 0)))
 
-    results = forward(
+    saved = forward(
         inputs, own_ids, table, length_here, wa, up_weight[0], down_weight[0], bias, vectors, ranks
     )
-    saved, leaving = results[:-1], results[-1]
-    layer_outputs = lax.all_to_all(leaving, "tensor", split_axis=1, concat_axis=0, tiled=True)
-    layer_outputs = layer_outputs.reshape(1, micro_count, sequences, length, width // ranks)
-
-    sums, dx, vecs = backward(cotangent, saved, length_here, vectors)
-
-    dcolumns = lax.all_to_all(dx, "tensor", split_axis=1, concat_axis=0, tiled=True)
-    layer_input_grads = dcolumns.astype(F32).reshape(
-        1, micro_count, sequences, length, width // ranks
+    depth = lax.axis_size("dp")
+    inner = depth <= 8 and width % (16 * depth) == 0
+    type_half = type_count // lax.axis_size("section")
+    half = -(-type_half // 16) * 16
+    turned_ids = jnp.swapaxes(ids, 1, 2).reshape(items * 4, length)
+    turned_ids = turned_ids + jnp.where(turned_ids >= type_half, half - type_half, 0)
+    sums, dx, leaving, vecs, table_part = backward(
+        cotangent, saved, length_here, vectors, turned_ids, half, inner
     )
-    picks = jax.nn.one_hot(ids.reshape(items * length, 4), type_count, dtype=BF).sum(axis=1)
-    table_term = lax.dot_general(
-        picks, dcolumns, (((0,), (0,)), ((), ())), preferred_element_type=F32
-    )
-    table_term = jnp.where(section == 0, table_term, 0.0).astype(BF)
-    table_sum = lax.psum(table_term, "dp")
-    table_grad = lax.psum_scatter(table_sum, "section", scatter_dimension=0, tiled=True).astype(F32)
-
-    summed = lax.psum_scatter(
-        sums.reshape(3, width, width), "dp", scatter_dimension=1, tiled=True
-    ).astype(F32)
-    order = jnp.arange(ranks) ^ tensor
-    packed = jnp.concatenate(
-        [jnp.take(vecs[0:ranks], order, axis=0), jnp.take(vecs[4 : 4 + ranks], order, axis=0)]
-        + [vecs[row].reshape(ranks, width // ranks) for row in range(8, 14)],
-        axis=1,
-    )
-    packed = lax.psum(packed, ("tensor", "dp"))
-    mine = lax.dynamic_slice_in_dim(packed, tensor, 1, 0)
+
+    def in_columns(value):
+        return jnp.swapaxes(value, 1, 2).reshape(
+            1, micro_count, sequences, length, width // ranks
+        )
+
+    layer_outputs = in_columns(leaving)
+    layer_input_grads = in_columns(dx).astype(F32)
+    table_grad = table_part[:type_half]
+    if inner:
+        summed = sums
+    else:
+        summed = lax.psum_scatter(
+            sums.reshape(3, width, width), "dp", scatter_dimension=1, tiled=True
+        ).astype(F32)
+        vecs = lax.psum(vecs, "dp")
+        table_grad = lax.psum(table_grad.astype(BF), "dp").astype(F32)
+    mine = lax.dynamic_slice_in_dim(
+        vecs[8:14].reshape(6, ranks, width // ranks), tensor, 1, 1
+    ).reshape(1, 6 * (width // ranks))
+    mine = jnp.concatenate([vecs[0:1], vecs[4:5], mine], axis=1)
 
     def vector(start, count):
         return mine[:, start : start + count]

time: 461 us -> 344 us (0.75)
  blocking collectives: 72.3 us -> 0 us
  Pallas kernels: 286 us -> 318 us
  waiting for transfers between devices: 22.4 us -> 0 us
  local copies, waits for them, and re-layouts: 32.3 us -> 16.5 us
  between operations: 15.1 us -> 0.79 us
  other arithmetic: 21 us -> 7.96 us
  starting transfers between devices: 10.9 us -> 0 us
    psum x1 -> x0, blocking collectives: 65 us -> none  [on_device(): packed = lax.psum(packed, ('tensor', 'dp'))]
    pallas_call x1, Pallas kernels: 182 us -> 214 us  [backward(): pl.pallas_call(functools.partial(backward_kernel, inner), name='backward_...]
    unnamed x4 -> x0, waiting for transfers between devices: 22.4 us -> none
    unnamed x32 -> x18, local copies, waits for them, and re-layouts: 18.8 us -> 1.71 us
    reduce_sum x1 -> x0, other arithmetic: 11.7 us -> none  [on_device(): jax.nn.one_hot(ids.reshape(items * length, 4), type_count, dtype=BF)]
    unnamed x1 -> x0, blocking collectives: 7.31 us -> none
    all_to_all x2 -> x0, starting transfers between devices: 6.99 us -> none  [the longest x1 3.5 us: on_device(): lax.all_to_all(leaving, 'tensor', split_axis=1, concat_axis=0, tiled=True)]
  transfers between devices with their start and end apart: 5 -> 0, of which waited for: 2 -> 0; matrix products, arithmetic and copies ran while one was open for 6% -> 0% of each run, Pallas kernels for 0% -> 0%
where the time goes in v2:
time: 344 us; the launch traced here: 343 us
  Pallas kernels  318 us (92%)
  local copies, waits for them, and re-layouts  16.5 us (5%)
  other arithmetic  7.96 us (2%)
    pallas_call x1, Pallas kernels, backward(): pl.pallas_call(functools.partial(backward_kernel, inner), name='backward_...  214 us
    pallas_call x1, Pallas kernels, forward(): pl.pallas_call(forward_kernel, name='forward_layer', out_shape=tuple((jax...  104 us

profile of v2, /device:TPU:0, one launch (start us, length us, event | category | flops | bytes accessed | tf_op | source)
XLA Modules:
  0.0 342.8 jit_solution(13327985470252250629)
XLA Ops:
  0.7 0.0 copy-start.3
  0.7 0.0 copy-start.4
  0.7 0.0 copy-start.5
  0.7 0.0 copy-start.6
  0.7 0.8 reshape.132
  1.5 0.6 dynamic_slice.11
  2.1 0.7 convert_element_type.43
  2.8 0.7 convert_element_type.44
  3.5 0.1 pad_maximum_fusion.1
  3.6 0.7 stack.20
  4.3 0.7 broadcast_add_fusion.2
  5.0 0.7 broadcast_add_fusion.1
  5.8 0.7 broadcast_add_fusion
  6.5 0.8 concatenate.16
  7.3 0.6 pad_convert_fusion.vec_ref
  7.9 0.7 pad_convert_fusion.1
  8.6 0.1 scatter.14.bias_ref
  8.7 0.0 copy-start.7
  8.7 0.6 select_add_fusion.ids_ref
  9.4 0.9 copy.45
  10.2 2.1 pad.16.table_ref
  12.3 0.0 copy-done.3
  12.3 0.0 copy-done.4
  12.3 0.0 copy-done.5
  12.3 0.0 copy-done.6
  12.3 1.1 pad_maximum_fusion.wa_ref
  13.4 0.0 copy-done.7
  13.4 103.7 %forward_layer.1 = (bf16[4,768,768]{2,1,0:T(8,128)(2,1)}, bf16[4,768,768]{2,1,0:T(8,128)(2,1)}, bf16[4,768,768]{2,1,0:T(8,128)(2,1)}, bf16[4,768,512]{2,1,0:T(8,...) custom-call(bf16[2,2,512,768]{3,2,1,0:T(8,128)(2,1)} %inputs_ref.1, ...), custom_call_target="tpu_custom_call" | custom-call | flops 8000000000 | bytes 60000000 | tf_op jit(solution)/shard_map/forward_layer/pallas_call | solution.py:336
  117.2 213.9 %backward_layer.1 = (f32[3,192,768]{2,1,0:T(8,128)}, bf16[4,192,512]{2,1,0:T(8,128)(2,1)}, bf16[4,192,512]{2,1,0:T(8,128)(2,1)}, f32[16,768]{1,0:T(8,128)}, f32[272,192]{1,0:T(8,128)}) custom-call(bf16[2,2,512,768]{3,2,1,0:T(8,128)(2,1)} %cotangent_ref.1, bf16[4,768,768]{2,1,0:T(8,128)(2,1)} %get-tuple-element.60.wa_ref, ...), custom_call_target="tpu_custom_call" | custom-call | flops 16999999488 | bytes 60000000 | tf_op jit(solution)/shard_map/backward_layer/pallas_call | solution.py:953
  331.0 0.0 copy-start
  331.1 1.4 slice.94
  332.5 0.7 slice.89
  333.2 0.1 reshape.137
  333.4 0.1 reshape.138
  333.4 1.4 fusion.1
  334.8 0.0 copy-start.2
  334.8 1.7 slice.99
  336.6 2.1 slice_bitcast_fusion.1
  338.7 0.0 copy-done
  338.7 0.0 copy-start.1
  338.7 1.1 slice_bitcast_fusion
  339.8 0.8 copy.46
  340.6 0.0 copy-done.2
  340.6 1.4 convert_element_type.46
  341.9 0.0 copy-done.1
  341.9 0.9 copy.49
  (9 shorter events, 0.2 us)
Async XLA Ops:
  0.7 11.7 %copy-start.3 = (bf16[1,192,768]{2,1,0:T(8,128)(2,1)S(1)}, bf16[1,192,768]{2,1,0:T(8,128)(2,1)}, u32[]{:S(2)}) copy-start(bf16[1,192,768]{2,1,0:T(8,128)(2,1)} %param.40) | copy-start | bytes 884740
  0.7 11.6 %copy-start.4 = (bf16[1,768,192]{1,2,0:T(8,128)(2,1)S(1)}, bf16[1,768,192]{1,2,0:T(8,128)(2,1)}, u32[]{:S(2)}) copy-start(bf16[1,768,192]{1,2,0:T(8,128)(2,1)} %param.38) | copy-start | bytes 884740
  0.7 11.6 %copy-start.5 = (bf16[1,768,192]{1,2,0:T(8,128)(2,1)S(1)}, bf16[1,768,192]{1,2,0:T(8,128)(2,1)}, u32[]{:S(2)}) copy-start(bf16[1,768,192]{1,2,0:T(8,128)(2,1)} %param.37) | copy-start | bytes 884740
  0.7 11.6 %copy-start.6 = (bf16[1,768,192]{1,2,0:T(8,128)(2,1)S(1)}, bf16[1,768,192]{1,2,0:T(8,128)(2,1)}, u32[]{:S(2)}) copy-start(bf16[1,768,192]{1,2,0:T(8,128)(2,1)} %param.35) | copy-start | bytes 884740
  8.7 4.8 %copy-start.7 = (f32[8,768]{1,0:T(8,128)}, f32[8,768]{1,0:T(8,128)S(1)}, u32[]{:S(2)}) copy-start(f32[8,768]{1,0:T(8,128)S(1)} %scatter.14.bias_ref) | copy-start | bytes 73732
  331.0 7.7 %copy-start = (f32[3,192,768]{2,1,0:T(8,128)S(1)}, f32[3,192,768]{2,1,0:T(8,128)}, u32[]{:S(2)}) copy-start(f32[3,192,768]{2,1,0:T(8,128)} %get-tuple-element.75) | copy-start | bytes 5308420
  334.8 5.8 %copy-start.2 = (bf16[4,192,512]{2,1,0:T(8,128)(2,1)S(1)}, bf16[4,192,512]{2,1,0:T(8,128)(2,1)}, u32[]{:S(2)}) copy-start(bf16[4,192,512]{2,1,0:T(8,128)(2,1)} %get-tuple-element.74) | copy-start | bytes 2359300
  338.7 3.2 copy-start.1

commit v3 on v2

--- a/solution.py
+++ b/solution.py
@@ -62,14 +62,24 @@
 
 def forward_kernel(
     inputs_ref,
-    ids_ref,
+    segment_ref,
+    column_ref,
+    row_ref,
+    answer_ref,
     table_ref,
     length_ref,
     wa_ref,
     wu_ref,
     wd_ref,
-    bias_ref,
-    vec_ref,
+    query_bias_ref,
+    value_bias_ref,
+    up_bias_ref,
+    output_bias_ref,
+    first_gain_ref,
+    first_shift_ref,
+    down_bias_ref,
+    second_gain_ref,
+    second_shift_ref,
     wa_out,
     wu_out,
     wd_out,
@@ -87,6 +97,7 @@
     wu,
     wd,
     bias,
+    table,
     p,
     lse,
     act,
@@ -102,6 +113,8 @@
     y,
     gather_send,
     gather_recv,
+    chain_send,
+    chain_recv,
     relay_send,
     relay_recv,
     local_sem,
@@ -117,41 +130,133 @@
     near = (section, data, beside)
     far = (section, data, across)
     other = (1 - section, data, tensor)
-    greet((near, far, other))
-
-    shards = ((wa_ref, wa), (bias_ref, bias), (wu_ref, wu), (wd_ref, wd))
+    depth = lax.axis_size("dp")
+    group = 4 if depth % 4 == 0 else 1
+    spot = data % group
+    before = (section, data - spot + (spot + group - 1) % group, tensor)
+    after = (section, data - spot + (spot + 1) % group, tensor)
+    greet([near, far, other] + ([before, after] if group > 1 else []))
+
+    shards = ((wa_ref, wa), (wu_ref, wu), (wd_ref, wd))
+    direct = wa.shape[1] // 3
+    piece = 2 * direct // group
+
+    def rows_of(number):
+        return pl.ds(pl.multiple_of(direct + number * piece, piece), piece)
+
     to_far = []
     to_near = []
     onward = []
     own = []
     for number, (source, target) in enumerate(shards):
         to_far.append(
-            remote(source, target.at[2], gather_send.at[number, 0], gather_recv.at[number, 0], far)
+            [
+                remote(
+                    source.at[rows],
+                    target.at[2, rows],
+                    gather_send.at[number, which],
+                    gather_recv.at[number, which],
+                    far,
+                )
+                for which, rows in enumerate((rows_of(spot), pl.ds(0, direct)))
+            ]
         )
         to_near.append(
-            remote(source, target.at[1], gather_send.at[number, 1], gather_recv.at[number, 1], near)
+            remote(source, target.at[1], gather_send.at[number, 2], gather_recv.at[number, 2], near)
         )
         onward.append(
             remote(
-                target.at[2], target.at[3], gather_send.at[number, 2], gather_recv.at[number, 2], near
+                target.at[2], target.at[3], gather_send.at[number, 3], gather_recv.at[number, 3], near
             )
         )
         own.append(pltpu.make_async_copy(source, target.at[0], local_sem.at[number]))
-    for copy in to_far:
-        copy.start()
+    to_far[0][0].start()
     for copy in to_near:
         copy.start()
     for copy in own:
         copy.start()
+    bias[0] = jnp.zeros(bias.shape[1:], F32)
+    bias[0, 0:1, :] = up_bias_ref[...].astype(F32)
+    bias[0, 1:2, 0:part] = query_bias_ref[...].astype(F32)
+    bias[0, 1:2, 2 * part : 3 * part] = value_bias_ref[...].astype(F32)
+    bias_copies = [
+        remote(bias.at[0], bias.at[1 + which], gather_send.at[3, which], gather_recv.at[3, which], to)
+        for which, to in enumerate((near, far))
+    ]
+    bias_onward = remote(bias.at[2], bias.at[3], gather_send.at[3, 2], gather_recv.at[3, 2], near)
+    for copy in bias_copies:
+        copy.start()
+
+    def chain(number, hop, up):
+        rows = rows_of(spot - (hop - 1) if up else spot + (hop - 1))
+        target = shards[number][1]
+        at = 0 if up else 1
+        return remote(
+            target.at[2, rows],
+            target.at[2, rows],
+            chain_send.at[number, at, hop - 1],
+            chain_recv.at[number, at, hop - 1],
+            after if up else before,
+        )
+
+    def chained(number, hop, up):
+        rows = rows_of(spot - hop if up else spot + hop)
+        target = shards[number][1]
+        at = 0 if up else 1
+        return remote(
+            target.at[2, rows],
+            target.at[2, rows],
+            chain_send.at[number, at, hop - 1],
+            chain_recv.at[number, at, hop - 1],
+            before if up else after,
+        )
+
+    def piece_in(number):
+        to_far[number][0].wait_recv()
+
+    def send_piece(number):
+        to_far[number][0].start()
+
+    def send_direct(number):
+        to_far[number][1].start()
+
+    def hand_on(number, hop):
+        if group == 1 or hop == group:
+            return
+        if hop > 0:
+
+            @pl.when(spot >= hop)
+            def _():
+                chained(number, hop, True).wait_recv()
+
+            @pl.when(spot + hop < group)
+            def _():
+                chained(number, hop, False).wait_recv()
+
+        if hop + 1 < group:
+
+            @pl.when((spot >= hop) & (spot + 1 < group))
+            def _():
+                chain(number, hop + 1, True).start()
+
+            @pl.when((spot + hop < group) & (spot >= 1))
+            def _():
+                chain(number, hop + 1, False).start()
 
     def pass_on(number):
-        to_far[number].wait_recv()
+        to_far[number][1].wait_recv()
         onward[number].start()
 
     def ready(number):
         own[number].wait()
         to_near[number].wait_recv()
         onward[number].wait_recv()
+
+    def at_first(actions):
+        @pl.when(section == 0)
+        def _():
+            for action, *values in actions:
+                action(*values)
 
     out_copies = []
 
@@ -179,30 +284,60 @@
         copy.start()
         copy.wait()
 
-        def embed(step, carry):
-            rows = pl.ds(pl.multiple_of(step * STEP, STEP), STEP)
-            lane = lax.broadcasted_iota(jnp.int32, (STEP, table_ref.shape[0]), 1)
-            picks = jnp.zeros((STEP, table_ref.shape[0]), F32)
-            for column in range(4):
-                picks = picks + jnp.where(ids_ref[rows, column : column + 1] == lane, 1.0, 0.0)
-            value = xb[rows, :].astype(F32) + nn(picks.astype(BF), table_ref[...])
-            xf[rows, :] = value
-            xb[rows, :] = value.astype(BF)
-            return carry
-
-        lax.fori_loop(0, steps, embed, 0)
-
+        types = table.shape[0]
+        table[...] = jnp.zeros_like(table)
+        table[0 : table_ref.shape[0], :] = table_ref[...]
+        micro, item = tensor // sequences, tensor % sequences
+        offset = 0
+        row = lax.broadcasted_iota(jnp.int32, (types, length), 0)
+        picks = jnp.zeros((types, length), F32)
+        for ids_ref, count in (
+            (segment_ref, 2),
+            (column_ref, COLS),
+            (row_ref, ROWS),
+            (answer_ref, 2),
+        ):
+            ids = ids_ref[micro, pl.ds(item, 1), :] + offset
+            picks = picks + jnp.where(ids == row, 1.0, 0.0)
+            offset += count
+        xf[...] = xb[...].astype(F32) + tn(picks.astype(BF), table[...])
+        xb[...] = xf[...].astype(BF)
+
+    piece_in(0)
+    hand_on(0, 0)
+    send_piece(1)
+    bias_copies[1].wait_recv()
+    bias_onward.start()
+    hand_on(0, 1)
+    piece_in(1)
+    hand_on(1, 0)
+    send_piece(2)
+    hand_on(0, 2)
+    piece_in(2)
+    send_direct(0)
+    hand_on(1, 1)
+    hand_on(0, 3)
     pass_on(0)
-    pass_on(1)
+    send_direct(1)
 
     @pl.when(section != 0)
     def _():
+        hand_on(1, 2)
+        hand_on(2, 0)
+        hand_on(1, 3)
+        hand_on(2, 1)
+        pass_on(1)
+        send_direct(2)
+        hand_on(2, 2)
+        hand_on(2, 3)
+        pass_on(2)
         for relay in relays:
             relay.wait_recv()
         xf[...] = xb[...].astype(F32)
 
     ready(0)
-    ready(1)
+    bias_copies[0].wait_recv()
+    bias_onward.wait_recv()
     put_out(wa, wa_out)
     put_out(xb, x_out)
 
@@ -214,9 +349,10 @@
         return carry
 
     lax.fori_loop(0, ranks, project, 0)
-    pass_on(2)
-
-    visible = lax.broadcasted_iota(jnp.int32, (length, length), 0) < length_ref[0, 0]
+    at_first([(hand_on, 1, 2), (hand_on, 2, 0)])
+
+    here = length_ref[tensor // sequences, tensor % sequences]
+    visible = lax.broadcasted_iota(jnp.int32, (length, length), 0) < here
 
     def attend(head, carry):
         rank = head // heads
@@ -232,6 +368,18 @@
         context = nn(values, raised.astype(BF)) / total
         p[rank, pl.ds(pl.multiple_of(3 * part + base, HD), HD), :] = context.astype(BF)
         lse[head] = maximum + jnp.log(total)
+        for at, action in (
+            (2, (hand_on, 1, 3)),
+            (4, (pass_on, 1)),
+            (4, (send_direct, 2)),
+            (5, (hand_on, 2, 1)),
+            (9, (hand_on, 2, 2)),
+        ):
+
+            @pl.when((section == 0) & (head == at))
+            def _():
+                action[0](*action[1:])
+
         return carry
 
     lax.fori_loop(0, ranks * heads, attend, 0)
@@ -240,11 +388,11 @@
 
     def first_norm(step, carry):
         rows = pl.ds(pl.multiple_of(step * STEP, STEP), STEP)
-        total = xf[rows, :] + vec_ref[0:1, :]
+        total = xf[rows, :] + output_bias_ref[...].astype(F32)
         for rank in range(ranks):
             total = total + tn(p[rank, 3 * part : 4 * part, rows], wa[rank, 3 * part : 4 * part, :])
         normal, scale = normalize(total)
-        value = normal * vec_ref[1:2, :] + vec_ref[2:3, :]
+        value = normal * first_gain_ref[...].astype(F32) + first_shift_ref[...].astype(F32)
         first[rows, :] = value
         low[rows, :] = value.astype(BF)
         n1[rows, :] = normal.astype(BF)
@@ -254,7 +402,8 @@
     lax.fori_loop(0, steps, first_norm, 0)
     put_out(n1, n1_out)
     put_out(rs1, rs1_out)
-    ready(2)
+    at_first([(hand_on, 2, 3)])
+    ready(1)
     put_out(wu, wu_out)
     block = 256
     blocks = wu.shape[2] // block
@@ -267,22 +416,25 @@
         act[rank, :, columns] = (hidden * inner).astype(BF)
         density = jnp.exp(hidden * hidden * (-0.5)) * 0.3989422804014327
         slope[rank, :, columns] = (inner + hidden * density).astype(BF)
+
         return carry
 
     lax.fori_loop(0, ranks * blocks, widen, 0)
     put_out(act, act_out)
     put_out(slope, slope_out)
-    pass_on(3)
-    ready(3)
+    at_first([(pass_on, 2)])
+    ready(2)
     put_out(wd, wd_out)
 
     for step in range(steps):
         rows = pl.ds(step * STEP, STEP)
-        total = first[rows, :] + vec_ref[3:4, :]
+        total = first[rows, :] + down_bias_ref[...].astype(F32)
         for rank in range(ranks):
             total = total + nn(act[rank, rows, :], wd[rank])
         normal, scale = normalize(total)
-        y[rows, :] = (normal * vec_ref[4:5, :] + vec_ref[5:6, :]).astype(BF)
+        y[rows, :] = (
+            normal * second_gain_ref[...].astype(F32) + second_shift_ref[...].astype(F32)
+        ).astype(BF)
         n2[rows, :] = normal.astype(BF)
         rs2[rows, :] = jnp.broadcast_to(scale, (STEP, 128))
 
@@ -295,9 +447,20 @@
     put_out(y, y_out)
     for copy in out_copies:
         copy.wait()
-    for group in (to_far, to_near, onward):
-        for copy in group:
+    for copies in to_far + [to_near, onward, bias_copies, [bias_onward]]:
+        for copy in copies:
             copy.wait_send()
+    for number in range(3):
+        for hop in range(group - 1):
+
+            @pl.when((spot >= hop) & (spot + 1 < group))
+            def _():
+                chain(number, hop + 1, True).wait_send()
+
+            @pl.when((spot + hop < group) & (spot >= 1))
+            def _():
+                chain(number, hop + 1, False).wait_send()
+
 
     @pl.when(section == 0)
     def _():
@@ -305,7 +468,7 @@
             relay.wait_send()
 
 
-def forward(inputs, ids, table, length_here, wa, wu, wd, bias, vectors, ranks):
+def forward(inputs, ids, table, lengths, wa, wu, wd, vectors, ranks):
     length, width = inputs.shape[2], inputs.shape[3]
     rows_a = wa.shape[0]
     hidden = wu.shape[1]
@@ -341,19 +504,22 @@
             anywhere,
             inside,
             inside,
+            inside,
+            inside,
+            inside,
             pl.BlockSpec(memory_space=pltpu.SMEM),
             anywhere,
             anywhere,
             anywhere,
-            anywhere,
-            inside,
-        ],
+        ]
+        + [inside] * len(vectors),
         out_specs=tuple(anywhere for _ in outs),
         scratch_shapes=[
             buffer("wa"),
             buffer("wu"),
             buffer("wd"),
-            pltpu.VMEM((ranks,) + bias.shape, F32),
+            pltpu.VMEM((ranks, 8, hidden), F32),
+            pltpu.VMEM((-(-table.shape[0] // 16) * 16, width), BF),
             buffer("p"),
             buffer("lse"),
             buffer("act"),
@@ -367,8 +533,10 @@
             buffer("rs1"),
             buffer("rs2"),
             buffer("y"),
-            pltpu.SemaphoreType.DMA((4, 3)),
-            pltpu.SemaphoreType.DMA((4, 3)),
+            pltpu.SemaphoreType.DMA((4, 4)),
+            pltpu.SemaphoreType.DMA((4, 4)),
+            pltpu.SemaphoreType.DMA((3, 2, 3)),
+            pltpu.SemaphoreType.DMA((3, 2, 3)),
             pltpu.SemaphoreType.DMA((steps,)),
             pltpu.SemaphoreType.DMA((steps,)),
             pltpu.SemaphoreType.DMA((5,)),
@@ -380,7 +548,7 @@
         cost_estimate=pl.CostEstimate(
             flops=8_000_000_000, bytes_accessed=60_000_000, transcendentals=6_000_000
         ),
-    )(inputs, ids, table, length_here, wa, wu, wd, bias, vectors)
+    )(inputs, *ids, table, lengths, wa, wu, wd, *vectors)
 
 
 def backward_kernel(
@@ -400,8 +568,13 @@
     x_ref,
     y_ref,
     length_ref,
-    vec_ref,
-    ids_ref,
+    first_gain_ref,
+    first_shift_ref,
+    second_gain_ref,
+    segment_ref,
+    column_ref,
+    row_ref,
+    answer_ref,
     sums_out,
     dx_out,
     y_out,
@@ -419,14 +592,11 @@
     rs1,
     rs2,
     xb,
-    y,
     g,
     dsum,
     low,
     low_t,
-    out_t,
     first_t,
-    x_t,
     dcontext,
     dx,
     dx_t,
@@ -442,6 +612,7 @@
     table,
     table_away,
     table_in,
+    table_sum,
     load_sem,
     near_send,
     near_recv,
@@ -478,13 +649,16 @@
     corner = (section, data, diagonal)
     other = (1 - section, data, tensor)
     deep = []
+    left = right = None
     if inner:
         deep = [(section, (data + 1 + hop) % depth, tensor) for hop in range(depth - 1)]
+        left = (section, (data + depth - 1) % depth, tensor)
+        right = (section, (data + 1) % depth, tensor)
     greet([near, far, corner, other] + deep)
 
     loads = {}
     for name, source, target in (
-        ("y", y_ref, y),
+        ("y", y_ref, dx),
         ("n2", n2_ref, n2),
         ("rs2", rs2_ref, rs2),
         ("wd", wd_ref, wd),
@@ -502,16 +676,11 @@
     start_g = pltpu.make_async_copy(
         cotangent_ref.at[tensor // sequences, tensor % sequences], g, load_sem.at[len(loads)]
     )
-    relays = [
-        remote(
-            dx.at[pl.ds(step * STEP, STEP)],
-            g.at[pl.ds(step * STEP, STEP)],
-            relay_send.at[step],
-            relay_recv.at[step],
-            other,
-        )
-        for step in range(steps)
-    ]
+
+    def relay(step):
+        rows = pl.ds(pl.multiple_of(step * STEP, STEP), STEP)
+        return remote(dx.at[rows], g.at[rows], relay_send.at[step], relay_recv.at[step], other)
+
     around = ((beside, near), (across, far), (diagonal, corner))
     y_copies = [
         remote(y_t.at[rank], y_out.at[tensor], y_send.at[number], y_recv.at[number], device)
@@ -534,7 +703,7 @@
         lax.fori_loop(0, steps, body, 0)
 
     def share_outputs():
-        turn(y, y_t)
+        turn(dx, y_t)
         for copy in y_copies:
             copy.start()
         y_own.start()
@@ -547,11 +716,7 @@
         loads[name].start()
     vec[0] = jnp.zeros(vec.shape[1:], F32)
     loads["y"].wait()
-
-    @pl.when(section == 0)
-    def _():
-        share_outputs()
-
+    share_outputs()
     loads["n2"].wait()
     loads["rs2"].wait()
 
@@ -570,30 +735,33 @@
             - normal * jnp.mean(scaled * normal, axis=-1, keepdims=True)
         ) * scale
 
-    for step in range(steps):
-        rows = pl.ds(step * STEP, STEP)
+    def second_back(step, carry):
+        rows = pl.ds(pl.multiple_of(step * STEP, STEP), STEP)
 
         @pl.when(section == 0)
         def _():
-            relays[step].wait_recv()
+            relay(step).wait_recv()
 
         arriving = g[rows, :].astype(F32)
         normal = n2[rows, :].astype(F32)
         add_row(12, arriving * normal)
         add_row(13, arriving)
-        value = norm_back(arriving, normal, rs2[rows, 0:1], vec_ref[4:5, :])
+        value = norm_back(arriving, normal, rs2[rows, 0:1], second_gain_ref[...].astype(F32))
         dsum[rows, :] = value
         value = value.astype(BF)
         low[rows, :] = value
         value = value.astype(F32)
         add_row(9, value)
         low_t[:, rows] = jnp.transpose(value, (1, 0)).astype(BF)
+        return carry
+
+    lax.fori_loop(0, steps, second_back, 0)
 
     def to_near(number, unit, which):
         return remote(
-            near_out.at[unit, which],
+            near_out.at[unit % 2, which],
             near_in.at[number, unit, which],
-            near_send.at[unit, which],
+            near_send.at[unit % 2, which],
             near_recv.at[number, unit, which],
             near,
         )
@@ -607,25 +775,39 @@
             far,
         )
 
-    def to_depth(number, unit):
+    factor = (depth - data) * (depth - data) * (depth - data) % (depth + 1)
+
+    def owner(unit):
+        return (factor * (unit + 1)) % (depth + 1) - 1
+
+    def rightward(number, block, slot):
         return remote(
-            near_in.at[number, unit, 0],
-            depth_in.at[number, unit],
-            depth_send.at[number, unit],
-            depth_recv.at[number, unit],
-            (section, (data + 1 + unit) % depth, tensor),
+            near_in.at[number, slot, 0],
+            depth_in.at[number, block],
+            depth_send.at[number, slot],
+            depth_recv.at[number, block],
+            right,
         )
 
+    def leftward(number, block, slot, landing):
+        return remote(
+            near_in.at[number, slot, 0],
+            depth_in.at[number, landing],
+            depth_send.at[number, slot],
+            depth_recv.at[number, landing],
+            left,
+        )
+
     def gradient(number, unit, rank):
-        at = (data + 1 + unit) % depth if inner else unit
+        at = owner(unit) if inner else unit
         rows = pl.ds(pl.multiple_of(at * share, share), share)
         if number == 0:
             return nn(low_t[rows, :], act[rank])
         if number == 1:
             return nn(first_t[rows, :], slope[rank])
-        main = nt(x_t[rows, :], p[rank])
+        main = nt(first_t[rows, :], p[rank])
         edge = (3 * part // 256) * 256
-        tail = nt(out_t[rows, :], p[rank, edge : 4 * part, :])
+        tail = nt(low_t[rows, :], p[rank, edge : 4 * part, :])
         lane = lax.broadcasted_iota(jnp.int32, tail.shape, 1)
         tail = jnp.where(lane < 3 * part - edge, main[:, edge:], tail)
         return jnp.concatenate([main[:, :edge], tail], axis=1)
@@ -635,9 +817,12 @@
             @pl.when(index < units)
             def _():
                 for which, rank in ((1, 3), (0, 1)):
-                    if number > 0:
-                        to_near(number - 1, index, which).wait_send()
-                    near_out[index, which] = gradient(number, index, rank).astype(BF)
+
+                    @pl.when((index >= 2) | (number > 0))
+                    def _():
+                        to_near(number, index, which).wait_send()
+
+                    near_out[index % 2, which] = gradient(number, index, rank).astype(BF)
                     to_near(number, index, which).start()
 
             @pl.when(index > 0)
@@ -649,8 +834,11 @@
                     near_in[number, unit, which] = (
                         mine + near_in[number, unit, which].astype(F32)
                     ).astype(BF)
-                    if which == 1:
-                        to_far(number, unit).start()
+                    if which == 1 and number == 0:
+
+                        @pl.when(unit < 2)
+                        def _():
+                            to_far(number, unit).start()
 
             return carry
 
@@ -664,10 +852,27 @@
             near_in[number, unit, 0].astype(F32) + far_in[number, unit].astype(F32)
         ).astype(BF)
         if inner:
-
-            @pl.when(unit < units - 1)
+            block = owner(unit)
+
+            @pl.when(((block > data) & (data > 0)) | ((block < data) & (data < depth - 1)))
             def _():
-                to_depth(number, unit).start()
+                rightward(number, block, unit).wait_recv()
+                near_in[number, unit, 0] = (
+                    near_in[number, unit, 0].astype(F32) + depth_in[number, block].astype(F32)
+                ).astype(BF)
+
+            @pl.when(block > data)
+            def _():
+                rightward(number, block, unit).start()
+
+            @pl.when(block < data)
+            def _():
+                landing = block + (depth - block) * ((block + 1) // data)
+                leftward(number, block, unit, landing).start()
+
+        @pl.when(index + 2 < 3 * units)
+        def _():
+            to_far((index + 2) // units, (index + 2) % units).start()
 
     loads["act"].wait()
 
@@ -690,12 +895,18 @@
         return carry
 
     lax.fori_loop(0, ranks * blocks, narrow, 0)
+
+    @pl.when(section == 0)
+    def _():
+        finish(0)
+
     loads["n1"].wait()
     loads["rs1"].wait()
 
     def first_transpose(step, carry):
         rows = pl.ds(pl.multiple_of(step * STEP, STEP), STEP)
-        value = n1[rows, :].astype(F32) * vec_ref[1:2, :] + vec_ref[2:3, :]
+        value = n1[rows, :].astype(F32) * first_gain_ref[...].astype(F32)
+        value = value + first_shift_ref[...].astype(F32)
         first_t[:, rows] = jnp.transpose(value, (1, 0)).astype(BF)
         return carry
 
@@ -704,6 +915,7 @@
     @pl.when(section == 0)
     def _():
         reduce_stage(1)
+        finish(1)
 
     loads["wu"].wait()
 
@@ -715,21 +927,18 @@
         normal = n1[rows, :].astype(F32)
         add_row(10, arriving * normal)
         add_row(11, arriving)
-        value = norm_back(arriving, normal, rs1[rows, 0:1], vec_ref[1:2, :])
+        value = norm_back(arriving, normal, rs1[rows, 0:1], first_gain_ref[...].astype(F32))
         dsum[rows, :] = value
         value = value.astype(BF)
         low[rows, :] = value
-        value = value.astype(F32)
-        add_row(8, value)
-        out_t[:, rows] = jnp.transpose(value, (1, 0)).astype(BF)
+        add_row(8, value.astype(F32))
         return carry
 
     lax.fori_loop(0, steps, first_back, 0)
 
     @pl.when(section == 0)
     def _():
-        finish(0)
-        finish(1)
+        finish(2)
 
     loads["wa"].wait()
     loads["p"].wait()
@@ -740,7 +949,8 @@
         return carry
 
     lax.fori_loop(0, ranks, context_back, 0)
-    visible = lax.broadcasted_iota(jnp.int32, (length, length), 0) < length_ref[0, 0]
+    here = length_ref[tensor // sequences, tensor % sequences]
+    visible = lax.broadcasted_iota(jnp.int32, (length, length), 0) < here
 
     def attend_back(head, carry):
         rank = head // heads
@@ -760,22 +970,22 @@
         p[rank, at_keys, :] = nt(query, dscores).astype(BF)
         p[rank, at_values, :] = nt(dout, weights.astype(BF)).astype(BF)
 
-        @pl.when((section == 0) & (head % 3 == 2))
+        @pl.when((section == 0) & (head % 5 == 4))
         def _():
-            finish(2 + head // 3)
+            finish(3 + head // 5)
 
         return carry
 
     lax.fori_loop(0, ranks * heads, attend_back, 0)
-    early = 2 + ranks * heads // 3
+    early = 3 + ranks * heads // 5 + 1
     for rank in range(ranks):
         vec[0, 4 + rank : 5 + rank, :] = nt(jnp.ones((8, length), BF), p[rank])[0:1, :]
     vec_near = remote(vec.at[0], vec_in.at[0], vec_send.at[0], vec_recv.at[0], near)
     vec_near.start()
     loads["xb"].wait()
 
-    for step in range(steps):
-        rows = pl.ds(step * STEP, STEP)
+    def entering_back(step, carry):
+        rows = pl.ds(pl.multiple_of(step * STEP, STEP), STEP)
         total = dsum[rows, :]
         for rank in range(ranks):
             total = total + tn(p[rank, 0 : 3 * part, rows], wa[rank, 0 : 3 * part, :])
@@ -783,8 +993,11 @@
 
         @pl.when(section != 0)
         def _():
-            relays[step].start()
-
+            relay(step).start()
+
+        return carry
+
+    lax.fori_loop(0, steps, entering_back, 0)
     vec_near.wait_recv()
 
     def join(level, swap):
@@ -802,14 +1015,20 @@
         copy.start()
     dx_in[tensor] = dx_t[tensor]
 
+    @pl.when(section == 0)
+    def _():
+        finish(early - 1)
+
     @pl.when(section != 0)
     def _():
         reduce_stage(0)
         reduce_stage(1)
+        finish(0)
 
     def entering_transpose(step, carry):
         rows = pl.ds(pl.multiple_of(step * STEP, STEP), STEP)
-        x_t[:, rows] = jnp.transpose(xb[rows, :].astype(F32), (1, 0)).astype(BF)
+        first_t[:, rows] = jnp.transpose(xb[rows, :].astype(F32), (1, 0)).astype(BF)
+        low_t[:, rows] = jnp.transpose(low[rows, :].astype(F32), (1, 0)).astype(BF)
         return carry
 
     lax.fori_loop(0, steps, entering_transpose, 0)
@@ -826,53 +1045,78 @@
 
     @pl.when(section != 0)
     def _():
-        share_outputs()
-        lax.fori_loop(0, early, lambda index, carry: (finish(index), carry)[1], 0)
-
+        lax.fori_loop(1, early, lambda index, carry: (finish(index), carry)[1], 0)
+
+    lax.fori_loop(early, 2 * units, lambda index, carry: (finish(index), carry)[1], 0)
     for copy in dx_copies:
         copy.wait_recv()
     dx_done = pltpu.make_async_copy(dx_in, dx_out, out_sem.at[1])
     dx_done.start()
     half = table.shape[0]
     table_x = remote(table_away, table, table_send.at[0], table_recv.at[0], other)
+    table_deep = [
+        remote(table, table_in.at[hop], table_send.at[1 + hop], table_recv.at[1 + hop], device)
+        for hop, device in enumerate(deep)
+    ]
 
     @pl.when(section == 0)
     def _():
-        total = jnp.zeros((2 * half, columns_each), F32)
-        for item in range(ranks):
+        types_each = table_out.shape[0]
+        table_sum[...] = jnp.zeros_like(table_sum)
+
+        def count(number, carry):
             row = lax.broadcasted_iota(jnp.int32, (2 * half, length), 0)
             picks = jnp.zeros((2 * half, length), F32)
-            for kind in range(4):
-                at = 4 * item + kind
-                picks = picks + jnp.where(ids_ref[at : at + 1, :] == row, 1.0, 0.0)
-            total = total + nt(picks.astype(BF), dx_in[item])
-        table[...] = total[:half].astype(BF)
-        table_away[...] = total[half:].astype(BF)
+            micro, item = number // sequences, number % sequences
+            offset = 0
+            for ids_ref, number_of in (
+                (segment_ref, 2),
+                (column_ref, COLS),
+                (row_ref, ROWS),
+                (answer_ref, 2),
+            ):
+                ids = ids_ref[micro, pl.ds(item, 1), :] + offset
+                ids = ids + jnp.where(ids >= types_each, half - types_each, 0)
+                picks = picks + jnp.where(ids == row, 1.0, 0.0)
+                offset += number_of
+            table_sum[...] += nt(picks.astype(BF), dx_in[number])
+            return carry
+
+        lax.fori_loop(0, ranks, count, 0)
+        table[...] = table_sum[:half].astype(BF)
+        table_away[...] = table_sum[half:].astype(BF)
         table_x.start()
-
-    lax.fori_loop(early, 3 * units, lambda index, carry: (finish(index), carry)[1], 0)
+        for copy in table_deep:
+            copy.start()
+
+    lax.fori_loop(2 * units, 3 * units - 1, lambda index, carry: (finish(index), carry)[1], 0)
 
     @pl.when(section != 0)
     def _():
         table_x.wait_recv()
-
-    table_deep = [
-        remote(
-            table, table_in.at[hop], table_send.at[1 + hop], table_recv.at[1 + hop], device
-        )
-        for hop, device in enumerate(deep)
-    ]
-    for copy in table_deep:
-        copy.start()
-
+        for copy in table_deep:
+            copy.start()
+
+    finish(3 * units - 1)
     copies = []
     if inner:
         for number in range(3):
-            total = near_in[number, units - 1, 0].astype(F32)
-            for unit in range(units - 1):
-                to_depth(number, unit).wait_recv()
-                total = total + depth_in[number, unit].astype(F32)
+            total = jnp.zeros(final.shape[1:], F32)
+            for unit in range(units):
+                keep = jnp.where(owner(unit) == data, 1.0, 0.0)
+                total = total + near_in[number, unit, 0].astype(F32) * keep
             final[number] = total
+
+            @pl.when(data > 0)
+            def _():
+                rightward(number, data, 0).wait_recv()
+                final[number] = final[number] + depth_in[number, data].astype(F32)
+
+            @pl.when(data < depth - 1)
+            def _():
+                leftward(number, data, 0, depth).wait_recv()
+                final[number] = final[number] + depth_in[number, depth].astype(F32)
+
             copy = pltpu.make_async_copy(
                 final.at[number], sums_out.at[number], out_sem.at[2 + number]
             )
@@ -893,7 +1137,7 @@
     for hop, copy in enumerate(table_deep):
         copy.wait_recv()
         total = total + table_in[hop].astype(F32)
-    table_out[...] = total
+    table_out[...] = total[: table_out.shape[0]]
 
     for copy in y_copies:
         copy.wait()
@@ -904,19 +1148,22 @@
     vec_far.wait_send()
     for copy in vec_deep + table_deep:
         copy.wait_send()
-    for unit in range(units):
+    for unit in range(2):
         for which in range(2):
             to_near(2, unit, which).wait_send()
     for number in range(3):
         for unit in range(units):
             to_far(number, unit).wait_send()
-            if inner and unit < units - 1:
-                to_depth(number, unit).wait_send()
+            if inner:
+
+                @pl.when(owner(unit) != data)
+                def _():
+                    rightward(number, 0, unit).wait_send()
 
     @pl.when(section != 0)
     def _():
-        for relay in relays:
-            relay.wait_send()
+        for step in range(steps):
+            relay(step).wait_send()
 
     @pl.when(section == 0)
     def _():
@@ -927,7 +1174,7 @@
         copy.wait()
 
 
-def backward(cotangent, saved, length_here, vectors, ids, half, inner):
+def backward(cotangent, saved, lengths, vectors, ids, type_half, inner):
     wa, wu, wd, p, lse, act, slope, n1, n2, rs1, rs2, x, y = saved
     ranks = wa.shape[0]
     length, width = x.shape
@@ -940,6 +1187,7 @@
     inside = pl.BlockSpec(memory_space=pltpu.VMEM)
     part = wa.shape[1] // 4
     each = width // ranks
+    half = -(-type_half // 16) * 16
 
     def like(value):
         return pltpu.VMEM(value.shape, value.dtype)
@@ -958,17 +1206,17 @@
             jax.ShapeDtypeStruct(spread, BF),
             jax.ShapeDtypeStruct(spread, BF),
             jax.ShapeDtypeStruct((16, width), F32),
-            jax.ShapeDtypeStruct((half, each), F32),
+            jax.ShapeDtypeStruct((type_half, each), F32),
         ),
-        in_specs=[anywhere] * 14 + [pl.BlockSpec(memory_space=pltpu.SMEM), inside, inside],
+        in_specs=[anywhere] * 14
+        + [pl.BlockSpec(memory_space=pltpu.SMEM)]
+        + [inside] * (len(vectors) + len(ids)),
         out_specs=(anywhere, anywhere, anywhere, inside, inside),
-        scratch_shapes=[like(value) for value in saved]
+        scratch_shapes=[like(value) for value in saved[:-1]]
         + [
             pltpu.VMEM(plane, BF),
             pltpu.VMEM(plane, F32),
             pltpu.VMEM(plane, BF),
-            pltpu.VMEM(turned, BF),
-            pltpu.VMEM(turned, BF),
             pltpu.VMEM(turned, BF),
             pltpu.VMEM(turned, BF),
             pltpu.VMEM((ranks, part, length), BF),
@@ -976,23 +1224,24 @@
             pltpu.VMEM(spread, BF),
             pltpu.VMEM(spread, BF),
             pltpu.VMEM(spread, BF),
-            pltpu.VMEM((units, 2) + chunk, BF),
+            pltpu.VMEM((2, 2) + chunk, BF),
             pltpu.VMEM((3, units, 2) + chunk, BF),
             pltpu.VMEM((3, units) + chunk, BF),
-            pltpu.VMEM((3, max(hops, 1)) + (chunk if inner else (16, 128)), BF),
+            pltpu.VMEM((3, units + 1) + (chunk if inner else (16, 128)), BF),
             pltpu.VMEM((3,) + (chunk if inner else (16, 128)), F32),
             pltpu.VMEM((3, 16, width), F32),
             pltpu.VMEM((2 + hops, 16, width), F32),
             pltpu.VMEM((half, each), BF),
             pltpu.VMEM((half, each), BF),
             pltpu.VMEM((max(hops, 1), half, each), BF),
+            pltpu.VMEM((2 * half, each), F32),
             semaphores((14,)),
-            semaphores((units, 2)),
+            semaphores((2, 2)),
             semaphores((3, units, 2)),
             semaphores((3, units)),
             semaphores((3, units)),
             semaphores((3, units)),
-            semaphores((3, units)),
+            semaphores((3, units + 1)),
             semaphores((steps,)),
             semaphores((steps,)),
             semaphores((3,)),
@@ -1011,7 +1260,7 @@
         cost_estimate=pl.CostEstimate(
             flops=17_000_000_000, bytes_accessed=60_000_000, transcendentals=3_000_000
         ),
-    )(cotangent, *saved, length_here, vectors, ids)
+    )(cotangent, *saved, lengths, *vectors, *ids)
 
 
 def on_device(
@@ -1039,47 +1288,36 @@
     second_gain,
     second_shift,
 ):
-    section = lax.axis_index("section")
     tensor = lax.axis_index("tensor")
     ranks = lax.axis_size("tensor")
     micro_count, sequences, length, width = inputs.shape
-    items = micro_count * sequences
     type_count = 4 + COLS + ROWS
-    padded_types = -(-type_count // 16) * 16
     part = query_weight.shape[2]
     hidden = up_weight.shape[2]
 
-    ids = jnp.stack(
-        [segment_ids, column_ids + 2, row_ids + 2 + COLS, answer_ids + 2 + COLS + ROWS], axis=-1
-    ).reshape(items, length, 4)
-    own_ids = lax.dynamic_index_in_dim(ids, tensor, 0, keepdims=False)
-    length_here = lax.dynamic_slice_in_dim(lengths.reshape(items), tensor, 1, 0).reshape(1, 1)
-    table = jnp.pad(type_table, ((0, padded_types - type_count), (0, 0)))
+    ids = (segment_ids, column_ids, row_ids, answer_ids)
     wa = jnp.concatenate(
         [query_weight[0].T, key_weight[0].T, value_weight[0].T, output_weight[0]], axis=0
     )
-    gap = jnp.zeros((part,), F32)
-    bias = jnp.zeros((8, hidden), F32)
-    bias = bias.at[0].set(up_bias[0].astype(F32))
-    bias = bias.at[1].set(
-        jnp.concatenate([query_bias[0].astype(F32), gap, value_bias[0].astype(F32), gap])
+    vectors = (
+        query_bias,
+        value_bias,
+        up_bias,
+        output_bias,
+        first_gain,
+        first_shift,
+        down_bias,
+        second_gain,
+        second_shift,
     )
-    vectors = jnp.concatenate(
-        [output_bias, first_gain, first_shift, down_bias, second_gain, second_shift]
-    ).astype(F32)
-    vectors = jnp.pad(vectors, ((0, 2), (0, 0)))
-
     saved = forward(
-        inputs, own_ids, table, length_here, wa, up_weight[0], down_weight[0], bias, vectors, ranks
+        inputs, ids, type_table, lengths, wa, up_weight[0], down_weight[0], vectors, ranks
     )
     depth = lax.axis_size("dp")
-    inner = depth <= 8 and width % (16 * depth) == 0
+    inner = depth == 4 and width % (16 * depth) == 0
     type_half = type_count // lax.axis_size("section")
-    half = -(-type_half // 16) * 16
-    turned_ids = jnp.swapaxes(ids, 1, 2).reshape(items * 4, length)
-    turned_ids = turned_ids + jnp.where(turned_ids >= type_half, half - type_half, 0)
-    sums, dx, leaving, vecs, table_part = backward(
-        cotangent, saved, length_here, vectors, turned_ids, half, inner
+    sums, dx, leaving, vecs, table_grad = backward(
+        cotangent, saved, lengths, (first_gain, first_shift, second_gain), ids, type_half, inner
     )
 
     def in_columns(value):
@@ -1089,7 +1327,6 @@
 
     layer_outputs = in_columns(leaving)
     layer_input_grads = in_columns(dx).astype(F32)
-    table_grad = table_part[:type_half]
     if inner:
         summed = sums
     else:

time: 344 us -> 287 us (0.83)
  Pallas kernels: 318 us -> 273 us
  local copies, waits for them, and re-layouts: 16.5 us -> 8.13 us
    pallas_call x1, Pallas kernels: 214 us -> 191 us  [backward(): pl.pallas_call(functools.partial(backward_kernel, inner), name='backward_...]
    pallas_call x1, Pallas kernels: 104 us -> 82.2 us  [forward(): pl.pallas_call(forward_kernel, name='forward_layer', out_shape=tuple((jax...]
where the time goes in v3:
time: 287 us
  Pallas kernels  273 us (95%)
  local copies, waits for them, and re-layouts  8.13 us (3%)
  other arithmetic  4.81 us (2%)
    pallas_call x1, Pallas kernels, backward(): pl.pallas_call(functools.partial(backward_kernel, inner), name='backward_...  191 us
    pallas_call x1, Pallas kernels, forward(): pl.pallas_call(forward_kernel, name='forward_layer', out_shape=tuple((jax...  82.2 us

profile of v3, /device:TPU:0, one launch (start us, length us, event | category | flops | bytes accessed | tf_op | source)
XLA Modules:
  0.0 286.5 jit_solution(3833887207741522241)
XLA Ops:
  0.7 2.3 pad_maximum_fusion.wa_ref
  3.0 82.2 %forward_layer.1 = (bf16[4,768,768]{2,1,0:T(8,128)(2,1)}, bf16[4,768,768]{2,1,0:T(8,128)(2,1)}, bf16[4,768,768]{2,1,0:T(8,128)(2,1)}, bf16[4,768,512]{2,1,0:T(8,...) custom-call(bf16[2,2,512,768]{3,2,1,0:T(8,128)(2,1)} %inputs_ref.1, ...), custom_call_target="tpu_custom_call" | custom-call | flops 8000000000 | bytes 60000000 | tf_op jit(solution)/shard_map/forward_layer/pallas_call | solution.py:499
  85.2 190.7 %backward_layer.1 = (f32[3,192,768]{2,1,0:T(8,128)}, bf16[4,192,512]{2,1,0:T(8,128)(2,1)}, bf16[4,192,512]{2,1,0:T(8,128)(2,1)}, f32[16,768]{1,0:T(8,128)}, f32[258,192]{1,0:T(8,128)}) custom-call(bf16[2,2,512,768]{3,2,1,0:T(8,128)(2,1)} %cotangent_ref.1, bf16[4,768,768]{2,1,0:T(8,128)(2,1)} %get-tuple-element.36.wa_ref, ...), custom_call_target="tpu_custom_call" | custom-call | flops 16999999488 | bytes 60000000 | tf_op jit(solution)/shard_map/backward_layer/pallas_call | solution.py:1201
  275.9 0.0 copy-start
  275.9 0.9 slice.57
  276.8 0.1 reshape.61
  276.9 0.1 reshape.62
  277.0 1.4 fusion
  278.3 2.5 convert_element_type.21
  280.8 0.0 copy-start.1
  280.8 0.0 copy-done
  280.8 1.1 slice_bitcast_fusion
  281.9 0.0 copy-start.2
  281.9 0.9 slice_bitcast_fusion.1
  282.8 0.8 copy.41
  283.6 1.3 slice.62
  284.9 0.0 copy-done.1
  284.9 0.9 copy.44
  285.8 0.0 copy-done.2
  285.8 0.7 copy.45
  (1 shorter events, 0.0 us)
Async XLA Ops:
  275.9 4.9 %copy-start = (f32[3,192,768]{2,1,0:T(8,128)S(1)}, f32[3,192,768]{2,1,0:T(8,128)}, u32[]{:S(2)}) copy-start(f32[3,192,768]{2,1,0:T(8,128)} %get-tuple-element.51) | copy-start | bytes 5308420
  280.8 4.1 %copy-start.1 = (bf16[4,192,512]{2,1,0:T(8,128)(2,1)S(1)}, bf16[4,192,512]{2,1,0:T(8,128)(2,1)}, u32[]{:S(2)}) copy-start(bf16[4,192,512]{2,1,0:T(8,128)(2,1)} %get-tuple-element.49) | copy-start | bytes 2359300
  281.9 3.9 %copy-start.2 = (f32[258,192]{1,0:T(8,128)S(1)}, f32[258,192]{1,0:T(8,128)}, u32[]{:S(2)}) copy-start(f32[258,192]{1,0:T(8,128)} %get-tuple-element.127) | copy-start | bytes 594436

commit v4 on v3

--- a/solution.py
+++ b/solution.py
@@ -16,7 +16,8 @@
 F32 = jnp.float32
 MESH = pl.DeviceIdType.MESH
 VMEM_LIMIT = 60 * 1024 * 1024
-STEP = 128
+STEP = 256
+OUTS = ("wa", "wu", "wd", "p", "lse", "act", "slope", "n1", "n2", "rs1", "rs2", "x", "y")
 
 
 def nn(left, right):
@@ -119,6 +120,7 @@
     relay_recv,
     local_sem,
     out_sem,
+    turn_sem,
 ):
     section, data, tensor, beside, across = place()
     length, width = xf.shape
@@ -138,11 +140,11 @@
     greet([near, far, other] + ([before, after] if group > 1 else []))
 
     shards = ((wa_ref, wa), (wu_ref, wu), (wd_ref, wd))
-    direct = wa.shape[1] // 3
-    piece = 2 * direct // group
+    direct = wa.shape[1] * 5 // 12
+    piece = (wa.shape[1] - direct) // group
 
     def rows_of(number):
-        return pl.ds(pl.multiple_of(direct + number * piece, piece), piece)
+        return pl.ds(pl.multiple_of(direct + number * piece, 16), piece)
 
     to_far = []
     to_near = []
@@ -260,6 +262,9 @@
 
     out_copies = []
 
+    wu_copy = pltpu.make_async_copy(wu, wu_out, out_sem.at[len(OUTS)])
+    wd_copy = pltpu.make_async_copy(wd, wd_out, out_sem.at[len(OUTS) + 1])
+
     def put_out(source, target):
         copy = pltpu.make_async_copy(source, target, out_sem.at[len(out_copies)])
         copy.start()
@@ -276,14 +281,24 @@
         for step in range(steps)
     ]
 
+    load_input = pltpu.make_async_copy(
+        inputs_ref.at[tensor // sequences, tensor % sequences], xb, local_sem.at[3]
+    )
+
     @pl.when(section == 0)
     def _():
-        copy = pltpu.make_async_copy(
-            inputs_ref.at[tensor // sequences, tensor % sequences], xb, local_sem.at[4]
-        )
-        copy.start()
-        copy.wait()
-
+        load_input.start()
+
+    piece_in(0)
+    hand_on(0, 0)
+    send_piece(1)
+    send_direct(0)
+    bias_copies[1].wait_recv()
+    bias_onward.start()
+
+    @pl.when(section == 0)
+    def _():
+        load_input.wait()
         types = table.shape[0]
         table[...] = jnp.zeros_like(table)
         table[0 : table_ref.shape[0], :] = table_ref[...]
@@ -303,42 +318,40 @@
         xf[...] = xb[...].astype(F32) + tn(picks.astype(BF), table[...])
         xb[...] = xf[...].astype(BF)
 
-    piece_in(0)
-    hand_on(0, 0)
-    send_piece(1)
-    bias_copies[1].wait_recv()
-    bias_onward.start()
     hand_on(0, 1)
     piece_in(1)
     hand_on(1, 0)
     send_piece(2)
     hand_on(0, 2)
     piece_in(2)
-    send_direct(0)
+    hand_on(2, 0)
+    send_direct(1)
     hand_on(1, 1)
     hand_on(0, 3)
     pass_on(0)
-    send_direct(1)
+    ready(0)
+    put_out(wa, wa_out)
 
     @pl.when(section != 0)
     def _():
         hand_on(1, 2)
-        hand_on(2, 0)
+        hand_on(2, 1)
         hand_on(1, 3)
-        hand_on(2, 1)
         pass_on(1)
         send_direct(2)
         hand_on(2, 2)
         hand_on(2, 3)
         pass_on(2)
+        ready(1)
+        wu_copy.start()
+        ready(2)
+        wd_copy.start()
         for relay in relays:
             relay.wait_recv()
         xf[...] = xb[...].astype(F32)
 
-    ready(0)
     bias_copies[0].wait_recv()
     bias_onward.wait_recv()
-    put_out(wa, wa_out)
     put_out(xb, x_out)
 
     def project(rank, carry):
@@ -349,7 +362,7 @@
         return carry
 
     lax.fori_loop(0, ranks, project, 0)
-    at_first([(hand_on, 1, 2), (hand_on, 2, 0)])
+    at_first([(hand_on, 1, 2), (hand_on, 2, 1)])
 
     here = length_ref[tensor // sequences, tensor % sequences]
     visible = lax.broadcasted_iota(jnp.int32, (length, length), 0) < here
@@ -370,10 +383,10 @@
         lse[head] = maximum + jnp.log(total)
         for at, action in (
             (2, (hand_on, 1, 3)),
-            (4, (pass_on, 1)),
-            (4, (send_direct, 2)),
-            (5, (hand_on, 2, 1)),
-            (9, (hand_on, 2, 2)),
+            (2, (pass_on, 1)),
+            (2, (send_direct, 2)),
+            (4, (hand_on, 2, 2)),
+            (8, (hand_on, 2, 3)),
         ):
 
             @pl.when((section == 0) & (head == at))
@@ -402,9 +415,7 @@
     lax.fori_loop(0, steps, first_norm, 0)
     put_out(n1, n1_out)
     put_out(rs1, rs1_out)
-    at_first([(hand_on, 2, 3)])
-    ready(1)
-    put_out(wu, wu_out)
+    at_first([(pass_on, 2), (ready, 1), (wu_copy.start,)])
     block = 256
     blocks = wu.shape[2] // block
 
@@ -422,9 +433,7 @@
     lax.fori_loop(0, ranks * blocks, widen, 0)
     put_out(act, act_out)
     put_out(slope, slope_out)
-    at_first([(pass_on, 2)])
-    ready(2)
-    put_out(wd, wd_out)
+    at_first([(ready, 2), (wd_copy.start,)])
 
     for step in range(steps):
         rows = pl.ds(step * STEP, STEP)
@@ -438,14 +447,29 @@
         n2[rows, :] = normal.astype(BF)
         rs2[rows, :] = jnp.broadcast_to(scale, (STEP, 128))
 
-        @pl.when(section == 0)
+        @pl.when((section == 0) & (tensor % 2 == 0))
         def _():
             relays[step].start()
 
     put_out(n2, n2_out)
     put_out(rs2, rs2_out)
     put_out(y, y_out)
-    for copy in out_copies:
+
+    @pl.when((section == 0) & (tensor % 2 == 0))
+    def _():
+        for relay in relays:
+            relay.wait_send()
+        pl.semaphore_signal(turn_sem, inc=1, device_id=near, device_id_type=MESH)
+
+    @pl.when((section == 0) & (tensor % 2 == 1))
+    def _():
+        pl.semaphore_wait(turn_sem, 1)
+        for relay in relays:
+            relay.start()
+        for relay in relays:
+            relay.wait_send()
+
+    for copy in out_copies + [wu_copy, wd_copy]:
         copy.wait()
     for copies in to_far + [to_near, onward, bias_copies, [bias_onward]]:
         for copy in copies:
@@ -460,12 +484,6 @@
             @pl.when((spot + hop < group) & (spot >= 1))
             def _():
                 chain(number, hop + 1, False).wait_send()
-
-
-    @pl.when(section == 0)
-    def _():
-        for relay in relays:
-            relay.wait_send()
 
 
 def forward(inputs, ids, table, lengths, wa, wu, wd, vectors, ranks):
@@ -493,13 +511,12 @@
     def buffer(name):
         return pltpu.VMEM(*shapes[name])
 
-    outs = ("wa", "wu", "wd", "p", "lse", "act", "slope", "n1", "n2", "rs1", "rs2", "x", "y")
     anywhere = pl.BlockSpec(memory_space=pl.ANY)
     inside = pl.BlockSpec(memory_space=pltpu.VMEM)
     return pl.pallas_call(
         forward_kernel,
         name="forward_layer",
-        out_shape=tuple(jax.ShapeDtypeStruct(*shapes[name]) for name in outs),
+        out_shape=tuple(jax.ShapeDtypeStruct(*shapes[name]) for name in OUTS),
         in_specs=[
             anywhere,
             inside,
@@ -513,7 +530,7 @@
             anywhere,
         ]
         + [inside] * len(vectors),
-        out_specs=tuple(anywhere for _ in outs),
+        out_specs=tuple(anywhere for _ in OUTS),
         scratch_shapes=[
             buffer("wa"),
             buffer("wu"),
@@ -540,7 +557,8 @@
             pltpu.SemaphoreType.DMA((steps,)),
             pltpu.SemaphoreType.DMA((steps,)),
             pltpu.SemaphoreType.DMA((5,)),
-            pltpu.SemaphoreType.DMA((len(outs),)),
+            pltpu.SemaphoreType.DMA((len(OUTS) + 2,)),
+            pltpu.SemaphoreType.REGULAR,
         ],
         compiler_params=pltpu.CompilerParams(
             collective_id=0, has_side_effects=True, vmem_limit_bytes=VMEM_LIMIT
@@ -654,11 +672,17 @@
         deep = [(section, (data + 1 + hop) % depth, tensor) for hop in range(depth - 1)]
         left = (section, (data + depth - 1) % depth, tensor)
         right = (section, (data + 1) % depth, tensor)
-    greet([near, far, corner, other] + deep)
+    partners = [near, far, corner, other] + deep
+    barrier = pltpu.get_barrier_semaphore()
+    for partner in partners:
+        pl.semaphore_signal(barrier, inc=1, device_id=partner, device_id_type=MESH)
+
+    @pl.when(section == 0)
+    def _():
+        pl.semaphore_wait(barrier, len(partners))
 
     loads = {}
     for name, source, target in (
-        ("y", y_ref, dx),
         ("n2", n2_ref, n2),
         ("rs2", rs2_ref, rs2),
         ("wd", wd_ref, wd),
@@ -676,6 +700,23 @@
     start_g = pltpu.make_async_copy(
         cotangent_ref.at[tensor // sequences, tensor % sequences], g, load_sem.at[len(loads)]
     )
+    first_y = pltpu.make_async_copy(y_ref, dx, load_sem.at[len(loads) + 1])
+    later_y = pltpu.make_async_copy(y_ref, g, load_sem.at[len(loads) + 1])
+    waves = (("n2", "rs2"), ("wd", "slope"), ("wu", "n1", "rs1"), ("wa", "p", "lse"), ("act", "xb"))
+
+    def begin(wave):
+        for name in waves[wave]:
+            loads[name].start()
+
+    def arrived(wave):
+        for name in waves[wave]:
+            loads[name].wait()
+        if wave + 1 < len(waves):
+
+            @pl.when(section != 0)
+            def _():
+                begin(wave + 1)
+
 
     def relay(step):
         rows = pl.ds(pl.multiple_of(step * STEP, STEP), STEP)
@@ -702,27 +743,29 @@
 
         lax.fori_loop(0, steps, body, 0)
 
-    def share_outputs():
-        turn(dx, y_t)
+    def share_outputs(source):
+        turn(source, y_t)
         for copy in y_copies:
             copy.start()
         y_own.start()
 
+    begin(0)
+    vec[0] = jnp.zeros(vec.shape[1:], F32)
+
+    @pl.when(section == 0)
+    def _():
+        first_y.start()
+        for wave in range(1, len(waves)):
+            begin(wave)
+        first_y.wait()
+        share_outputs(dx)
+
     @pl.when(section != 0)
     def _():
         start_g.start()
-
-    for name in loads:
-        loads[name].start()
-    vec[0] = jnp.zeros(vec.shape[1:], F32)
-    loads["y"].wait()
-    share_outputs()
-    loads["n2"].wait()
-    loads["rs2"].wait()
-
-    @pl.when(section != 0)
-    def _():
         start_g.wait()
+
+    arrived(0)
 
     def add_row(row, value):
         vec[0, row : row + 1, :] += jnp.sum(value, axis=0, keepdims=True)
@@ -874,14 +917,17 @@
         def _():
             to_far((index + 2) // units, (index + 2) % units).start()
 
-    loads["act"].wait()
 
     @pl.when(section == 0)
     def _():
+        arrived(4)
         reduce_stage(0)
 
-    loads["wd"].wait()
-    loads["slope"].wait()
+    @pl.when(section != 0)
+    def _():
+        later_y.start()
+
+    arrived(1)
     block = 256
     blocks = wu.shape[2] // block
 
@@ -900,8 +946,7 @@
     def _():
         finish(0)
 
-    loads["n1"].wait()
-    loads["rs1"].wait()
+    arrived(2)
 
     def first_transpose(step, carry):
         rows = pl.ds(pl.multiple_of(step * STEP, STEP), STEP)
@@ -910,14 +955,14 @@
         first_t[:, rows] = jnp.transpose(value, (1, 0)).astype(BF)
         return carry
 
-    lax.fori_loop(0, steps, first_transpose, 0)
+    def up_gradients():
+        lax.fori_loop(0, steps, first_transpose, 0)
+        reduce_stage(1)
 
     @pl.when(section == 0)
     def _():
-        reduce_stage(1)
+        up_gradients()
         finish(1)
-
-    loads["wu"].wait()
 
     def first_back(step, carry):
         rows = pl.ds(pl.multiple_of(step * STEP, STEP), STEP)
@@ -940,9 +985,13 @@
     def _():
         finish(2)
 
-    loads["wa"].wait()
-    loads["p"].wait()
-    loads["lse"].wait()
+    @pl.when(section != 0)
+    def _():
+        later_y.wait()
+        pl.semaphore_wait(barrier, len(partners))
+        share_outputs(g)
+
+    arrived(3)
 
     def context_back(rank, carry):
         dcontext[rank] = nt(wa[rank, 3 * part : 4 * part, :], low[...]).astype(BF)
@@ -980,9 +1029,13 @@
     early = 3 + ranks * heads // 5 + 1
     for rank in range(ranks):
         vec[0, 4 + rank : 5 + rank, :] = nt(jnp.ones((8, length), BF), p[rank])[0:1, :]
+
+    @pl.when(section != 0)
+    def _():
+        arrived(4)
+
     vec_near = remote(vec.at[0], vec_in.at[0], vec_send.at[0], vec_recv.at[0], near)
     vec_near.start()
-    loads["xb"].wait()
 
     def entering_back(step, carry):
         rows = pl.ds(pl.multiple_of(step * STEP, STEP), STEP)
@@ -1022,7 +1075,7 @@
     @pl.when(section != 0)
     def _():
         reduce_stage(0)
-        reduce_stage(1)
+        up_gradients()
         finish(0)
 
     def entering_transpose(step, carry):
@@ -1235,7 +1288,7 @@
             pltpu.VMEM((half, each), BF),
             pltpu.VMEM((max(hops, 1), half, each), BF),
             pltpu.VMEM((2 * half, each), F32),
-            semaphores((14,)),
+            semaphores((15,)),
             semaphores((2, 2)),
             semaphores((3, units, 2)),
             semaphores((3, units)),

time: 287 us -> 269 us (0.937)
  Pallas kernels: 273 us -> 255 us
    pallas_call x1, Pallas kernels: 82.2 us -> 72.1 us  [forward(): pl.pallas_call(forward_kernel, name='forward_layer', out_shape=tuple((jax...]
    pallas_call x1, Pallas kernels: 191 us -> 182 us  [backward(): pl.pallas_call(functools.partial(backward_kernel, inner), name='backward_...]
where the time goes in v4:
time: 269 us; the launch traced here: 268 us
  Pallas kernels  255 us (95%)
  local copies, waits for them, and re-layouts  8.13 us (3%)
  other arithmetic  4.81 us (2%)
    pallas_call x1, Pallas kernels, backward(): pl.pallas_call(functools.partial(backward_kernel, inner), name='backward_...  182 us
    pallas_call x1, Pallas kernels, forward(): pl.pallas_call(forward_kernel, name='forward_layer', out_shape=tuple((jax...  72.1 us

profile of v4, /device:TPU:0, one launch (start us, length us, event | category | flops | bytes accessed | tf_op | source)
XLA Modules:
  0.0 268.2 jit_solution(5658821815058901311)
XLA Ops:
  0.7 2.3 pad_maximum_fusion.wa_ref
  3.0 72.1 %forward_layer.1 = (bf16[4,768,768]{2,1,0:T(8,128)(2,1)}, bf16[4,768,768]{2,1,0:T(8,128)(2,1)}, bf16[4,768,768]{2,1,0:T(8,128)(2,1)}, bf16[4,768,512]{2,1,0:T(8,...) custom-call(bf16[2,2,512,768]{3,2,1,0:T(8,128)(2,1)} %inputs_ref.1, ...), custom_call_target="tpu_custom_call" | custom-call | flops 8000000000 | bytes 60000000 | tf_op jit(solution)/shard_map/forward_layer/pallas_call | solution.py:516
  75.1 182.4 %backward_layer.1 = (f32[3,192,768]{2,1,0:T(8,128)}, bf16[4,192,512]{2,1,0:T(8,128)(2,1)}, bf16[4,192,512]{2,1,0:T(8,128)(2,1)}, f32[16,768]{1,0:T(8,128)}, f32[258,192]{1,0:T(8,128)}) custom-call(bf16[2,2,512,768]{3,2,1,0:T(8,128)(2,1)} %cotangent_ref.1, bf16[4,768,768]{2,1,0:T(8,128)(2,1)} %get-tuple-element.36.wa_ref, ...), custom_call_target="tpu_custom_call" | custom-call | flops 16999999488 | bytes 60000000 | tf_op jit(solution)/shard_map/backward_layer/pallas_call | solution.py:1254
  257.5 0.0 copy-start
  257.5 0.9 slice.57
  258.4 0.1 reshape.61
  258.5 0.1 reshape.62
  258.6 1.4 fusion
  260.0 2.5 convert_element_type.21
  262.5 0.0 copy-start.1
  262.5 0.0 copy-done
  262.5 1.1 slice_bitcast_fusion
  263.6 0.0 copy-start.2
  263.6 0.9 slice_bitcast_fusion.1
  264.5 0.8 copy.41
  265.3 1.3 slice.62
  266.6 0.0 copy-done.1
  266.6 0.9 copy.44
  267.5 0.0 copy-done.2
  267.5 0.7 copy.45
  (1 shorter events, 0.0 us)
Async XLA Ops:
  257.5 4.9 %copy-start = (f32[3,192,768]{2,1,0:T(8,128)S(1)}, f32[3,192,768]{2,1,0:T(8,128)}, u32[]{:S(2)}) copy-start(f32[3,192,768]{2,1,0:T(8,128)} %get-tuple-element.51) | copy-start | bytes 5308420
  262.5 4.1 %copy-start.1 = (bf16[4,192,512]{2,1,0:T(8,128)(2,1)S(1)}, bf16[4,192,512]{2,1,0:T(8,128)(2,1)}, u32[]{:S(2)}) copy-start(bf16[4,192,512]{2,1,0:T(8,128)(2,1)} %get-tuple-element.49) | copy-start | bytes 2359300
  263.6 3.9 %copy-start.2 = (f32[258,192]{1,0:T(8,128)S(1)}, f32[258,192]{1,0:T(8,128)}, u32[]{:S(2)}) copy-start(f32[258,192]{1,0:T(8,128)} %get-tuple-element.127) | copy-start | bytes 594436

commit v5 on v4

--- a/solution.py
+++ b/solution.py
@@ -166,10 +166,18 @@
         to_near.append(
             remote(source, target.at[1], gather_send.at[number, 2], gather_recv.at[number, 2], near)
         )
+        rest = wa.shape[1] - direct
         onward.append(
-            remote(
-                target.at[2], target.at[3], gather_send.at[number, 3], gather_recv.at[number, 3], near
-            )
+            [
+                remote(
+                    target.at[2, rows],
+                    target.at[3, rows],
+                    gather_send.at[number, 3 + which],
+                    gather_recv.at[number, 3 + which],
+                    near,
+                )
+                for which, rows in enumerate((pl.ds(0, direct), pl.ds(direct, rest)))
+            ]
         )
         own.append(pltpu.make_async_copy(source, target.at[0], local_sem.at[number]))
     to_far[0][0].start()
@@ -245,14 +253,18 @@
             def _():
                 chain(number, hop + 1, False).start()
 
+    def direct_in(number):
+        to_far[number][1].wait_recv()
+        onward[number][0].start()
+
     def pass_on(number):
-        to_far[number][1].wait_recv()
-        onward[number].start()
+        onward[number][1].start()
 
     def ready(number):
         own[number].wait()
         to_near[number].wait_recv()
-        onward[number].wait_recv()
+        for copy in onward[number]:
+            copy.wait_recv()
 
     def at_first(actions):
         @pl.when(section == 0)
@@ -319,28 +331,31 @@
         xb[...] = xf[...].astype(BF)
 
     hand_on(0, 1)
+    hand_on(0, 2)
     piece_in(1)
     hand_on(1, 0)
     send_piece(2)
-    hand_on(0, 2)
-    piece_in(2)
-    hand_on(2, 0)
+    direct_in(0)
     send_direct(1)
-    hand_on(1, 1)
     hand_on(0, 3)
     pass_on(0)
+    hand_on(1, 1)
     ready(0)
     put_out(wa, wa_out)
 
     @pl.when(section != 0)
     def _():
+        piece_in(2)
+        hand_on(2, 0)
         hand_on(1, 2)
         hand_on(2, 1)
         hand_on(1, 3)
+        direct_in(1)
         pass_on(1)
         send_direct(2)
         hand_on(2, 2)
         hand_on(2, 3)
+        direct_in(2)
         pass_on(2)
         ready(1)
         wu_copy.start()
@@ -362,7 +377,7 @@
         return carry
 
     lax.fori_loop(0, ranks, project, 0)
-    at_first([(hand_on, 1, 2), (hand_on, 2, 1)])
+    at_first([(piece_in, 2), (hand_on, 2, 0)])
 
     here = length_ref[tensor // sequences, tensor % sequences]
     visible = lax.broadcasted_iota(jnp.int32, (length, length), 0) < here
@@ -382,11 +397,12 @@
         p[rank, pl.ds(pl.multiple_of(3 * part + base, HD), HD), :] = context.astype(BF)
         lse[head] = maximum + jnp.log(total)
         for at, action in (
-            (2, (hand_on, 1, 3)),
-            (2, (pass_on, 1)),
-            (2, (send_direct, 2)),
-            (4, (hand_on, 2, 2)),
-            (8, (hand_on, 2, 3)),
+            (2, (hand_on, 1, 2)),
+            (7, (hand_on, 2, 1)),
+            (7, (direct_in, 1)),
+            (7, (send_direct, 2)),
+            (11, (hand_on, 1, 3)),
+            (11, (pass_on, 1)),
         ):
 
             @pl.when((section == 0) & (head == at))
@@ -415,7 +431,7 @@
     lax.fori_loop(0, steps, first_norm, 0)
     put_out(n1, n1_out)
     put_out(rs1, rs1_out)
-    at_first([(pass_on, 2), (ready, 1), (wu_copy.start,)])
+    at_first([(hand_on, 2, 2), (ready, 1), (wu_copy.start,)])
     block = 256
     blocks = wu.shape[2] // block
 
@@ -427,6 +443,12 @@
         act[rank, :, columns] = (hidden * inner).astype(BF)
         density = jnp.exp(hidden * hidden * (-0.5)) * 0.3989422804014327
         slope[rank, :, columns] = (inner + hidden * density).astype(BF)
+
+        @pl.when((section == 0) & (index == ranks * blocks - 4))
+        def _():
+            direct_in(2)
+            hand_on(2, 3)
+            pass_on(2)
 
         return carry
 
@@ -471,7 +493,7 @@
 
     for copy in out_copies + [wu_copy, wd_copy]:
         copy.wait()
-    for copies in to_far + [to_near, onward, bias_copies, [bias_onward]]:
+    for copies in to_far + onward + [to_near, bias_copies, [bias_onward]]:
         for copy in copies:
             copy.wait_send()
     for number in range(3):
@@ -550,8 +572,8 @@
             buffer("rs1"),
             buffer("rs2"),
             buffer("y"),
-            pltpu.SemaphoreType.DMA((4, 4)),
-            pltpu.SemaphoreType.DMA((4, 4)),
+            pltpu.SemaphoreType.DMA((4, 5)),
+            pltpu.SemaphoreType.DMA((4, 5)),
             pltpu.SemaphoreType.DMA((3, 2, 3)),
             pltpu.SemaphoreType.DMA((3, 2, 3)),
             pltpu.SemaphoreType.DMA((steps,)),

time: 269 us -> 265 us (0.985)
  Pallas kernels: 255 us -> 251 us
    pallas_call x1, Pallas kernels: 72.1 us -> 68.8 us  [forward(): pl.pallas_call(forward_kernel, name='forward_layer', out_shape=tuple((jax...]
where the time goes in v5:
time: 265 us; the launch traced here: 264 us
  Pallas kernels  251 us (95%)
  local copies, waits for them, and re-layouts  8.13 us (3%)
  other arithmetic  4.81 us (2%)
    pallas_call x1, Pallas kernels, backward(): pl.pallas_call(functools.partial(backward_kernel, inner), name='backward_...  182 us
    pallas_call x1, Pallas kernels, forward(): pl.pallas_call(forward_kernel, name='forward_layer', out_shape=tuple((jax...  68.8 us

profile of v5, /device:TPU:0, one launch (start us, length us, event | category | flops | bytes accessed | tf_op | source)
XLA Modules:
  0.0 264.4 jit_solution(14266115522470898229)
XLA Ops:
  0.7 2.3 pad_maximum_fusion.wa_ref
  3.0 68.8 %forward_layer.1 = (bf16[4,768,768]{2,1,0:T(8,128)(2,1)}, bf16[4,768,768]{2,1,0:T(8,128)(2,1)}, bf16[4,768,768]{2,1,0:T(8,128)(2,1)}, bf16[4,768,512]{2,1,0:T(8,...) custom-call(bf16[2,2,512,768]{3,2,1,0:T(8,128)(2,1)} %inputs_ref.1, ...), custom_call_target="tpu_custom_call" | custom-call | flops 8000000000 | bytes 60000000 | tf_op jit(solution)/shard_map/forward_layer/pallas_call | solution.py:538
  71.8 182.0 %backward_layer.1 = (f32[3,192,768]{2,1,0:T(8,128)}, bf16[4,192,512]{2,1,0:T(8,128)(2,1)}, bf16[4,192,512]{2,1,0:T(8,128)(2,1)}, f32[16,768]{1,0:T(8,128)}, f32[258,192]{1,0:T(8,128)}) custom-call(bf16[2,2,512,768]{3,2,1,0:T(8,128)(2,1)} %cotangent_ref.1, bf16[4,768,768]{2,1,0:T(8,128)(2,1)} %get-tuple-element.36.wa_ref, ...), custom_call_target="tpu_custom_call" | custom-call | flops 16999999488 | bytes 60000000 | tf_op jit(solution)/shard_map/backward_layer/pallas_call | solution.py:1276
  253.8 0.0 copy-start
  253.8 0.9 slice.57
  254.7 0.1 reshape.61
  254.8 0.1 reshape.62
  254.9 1.4 fusion
  256.2 2.5 convert_element_type.21
  258.7 0.0 copy-start.1
  258.7 0.0 copy-done
  258.7 1.1 slice_bitcast_fusion
  259.8 0.0 copy-start.2
  259.8 0.9 slice_bitcast_fusion.1
  260.7 0.8 copy.41
  261.5 1.3 slice.62
  262.8 0.0 copy-done.1
  262.8 0.9 copy.44
  263.7 0.0 copy-done.2
  263.7 0.7 copy.45
  (1 shorter events, 0.0 us)
Async XLA Ops:
  253.8 4.9 %copy-start = (f32[3,192,768]{2,1,0:T(8,128)S(1)}, f32[3,192,768]{2,1,0:T(8,128)}, u32[]{:S(2)}) copy-start(f32[3,192,768]{2,1,0:T(8,128)} %get-tuple-element.51) | copy-start | bytes 5308420
  258.7 4.1 %copy-start.1 = (bf16[4,192,512]{2,1,0:T(8,128)(2,1)S(1)}, bf16[4,192,512]{2,1,0:T(8,128)(2,1)}, u32[]{:S(2)}) copy-start(bf16[4,192,512]{2,1,0:T(8,128)(2,1)} %get-tuple-element.49) | copy-start | bytes 2359300
  259.8 3.9 %copy-start.2 = (f32[258,192]{1,0:T(8,128)S(1)}, f32[258,192]{1,0:T(8,128)}, u32[]{:S(2)}) copy-start(f32[258,192]{1,0:T(8,128)} %get-tuple-element.127) | copy-start | bytes 594436

commit v6 on v5

--- a/solution.py
+++ b/solution.py
@@ -17,6 +17,7 @@
 MESH = pl.DeviceIdType.MESH
 VMEM_LIMIT = 60 * 1024 * 1024
 STEP = 256
+SHARES = (5, 5, 5)
 OUTS = ("wa", "wu", "wd", "p", "lse", "act", "slope", "n1", "n2", "rs1", "rs2", "x", "y")
 
 
@@ -140,11 +141,12 @@
     greet([near, far, other] + ([before, after] if group > 1 else []))
 
     shards = ((wa_ref, wa), (wu_ref, wu), (wd_ref, wd))
-    direct = wa.shape[1] * 5 // 12
-    piece = (wa.shape[1] - direct) // group
-
-    def rows_of(number):
-        return pl.ds(pl.multiple_of(direct + number * piece, 16), piece)
+    direct = [wa.shape[1] * count // 12 for count in SHARES]
+    piece = [(wa.shape[1] - count) // group for count in direct]
+
+    def rows_of(number, part_at):
+        start = direct[number] + part_at * piece[number]
+        return pl.ds(pl.multiple_of(start, 16), piece[number])
 
     to_far = []
     to_near = []
@@ -160,13 +162,13 @@
                     gather_recv.at[number, which],
                     far,
                 )
-                for which, rows in enumerate((rows_of(spot), pl.ds(0, direct)))
+                for which, rows in enumerate((rows_of(number, spot), pl.ds(0, direct[number])))
             ]
         )
         to_near.append(
             remote(source, target.at[1], gather_send.at[number, 2], gather_recv.at[number, 2], near)
         )
-        rest = wa.shape[1] - direct
+        rest = wa.shape[1] - direct[number]
         onward.append(
             [
                 remote(
@@ -176,7 +178,9 @@
                     gather_recv.at[number, 3 + which],
                     near,
                 )
-                for which, rows in enumerate((pl.ds(0, direct), pl.ds(direct, rest)))
+                for which, rows in enumerate(
+                    (pl.ds(0, direct[number]), pl.ds(direct[number], rest))
+                )
             ]
         )
         own.append(pltpu.make_async_copy(source, target.at[0], local_sem.at[number]))
@@ -198,7 +202,7 @@
         copy.start()
 
     def chain(number, hop, up):
-        rows = rows_of(spot - (hop - 1) if up else spot + (hop - 1))
+        rows = rows_of(number, spot - (hop - 1) if up else spot + (hop - 1))
         target = shards[number][1]
         at = 0 if up else 1
         return remote(
@@ -210,7 +214,7 @@
         )
 
     def chained(number, hop, up):
-        rows = rows_of(spot - hop if up else spot + hop)
+        rows = rows_of(number, spot - hop if up else spot + hop)
         target = shards[number][1]
         at = 0 if up else 1
         return remote(
@@ -1049,15 +1053,11 @@
 
     lax.fori_loop(0, ranks * heads, attend_back, 0)
     early = 3 + ranks * heads // 5 + 1
-    for rank in range(ranks):
-        vec[0, 4 + rank : 5 + rank, :] = nt(jnp.ones((8, length), BF), p[rank])[0:1, :]
 
     @pl.when(section != 0)
     def _():
         arrived(4)
 
-    vec_near = remote(vec.at[0], vec_in.at[0], vec_send.at[0], vec_recv.at[0], near)
-    vec_near.start()
 
     def entering_back(step, carry):
         rows = pl.ds(pl.multiple_of(step * STEP, STEP), STEP)
@@ -1073,6 +1073,14 @@
         return carry
 
     lax.fori_loop(0, steps, entering_back, 0)
+    for rank in range(ranks):
+        vec[0, 4 + rank : 5 + rank, :] = nt(jnp.ones((8, length), BF), p[rank])[0:1, :]
+    vec_near = remote(vec.at[0], vec_in.at[0], vec_send.at[0], vec_recv.at[0], near)
+    vec_near.start()
+    turn(dx, dx_t)
+    for copy in dx_copies:
+        copy.start()
+    dx_in[tensor] = dx_t[tensor]
     vec_near.wait_recv()
 
     def join(level, swap):
@@ -1085,10 +1093,6 @@
     join(0, 1)
     vec_far = remote(vec.at[1], vec_in.at[1], vec_send.at[1], vec_recv.at[1], far)
     vec_far.start()
-    turn(dx, dx_t)
-    for copy in dx_copies:
-        copy.start()
-    dx_in[tensor] = dx_t[tensor]
 
     @pl.when(section == 0)
     def _():
@@ -1122,7 +1126,7 @@
     def _():
         lax.fori_loop(1, early, lambda index, carry: (finish(index), carry)[1], 0)
 
-    lax.fori_loop(early, 2 * units, lambda index, carry: (finish(index), carry)[1], 0)
+    lax.fori_loop(early, 2 * units - 1, lambda index, carry: (finish(index), carry)[1], 0)
     for copy in dx_copies:
         copy.wait_recv()
     dx_done = pltpu.make_async_copy(dx_in, dx_out, out_sem.at[1])
@@ -1164,7 +1168,7 @@
         for copy in table_deep:
             copy.start()
 
-    lax.fori_loop(2 * units, 3 * units - 1, lambda index, carry: (finish(index), carry)[1], 0)
+    lax.fori_loop(2 * units - 1, 3 * units - 1, lambda index, carry: (finish(index), carry)[1], 0)
 
     @pl.when(section != 0)
     def _():

time: 265 us -> 263 us (level)
  no operation moved by 1% of the time
where the time goes in v6:
time: 263 us
  Pallas kernels  249 us (95%)
  local copies, waits for them, and re-layouts  8.13 us (3%)
  other arithmetic  4.81 us (2%)
    pallas_call x1, Pallas kernels, backward(): pl.pallas_call(functools.partial(backward_kernel, inner), name='backward_...  181 us
    pallas_call x1, Pallas kernels, forward(): pl.pallas_call(forward_kernel, name='forward_layer', out_shape=tuple((jax...  68.8 us

profile of v6, /device:TPU:0, one launch (start us, length us, event | category | flops | bytes accessed | tf_op | source)
XLA Modules:
  0.0 263.0 jit_solution(8050083536782567342)
XLA Ops:
  0.7 2.3 pad_maximum_fusion.wa_ref
  3.0 68.8 %forward_layer.1 = (bf16[4,768,768]{2,1,0:T(8,128)(2,1)}, bf16[4,768,768]{2,1,0:T(8,128)(2,1)}, bf16[4,768,768]{2,1,0:T(8,128)(2,1)}, bf16[4,768,512]{2,1,0:T(8,...) custom-call(bf16[2,2,512,768]{3,2,1,0:T(8,128)(2,1)} %inputs_ref.1, ...), custom_call_target="tpu_custom_call" | custom-call | flops 8000000000 | bytes 60000000 | tf_op jit(solution)/shard_map/forward_layer/pallas_call | solution.py:542
  71.8 180.5 %backward_layer.1 = (f32[3,192,768]{2,1,0:T(8,128)}, bf16[4,192,512]{2,1,0:T(8,128)(2,1)}, bf16[4,192,512]{2,1,0:T(8,128)(2,1)}, f32[16,768]{1,0:T(8,128)}, f32[258,192]{1,0:T(8,128)}) custom-call(bf16[2,2,512,768]{3,2,1,0:T(8,128)(2,1)} %cotangent_ref.1, bf16[4,768,768]{2,1,0:T(8,128)(2,1)} %get-tuple-element.36.wa_ref, ...), custom_call_target="tpu_custom_call" | custom-call | flops 16999999488 | bytes 60000000 | tf_op jit(solution)/shard_map/backward_layer/pallas_call | solution.py:1280
  252.3 0.0 copy-start
  252.3 0.9 slice.57
  253.2 0.1 reshape.61
  253.3 0.1 reshape.62
  253.4 1.4 fusion
  254.8 2.5 convert_element_type.21
  257.3 0.0 copy-start.1
  257.3 0.0 copy-done
  257.3 1.1 slice_bitcast_fusion
  258.4 0.0 copy-start.2
  258.4 0.9 slice_bitcast_fusion.1
  259.3 0.8 copy.41
  260.1 1.3 slice.62
  261.4 0.0 copy-done.1
  261.4 0.9 copy.44
  262.3 0.0 copy-done.2
  262.3 0.7 copy.45
  (1 shorter events, 0.0 us)
Async XLA Ops:
  252.3 4.9 %copy-start = (f32[3,192,768]{2,1,0:T(8,128)S(1)}, f32[3,192,768]{2,1,0:T(8,128)}, u32[]{:S(2)}) copy-start(f32[3,192,768]{2,1,0:T(8,128)} %get-tuple-element.51) | copy-start | bytes 5308420
  257.3 4.1 %copy-start.1 = (bf16[4,192,512]{2,1,0:T(8,128)(2,1)S(1)}, bf16[4,192,512]{2,1,0:T(8,128)(2,1)}, u32[]{:S(2)}) copy-start(bf16[4,192,512]{2,1,0:T(8,128)(2,1)} %get-tuple-element.49) | copy-start | bytes 2359300
  258.4 3.9 %copy-start.2 = (f32[258,192]{1,0:T(8,128)S(1)}, f32[258,192]{1,0:T(8,128)}, u32[]{:S(2)}) copy-start(f32[258,192]{1,0:T(8,128)} %get-tuple-element.127) | copy-start | bytes 594436

commit v7 on v6

--- a/solution.py
+++ b/solution.py
@@ -1007,10 +1007,6 @@
 
     lax.fori_loop(0, steps, first_back, 0)
 
-    @pl.when(section == 0)
-    def _():
-        finish(2)
-
     @pl.when(section != 0)
     def _():
         later_y.wait()
@@ -1044,6 +1040,10 @@
         p[rank, at_query, :] = (nn(keys, dscores) * HD ** (-0.5)).astype(BF)
         p[rank, at_keys, :] = nt(query, dscores).astype(BF)
         p[rank, at_values, :] = nt(dout, weights.astype(BF)).astype(BF)
+
+        @pl.when((section == 0) & (head == 1))
+        def _():
+            finish(2)
 
         @pl.when((section == 0) & (head % 5 == 4))
         def _():

time: 263 us -> 263 us (level)
  no operation moved by 1% of the time
where the time goes in v7:
time: 263 us; the launch traced here: 262 us
  Pallas kernels  249 us (95%)
  local copies, waits for them, and re-layouts  8.13 us (3%)
  other arithmetic  4.81 us (2%)
    pallas_call x1, Pallas kernels, backward(): pl.pallas_call(functools.partial(backward_kernel, inner), name='backward_...  180 us
    pallas_call x1, Pallas kernels, forward(): pl.pallas_call(forward_kernel, name='forward_layer', out_shape=tuple((jax...  68.8 us

profile of v7, /device:TPU:0, one launch (start us, length us, event | category | flops | bytes accessed | tf_op | source)
XLA Modules:
  0.0 262.4 jit_solution(6794962174303858346)
XLA Ops:
  0.7 2.3 pad_maximum_fusion.wa_ref
  3.0 68.8 %forward_layer.1 = (bf16[4,768,768]{2,1,0:T(8,128)(2,1)}, bf16[4,768,768]{2,1,0:T(8,128)(2,1)}, bf16[4,768,768]{2,1,0:T(8,128)(2,1)}, bf16[4,768,512]{2,1,0:T(8,...) custom-call(bf16[2,2,512,768]{3,2,1,0:T(8,128)(2,1)} %inputs_ref.1, ...), custom_call_target="tpu_custom_call" | custom-call | flops 8000000000 | bytes 60000000 | tf_op jit(solution)/shard_map/forward_layer/pallas_call | solution.py:542
  71.8 180.0 %backward_layer.1 = (f32[3,192,768]{2,1,0:T(8,128)}, bf16[4,192,512]{2,1,0:T(8,128)(2,1)}, bf16[4,192,512]{2,1,0:T(8,128)(2,1)}, f32[16,768]{1,0:T(8,128)}, f32[258,192]{1,0:T(8,128)}) custom-call(bf16[2,2,512,768]{3,2,1,0:T(8,128)(2,1)} %cotangent_ref.1, bf16[4,768,768]{2,1,0:T(8,128)(2,1)} %get-tuple-element.36.wa_ref, ...), custom_call_target="tpu_custom_call" | custom-call | flops 16999999488 | bytes 60000000 | tf_op jit(solution)/shard_map/backward_layer/pallas_call | solution.py:1280
  251.8 0.0 copy-start
  251.8 0.9 slice.57
  252.7 0.1 reshape.61
  252.8 0.1 reshape.62
  252.9 1.4 fusion
  254.3 2.5 convert_element_type.21
  256.7 0.0 copy-start.1
  256.7 0.0 copy-done
  256.8 1.1 slice_bitcast_fusion
  257.8 0.0 copy-start.2
  257.8 0.9 slice_bitcast_fusion.1
  258.7 0.8 copy.41
  259.5 1.3 slice.62
  260.9 0.0 copy-done.1
  260.9 0.9 copy.44
  261.7 0.0 copy-done.2
  261.7 0.7 copy.45
  (1 shorter events, 0.0 us)
Async XLA Ops:
  251.8 4.9 %copy-start = (f32[3,192,768]{2,1,0:T(8,128)S(1)}, f32[3,192,768]{2,1,0:T(8,128)}, u32[]{:S(2)}) copy-start(f32[3,192,768]{2,1,0:T(8,128)} %get-tuple-element.51) | copy-start | bytes 5308420
  256.7 4.1 %copy-start.1 = (bf16[4,192,512]{2,1,0:T(8,128)(2,1)S(1)}, bf16[4,192,512]{2,1,0:T(8,128)(2,1)}, u32[]{:S(2)}) copy-start(bf16[4,192,512]{2,1,0:T(8,128)(2,1)} %get-tuple-element.49) | copy-start | bytes 2359300
  257.8 3.9 %copy-start.2 = (f32[258,192]{1,0:T(8,128)S(1)}, f32[258,192]{1,0:T(8,128)}, u32[]{:S(2)}) copy-start(f32[258,192]{1,0:T(8,128)} %get-tuple-element.127) | copy-start | bytes 594436
